TPU v7x, 32 devices: a whole 2x2x4 slice. The times are simulated.
32 devices in a mesh: groups: 2 (over y), gallery: 4 (over z), query: 4 (over x, core).
Axes of the slice: x: 2, y: 2, z: 4, core: 2. Of those that a mesh axis runs over, the one named last changes fastest.
Arguments:
- gallery: bfloat16 [2048, 2048], P(('groups', 'gallery'), 'query'), parts along dimension 0
- neighbour: int32 [2048, 10], P(('groups', 'gallery')), parts along dimension 0, may hold values from 0 to 319, as said below
- weights: int32 [2048, 10], P(('groups', 'gallery')), parts along dimension 0, may hold values from 1 to 4
- send_rows: int32 [8, 64], P(('groups', 'gallery')), parts along dimension 0, may hold values from 0 to 255, as said below
- queries: bfloat16 [1024, 2048], P('gallery', 'query'), may hold values from -6 to 6
Outputs:
- refined: bfloat16 [2048, 2048], P(('groups', 'gallery'), 'query'), parts along dimension 0
- scores: bfloat16 [2048, 1024], P(('groups', 'gallery'), 'query'), parts along dimension 0
There are 2 independent parts, one for each index of `groups`. A program takes and returns all parts, laid end to end along the dimension named above; an argument that names none is the same for every part. Nothing has to cross between parts.
Inputs may be any that keep to these rules, and one draw needn't show every extreme that they name: `neighbour`: A value below 256 names a row of the row's own shard. A value v of 256 or more names position (v - 256) % 16 of the list that shard (v - 256) // 16 sends to the row's shard, never the shard's own list. `send_rows`: row s, positions d * 16 to d * 16 + 15: rows of shard s, numbered within the shard, listed for shard d, all different.
All inputs are finite; a program needn't handle non-finite values.
Results may differ from a plain program's by a relative error of at most 0.0049.
Values may be sent and summed in bfloat16 or wider, within the bound.
No kernel may reach another device: no remote copies, remote signals or barrier semaphores. Data moves between devices by JAX's collectives and lax.ppermute only.
A program may use at most 64 MiB of HBM per device.

v0:
```python
import math

import jax
import jax.numpy as jnp
from jax import lax
from jax.sharding import PartitionSpec as P

D = 2048


self_weight = 4.0
epsilon = 1e-06


def per_device(gallery, neighbour, weights, send_rows, queries):
    row_count, col_count = gallery.shape
    outgoing = send_rows[0]
    arrived = lax.all_to_all(gallery[outgoing], "gallery", split_axis=0, concat_axis=0, tiled=True)
    table = jnp.concatenate([gallery, arrived], axis=0)
    is_local = neighbour < row_count
    slot_index = jnp.maximum(neighbour - row_count, 0)
    row_index = jnp.where(is_local, neighbour, row_count + slot_index)
    weight_floats = weights.astype(jnp.float32)
    weighted = jnp.zeros((row_count, col_count), jnp.float32)
    for which in range(neighbour.shape[1]):
        picked = table[row_index[:, which]].astype(jnp.float32)
        weighted = weighted + weight_floats[:, which][:, None] * picked
    denominator = self_weight + jnp.sum(weight_floats, axis=1)
    refined = (
        (self_weight * gallery.astype(jnp.float32) + weighted) / denominator[:, None]
    ).astype(jnp.bfloat16)
    floats = refined.astype(jnp.float32)
    squares = lax.psum(jnp.sum(floats * floats, axis=1), "query")
    partial_value = lax.dot_general(
        refined,
        lax.all_gather(queries, "gallery", axis=0, tiled=True),
        (((1,), (1,)), ((), ())),
        preferred_element_type=jnp.float32,
    )
    summed = lax.psum_scatter(partial_value, "query", scatter_dimension=1, tiled=True)
    inverse = lax.rsqrt(squares / D + epsilon) / math.sqrt(D)
    scores = (summed * inverse[:, None]).astype(jnp.bfloat16)
    return (refined, scores)


def solution(mesh):
    return jax.shard_map(
        per_device,
        mesh=mesh,
        in_specs=(
            P(("groups", "gallery"), "query"),
            P(("groups", "gallery"), None),
            P(("groups", "gallery"), None),
            P(("groups", "gallery"), None),
            P("gallery", "query"),
        ),
        out_specs=(P(("groups", "gallery"), "query"), P(("groups", "gallery"), "query")),
        check_vma=False,
    )
```

profile of v0, /device:TPU:0, one launch (start us, length us, event | category | flops | bytes accessed | tf_op | source)
XLA Modules:
  0.0 84.2 jit_solution(6721633504954892073)
XLA Ops:
  7.2 0.0 copy-start.4
  7.2 0.6 copy-done.4
  7.8 2.3 %gather_fusion = bf16[64,512]{1,0:T(8,128)(2,1)} fusion(bf16[256,512]{1,0:T(8,128)(2,1)} %param.5, s32[1024]{0:T(1024)S(1)} %pad_clamp_fusion.10), kind=kCustom, calls=%fused_computation | custom fusion | bytes 131328 | tf_op jit(solution)/shard_map/gather | solution.py:18
  10.2 0.0 copy-start.3
  10.2 6.4 %all-to-all-start = ((bf16[4,16,512]{2,1,0:T(8,128)(2,1)}), bf16[4,16,512]{2,1,0:T(8,128)(2,1)S(1)}, u32[]{:S(2)}, u32[]{:S(2)}) async-start(bf16[4,16,512]{2,1,0:T(8,128)(2,1)} %bitcast.3), calls=%async_computation | async-start | bytes 131072 | tf_op jit(solution)/shard_map/all_to_all | solution.py:18
  16.6 0.0 copy-start
  16.6 0.0 all-gather.2.cloned.1.call-start
  16.6 0.7 all-gather.2.cloned.1.call-update
  17.3 0.0 reduce-scatter.2.cloned.1.call-start
  17.4 0.0 copy-done.3
  17.4 0.0 copy-start.2
  17.5 0.7 copy-done.2
  18.3 4.1 %all-to-all-done = bf16[4,16,512]{2,1,0:T(8,128)(2,1)S(1)} async-done(((bf16[4,16,512]{2,1,0:T(8,128)(2,1)}), bf16[4,16,512]{2,1,0:T(8,128)(2,1)S(1)}, u32[]{:S(2)}, u32[]{:S(2)}) %all-to-all-start) | async-done | bytes 65568 | tf_op jit(solution)/shard_map/all_to_all | solution.py:18
  22.4 0.0 copy-done
  22.4 1.2 %gather_fusion.1 = bf16[256,512]{1,0:T(8,128)(2,1)S(1)} fusion(bf16[320,512]{1,0:T(8,128)(2,1)S(1)} %pad_maximum_fusion, s32[1024]{0:T(1024)S(1)} %pad_clamp_fusion.9), kind=kCustom, calls=%fused_computation.1 | custom fusion | bytes 525312 | tf_op jit(solution)/shard_map/gather | solution.py:26
  23.5 1.2 %gather_fusion.10 = bf16[256,512]{1,0:T(8,128)(2,1)S(1)} fusion(bf16[320,512]{1,0:T(8,128)(2,1)S(1)} %pad_maximum_fusion, s32[1024]{0:T(1024)S(1)} %pad_clamp_fusion), kind=kCustom, calls=%fused_computation.10 | custom fusion | bytes 525312 | tf_op jit(solution)/shard_map/gather | solution.py:26
  24.7 1.2 %gather_fusion.2 = bf16[256,512]{1,0:T(8,128)(2,1)S(1)} fusion(bf16[320,512]{1,0:T(8,128)(2,1)S(1)} %pad_maximum_fusion, s32[1024]{0:T(1024)S(1)} %pad_clamp_fusion.8), kind=kCustom, calls=%fused_computation.2 | custom fusion | bytes 525312 | tf_op jit(solution)/shard_map/gather | solution.py:26
  25.8 1.2 %gather_fusion.3 = bf16[256,512]{1,0:T(8,128)(2,1)S(1)} fusion(bf16[320,512]{1,0:T(8,128)(2,1)S(1)} %pad_maximum_fusion, s32[1024]{0:T(1024)S(1)} %pad_clamp_fusion.7), kind=kCustom, calls=%fused_computation.3 | custom fusion | bytes 525312 | tf_op jit(solution)/shard_map/gather | solution.py:26
  27.0 1.2 %gather_fusion.4 = bf16[256,512]{1,0:T(8,128)(2,1)S(1)} fusion(bf16[320,512]{1,0:T(8,128)(2,1)S(1)} %pad_maximum_fusion, s32[1024]{0:T(1024)S(1)} %pad_clamp_fusion.6), kind=kCustom, calls=%fused_computation.4 | custom fusion | bytes 525312 | tf_op jit(solution)/shard_map/gather | solution.py:26
  28.1 1.2 %gather_fusion.5 = bf16[256,512]{1,0:T(8,128)(2,1)S(1)} fusion(bf16[320,512]{1,0:T(8,128)(2,1)S(1)} %pad_maximum_fusion, s32[1024]{0:T(1024)S(1)} %pad_clamp_fusion.5), kind=kCustom, calls=%fused_computation.5 | custom fusion | bytes 525312 | tf_op jit(solution)/shard_map/gather | solution.py:26
  29.3 1.2 %gather_fusion.6 = bf16[256,512]{1,0:T(8,128)(2,1)S(1)} fusion(bf16[320,512]{1,0:T(8,128)(2,1)S(1)} %pad_maximum_fusion, s32[1024]{0:T(1024)S(1)} %pad_clamp_fusion.4), kind=kCustom, calls=%fused_computation.6 | custom fusion | bytes 525312 | tf_op jit(solution)/shard_map/gather | solution.py:26
  30.5 1.2 %gather_fusion.7 = bf16[256,512]{1,0:T(8,128)(2,1)S(1)} fusion(bf16[320,512]{1,0:T(8,128)(2,1)S(1)} %pad_maximum_fusion, s32[1024]{0:T(1024)S(1)} %pad_clamp_fusion.3), kind=kCustom, calls=%fused_computation.7 | custom fusion | bytes 525312 | tf_op jit(solution)/shard_map/gather | solution.py:26
  31.6 1.2 %gather_fusion.8 = bf16[256,512]{1,0:T(8,128)(2,1)S(1)} fusion(bf16[320,512]{1,0:T(8,128)(2,1)S(1)} %pad_maximum_fusion, s32[1024]{0:T(1024)S(1)} %pad_clamp_fusion.2), kind=kCustom, calls=%fused_computation.8 | custom fusion | bytes 525312 | tf_op jit(solution)/shard_map/gather | solution.py:26
  32.8 1.2 %gather_fusion.9 = bf16[256,512]{1,0:T(8,128)(2,1)S(1)} fusion(bf16[320,512]{1,0:T(8,128)(2,1)S(1)} %pad_maximum_fusion, s32[1024]{0:T(1024)S(1)} %pad_clamp_fusion.1), kind=kCustom, calls=%fused_computation.9 | custom fusion | bytes 525312 | tf_op jit(solution)/shard_map/gather | solution.py:26
  33.9 0.8 multiply_reduce_fusion
  34.7 0.0 copy-start.1
  34.7 13.7 %all-gather.2.cloned.1.call-done = bf16[1024,512]{1,0:T(8,128)(2,1)} async-done(((bf16[256,512]{1,0:T(8,128)(2,1)}), bf16[1024,512]{1,0:T(8,128)(2,1)}) %all-gather.2.cloned.1.call-update) | async-done | bytes 1048592 | tf_op jit(solution)/shard_map/all_gather | solution.py:36
  48.4 2.7 %fusion.2 = f32[256,1024]{1,0:T(8,128)} fusion(bf16[256,512]{1,0:T(8,128)(2,1)S(1)} %get-tuple-element.3, bf16[1024,512]{1,0:T(8,128)(2,1)} %all-gather.2.cloned.1.call-done), kind=kOutput, calls=%fused_computation.43 | convolution fusion | flops 268435456 | bytes 2359296 | tf_op jit(solution)/shard_map/dot_general | solution.py:34
  51.1 0.0 copy-done.1
  51.1 0.0 reduce-scatter.2.cloned.1.call-update
  51.1 6.4 %psum.7 = f32[256]{0:T(256)S(1)} all-reduce(f32[256]{0:T(256)S(1)} %get-tuple-element.2), channel_id=1, replica_groups=mesh['groups'=2,'gallery'=4,'query'=4] {'query'}, use_global_device_ids=true, to_apply=%region_3.4 | all-reduce | flops 256 | bytes 2048 | tf_op jit(solution)/shard_map/psum | solution.py:33
  57.6 18.1 %reduce-scatter.2.cloned.1.call-done = f32[256,256]{1,0:T(8,128)} async-done(((f32[256,1024]{1,0:T(8,128)}), f32[256,256]{1,0:T(8,128)}) %reduce-scatter.2.cloned.1.call-update) | async-done | bytes 262160 | tf_op jit(solution)/shard_map/reduce_scatter | solution.py:40
  75.7 1.7 %multiply_convert_fusion = bf16[256,256]{1,0:T(8,128)(2,1)} fusion(f32[256,256]{1,0:T(8,128)} %reduce-scatter.2.cloned.1.call-done, f32[256]{0:T(256)S(1)} %rsqrt_multiply_fusion), kind=kLoop, calls=%fused_computation.14 | loop fusion | flops 131072 | bytes 394240 | tf_op jit(solution)/shard_map/convert_element_type | solution.py:42
  (20 shorter events, 0.2 us)
Async XLA Ops:
  7.2 0.7 copy-start.4
  10.2 7.2 %copy-start.3 = (s32[256,10]{0,1:T(8,128)S(1)}, s32[256,10]{0,1:T(8,128)}, u32[]{:S(2)}) copy-start(s32[256,10]{0,1:T(8,128)} %param.6) | copy-start | bytes 30724
  10.2 12.2 %all-to-all-start = ((bf16[4,16,512]{2,1,0:T(8,128)(2,1)}), bf16[4,16,512]{2,1,0:T(8,128)(2,1)S(1)}, u32[]{:S(2)}, u32[]{:S(2)}) async-start(bf16[4,16,512]{2,1,0:T(8,128)(2,1)} %bitcast.3), calls=%async_computation | async-start | bytes 131072 | tf_op jit(solution)/shard_map/all_to_all | solution.py:18
  16.6 5.7 %copy-start = (bf16[256,512]{1,0:T(8,128)(2,1)S(1)}, bf16[256,512]{1,0:T(8,128)(2,1)}, u32[]{:S(2)}) copy-start(bf16[256,512]{1,0:T(8,128)(2,1)} %param.5) | copy-start | bytes 786436
  16.6 31.8 %all-gather.2.cloned.1.call-start = ((), (), s32[]{:S(2)}) async-start(), calls=%async_computation.2 | async-start | bytes 1310720 | tf_op jit(solution)/shard_map/all_gather | solution.py:36
  17.3 58.3 %reduce-scatter.2.cloned.1.call-start = ((), (), s32[]{:S(2)}) async-start(), calls=%async_computation.3 | async-start | bytes 1310720 | tf_op jit(solution)/shard_map/reduce_scatter | solution.py:40
  17.4 0.7 copy-start.2
  34.7 16.4 %copy-start.1 = (bf16[256,512]{1,0:T(8,128)(2,1)}, bf16[256,512]{1,0:T(8,128)(2,1)S(1)}, u32[]{:S(2)}) copy-start(bf16[256,512]{1,0:T(8,128)(2,1)S(1)} %get-tuple-element.3) | copy-start | bytes 786436
Sparse Core Ops, SparseCore 0:
  19.0 29.3 all-gather.1
  51.2 24.3 reduce-scatter.1
where the time goes:
time: 84.6 us; the launch traced here: 84.2 us
  waiting for transfers between devices  36.7 us (43%)
  local copies, waits for them, and re-layouts  15.2 us (18%)
  between operations  14.2 us (17%)
  starting transfers between devices  6.49 us (8%)
  blocking collectives  6.43 us (8%)
  matrix products  2.66 us (3%)
  other arithmetic  2.64 us (3%)
    reduce_scatter x1, waiting for transfers between devices, per_device(): lax.psum_scatter(partial_value, 'query', scatter_dimension=1, tiled=True)  18.1 us
    all_gather x1, waiting for transfers between devices, per_device(): lax.all_gather(queries, 'gallery', axis=0, tiled=True)  13.7 us
    gather x10, local copies, waits for them, and re-layouts, per_device(): picked = table[row_index[:, which]].astype(jnp.float32)  11.5 us
    all_to_all x1, starting transfers between devices, per_device(): lax.all_to_all(gallery[outgoing], 'gallery', split_axis=0, concat_axis=0,...  6.45 us
    psum x1, blocking collectives, per_device(): squares = lax.psum(jnp.sum(floats * floats, axis=1), 'query')  6.43 us
    all_to_all x1, waiting for transfers between devices, per_device(): lax.all_to_all(gallery[outgoing], 'gallery', split_axis=0, concat_axis=0,...  4.07 us
    dot_general x1, matrix products, per_device(): lax.dot_general(refined, lax.all_gather(queries, 'gallery', axis=0, tiled...  2.66 us
    gather x1, local copies, waits for them, and re-layouts, per_device(): gallery[outgoing]  2.33 us
  transfers between devices with their start and end apart: 3, of which 3 were waited for; matrix products, arithmetic and copies ran while one was open for 15% of the time, Pallas kernels for 0%

commit v1 on v0

v1 whole, which is shorter than its diff:
```python
import math

import jax
import jax.numpy as jnp
from jax import lax
from jax.sharding import PartitionSpec as P

D = 2048


self_weight = 4.0
epsilon = 1e-06

AXES = ("groups", "gallery", "query")


def weight_matrix(columns, neighbour, weights, width):
    row_count = neighbour.shape[0]
    places = lax.broadcasted_iota(jnp.int32, (row_count, width), 1)
    owners = lax.broadcasted_iota(jnp.int32, (row_count, width), 0)
    matrix = jnp.where(places == owners, jnp.int32(self_weight), 0)
    for which in range(neighbour.shape[1]):
        matrix = matrix + jnp.where(places == columns[:, which][:, None], weights[:, which][:, None], 0)
    return matrix.astype(jnp.bfloat16)


def dot_rows(left, right):
    return lax.dot_general(left, right, (((1,), (1,)), ((), ())), preferred_element_type=jnp.float32)


def generic(gallery, neighbour, weights, send_rows, queries):
    row_count = gallery.shape[0]
    arrived = lax.all_to_all(gallery[send_rows[0]], "gallery", split_axis=0, concat_axis=0, tiled=True)
    table = jnp.concatenate([gallery, arrived], axis=0)
    matrix = weight_matrix(neighbour, neighbour, weights, table.shape[0])
    summed = lax.dot_general(matrix, table, (((1,), (0,)), ((), ())), preferred_element_type=jnp.float32)
    denominator = self_weight + jnp.sum(weights.astype(jnp.float32), axis=1)
    refined = (summed / denominator[:, None]).astype(jnp.bfloat16)
    floats = refined.astype(jnp.float32)
    squares = lax.psum(jnp.sum(floats * floats, axis=1), "query")
    partial_value = dot_rows(refined, lax.all_gather(queries, "gallery", axis=0, tiled=True))
    raw = lax.psum_scatter(partial_value, "query", scatter_dimension=1, tiled=True)
    inverse = lax.rsqrt(squares / D + epsilon) / math.sqrt(D)
    return (refined, (raw * inverse[:, None]).astype(jnp.bfloat16))


def line_of_four(shape, gallery, neighbour, weights, send_rows, queries):
    groups, shards, blocks = shape
    row_count, col_count = gallery.shape
    cap = send_rows.shape[1] // shards
    half_rows = queries.shape[0] // 2
    g, z, q = (lax.axis_index(name) for name in AXES)

    def place(device):
        return (device[0] * shards + device[1]) * blocks + device[2]

    def send(value, to):
        pairs = []
        for gg in range(groups):
            for zz in range(shards):
                for qq in range(blocks):
                    target = to(gg, zz, qq)
                    if target is not None:
                        pairs.append((place((gg, zz, qq)), place(target)))
        return lax.ppermute(value, AXES, pairs)

    def is_far_core(zz, qq):
        return (qq + zz) % 2 == 1

    odd = is_far_core(z, q)
    near = q // 2 == z // 2

    mine = lax.dynamic_slice_in_dim(queries, g * half_rows, half_rows)
    other = lax.dynamic_slice_in_dim(queries, (1 - g) * half_rows, half_rows)
    third = send(mine, lambda g, z, q: (g, z ^ 3, q))
    first = send(mine, lambda g, z, q: (g, z ^ 1, q))

    rows = []
    for step in (1, 2, 3):
        wanted = lax.dynamic_slice_in_dim(send_rows[0], (z ^ step) * cap, cap)
        rows.append(send(gallery[wanted], lambda g, z, q, step=step: (g, z ^ step, q)))
    table = jnp.concatenate([gallery, *rows], axis=0)
    slot = jnp.maximum(neighbour - row_count, 0)
    columns = jnp.where(
        neighbour < row_count, neighbour, row_count + (((slot // cap) ^ z) - 1) * cap + slot % cap
    )
    matrix = weight_matrix(columns, neighbour, weights, table.shape[0])
    summed = lax.dot_general(matrix, table, (((1,), (0,)), ((), ())), preferred_element_type=jnp.float32)
    denominator = self_weight + jnp.sum(weights.astype(jnp.float32), axis=1)
    refined = (summed / denominator[:, None]).astype(jnp.bfloat16)
    refined_pair = send(refined, lambda g, z, q: (g, z, q ^ 1))
    floats = refined.astype(jnp.float32)
    floats_pair = refined_pair.astype(jnp.float32)
    squares = jnp.sum(floats * floats, axis=1) + jnp.sum(floats_pair * floats_pair, axis=1)
    squares = squares + send(squares, lambda g, z, q: (g, z, q ^ 2))
    inverse = lax.rsqrt(squares / D + epsilon) / math.sqrt(D)

    first_other = send(first, lambda g, z, q: (1 - g, z, q))
    leave = jnp.concatenate([jnp.where(odd, mine, first), jnp.where(odd, other, first_other)], axis=0)
    stay = jnp.concatenate([jnp.where(odd, first, mine), jnp.where(odd, first_other, other)], axis=0)
    came = send(leave, lambda g, z, q: (g, z, q ^ 1))
    early = dot_rows(refined, stay) + dot_rows(refined_pair, came)

    a = send(third, lambda g, z, q: (1 - g, z, q) if is_far_core(z, q) else (g, z ^ 1, q ^ 1))
    b = send(third, lambda g, z, q: (g, z ^ 1, q) if is_far_core(z, q) else (1 - g, z, q ^ 1))
    c = send(third, lambda g, z, q: (1 - g, z ^ 1, q) if is_far_core(z, q) else (g, z, q ^ 1))
    d = send(third, lambda g, z, q: None if is_far_core(z, q) else (1 - g, z ^ 1, q ^ 1))
    own = jnp.concatenate([jnp.where(odd, third, b), jnp.where(odd, a, c)], axis=0)
    pair = jnp.concatenate([jnp.where(odd, c, a), jnp.where(odd, b, d)], axis=0)
    late = dot_rows(refined, own) + dot_rows(refined_pair, pair)

    leaving = jnp.where(near, late, early).astype(jnp.bfloat16)
    arriving = send(leaving, lambda g, z, q: (g, z, q ^ 2))
    raw = jnp.where(near, early, late) + arriving.astype(jnp.float32)
    scores = (raw * inverse[:, None]).astype(jnp.bfloat16)
    scores = jnp.where(g == 0, scores, jnp.roll(scores, half_rows, axis=1))
    return (refined, scores)


def solution(mesh):
    shape = tuple(mesh.shape[name] for name in AXES)

    def per_device(*arrays):
        if shape == (2, 4, 4):
            return line_of_four(shape, *arrays)
        return generic(*arrays)

    return jax.shard_map(
        per_device,
        mesh=mesh,
        in_specs=(
            P(("groups", "gallery"), "query"),
            P(("groups", "gallery"), None),
            P(("groups", "gallery"), None),
            P(("groups", "gallery"), None),
            P("gallery", "query"),
        ),
        out_specs=(P(("groups", "gallery"), "query"), P(("groups", "gallery"), "query")),
        check_vma=False,
    )
```

time: 84.6 us -> 43.3 us (0.51)
  waiting for transfers between devices: 36.7 us -> 14.6 us
  starting transfers between devices: 6.49 us -> 20.7 us
  between operations: 14.2 us -> 0.93 us
  local copies, waits for them, and re-layouts: 15.2 us -> 4.19 us
  blocking collectives: 6.43 us -> 0 us
  other arithmetic: 2.64 us -> 0.55 us
    ppermute x0 -> x14, starting transfers between devices: none -> 20.7 us  [send(): return lax.ppermute(value, AXES, pairs)]
    reduce_scatter x1 -> x0, waiting for transfers between devices: 18.1 us -> none  [per_device(): lax.psum_scatter(partial_value, 'query', scatter_dimension=1, tiled=True)]
    ppermute x0 -> x14, waiting for transfers between devices: none -> 14.6 us  [send(): return lax.ppermute(value, AXES, pairs)]
    all_gather x1 -> x0, waiting for transfers between devices: 13.7 us -> none  [per_device(): lax.all_gather(queries, 'gallery', axis=0, tiled=True)]
    gather x11 -> x3, local copies, waits for them, and re-layouts: 13.8 us -> 1.77 us  [line_of_four(): gallery[wanted]]
    all_to_all x1 -> x0, starting transfers between devices: 6.45 us -> none  [per_device(): lax.all_to_all(gallery[outgoing], 'gallery', split_axis=0, concat_axis=0,...]
    psum x1 -> x0, blocking collectives: 6.43 us -> none  [per_device(): squares = lax.psum(jnp.sum(floats * floats, axis=1), 'query')]
    all_to_all x1 -> x0, waiting for transfers between devices: 4.07 us -> none  [per_device(): lax.all_to_all(gallery[outgoing], 'gallery', split_axis=0, concat_axis=0,...]
  transfers between devices with their start and end apart: 3 -> 14, of which waited for: 3 -> 6; matrix products, arithmetic and copies ran while one was open for 15% -> 10% of each run, Pallas kernels for 0% -> 0%
where the time goes in v1:
time: 43.3 us; the launch traced here: 43 us
  starting transfers between devices  20.7 us (48%)
  waiting for transfers between devices  14.6 us (34%)
  local copies, waits for them, and re-layouts  4.19 us (10%)
  matrix products  2.14 us (5%)
  between operations  0.93 us (2%)
  other arithmetic  0.55 us (1%)
    ppermute x14, starting transfers between devices, send(): return lax.ppermute(value, AXES, pairs)  20.7 us
    ppermute x14, waiting for transfers between devices, send(): return lax.ppermute(value, AXES, pairs)  14.6 us
    gather x3, local copies, waits for them, and re-layouts, line_of_four(): gallery[wanted]  1.77 us
    unnamed x13, local copies, waits for them, and re-layouts  1.44 us
    dot_general x1, matrix products, line_of_four(): lax.dot_general(matrix, table, (((1,), (0,)), ((), ())), preferred_elemen...  1.1 us
    dot_general x4, matrix products, dot_rows(): lax.dot_general(left, right, (((1,), (1,)), ((), ())), preferred_element_...  1.04 us
    dynamic_slice x1, local copies, waits for them, and re-layouts, line_of_four(): mine = lax.dynamic_slice_in_dim(queries, g * half_rows, half_rows)  0.96 us
  transfers between devices with their start and end apart: 14, of which 6 were waited for; matrix products, arithmetic and copies ran while one was open for 10% of the time, Pallas kernels for 0%

profile of v1, /device:TPU:0, one launch (start us, length us, event | category | flops | bytes accessed | tf_op | source)
XLA Modules:
  0.0 43.0 jit_solution(15565547297030313717)
XLA Ops:
  0.6 0.0 copy-start.1
  0.6 1.0 %constant_dynamic-slice_fusion = bf16[128,512]{1,0:T(8,128)(2,1)S(1)} fusion(bf16[256,512]{1,0:T(8,128)(2,1)} %param.9, s32[]{:T(128)S(6)} %select_n.190), kind=kLoop, calls=%fused_computation.94 | loop fusion | bytes 262148 | tf_op jit(solution)/shard_map/dynamic_slice | solution.py:73
  1.6 3.1 %collective-permute-start.3 = (bf16[128,512]{1,0:T(8,128)(2,1)S(1)}, bf16[128,512]{1,0:T(8,128)(2,1)S(1)}, u32[]{:S(2)}, u32[]{:S(2)}) collective-permute-start(bf16[128,512]{1,0:T(8,128)(2,1)S(1)} %constant_dynamic-slice_fusion), channel_id=1, source_target_pairs={{0,4},{1,5},{2,6},{3,7},{4,0},{5,1},{6,2},{7,3},{8,12},{9,13},{10,... | collective-permute-start | bytes 393224 | tf_op jit(solution)/shard_map/ppermute | solution.py:65
  4.7 2.5 %collective-permute-start.7 = (bf16[128,512]{1,0:T(8,128)(2,1)S(1)}, bf16[128,512]{1,0:T(8,128)(2,1)S(1)}, u32[]{:S(2)}, u32[]{:S(2)}) collective-permute-start(bf16[128,512]{1,0:T(8,128)(2,1)S(1)} %constant_dynamic-slice_fusion), channel_id=1, source_target_pairs={{0,12},{1,13},{2,14},{3,15},{4,8},{5,9},{6,10},{7,11},{8,4},{9,5},... | collective-permute-start | bytes 393224 | tf_op jit(solution)/shard_map/ppermute | solution.py:65
  7.2 0.7 %copy-done.5 = s32[1,64]{1,0:T(1,128)S(1)} copy-done((s32[1,64]{1,0:T(1,128)S(1)}, s32[1,64]{1,0:T(1,128)}, u32[]{:S(2)}) %copy-start.5) | copy-done | bytes 280
  7.8 0.1 fusion.54
  7.9 0.6 %gather_fusion.2 = bf16[16,512]{1,0:T(8,128)(2,1)S(1)} fusion(bf16[256,512]{1,0:T(8,128)(2,1)S(1)} %copy-done.1, s32[1024]{0:T(1024)S(1)} %pad_clamp_fusion), kind=kCustom, calls=%fused_computation.2 | custom fusion | bytes 32832 | tf_op jit(solution)/shard_map/gather | solution.py:81
  8.5 1.4 %collective-permute-start.2 = (bf16[16,512]{1,0:T(8,128)(2,1)S(1)}, bf16[16,512]{1,0:T(8,128)(2,1)S(1)}, u32[]{:S(2)}, u32[]{:S(2)}) collective-permute-start(bf16[16,512]{1,0:T(8,128)(2,1)S(1)} %gather_fusion.2), channel_id=1, source_target_pairs={{0,12},{1,13},{2,14},{3,15},{4,8},{5,9},{6,10},{7,11},{8,4},{9,5},... | collective-permute-start | bytes 49160 | tf_op jit(solution)/shard_map/ppermute | solution.py:65
  9.9 0.6 %gather_fusion.1 = bf16[16,512]{1,0:T(8,128)(2,1)S(1)} fusion(bf16[256,512]{1,0:T(8,128)(2,1)S(1)} %copy-done.1, s32[1024]{0:T(1024)S(1)} %pad_clamp_fusion.1), kind=kCustom, calls=%fused_computation.1 | custom fusion | bytes 32832 | tf_op jit(solution)/shard_map/gather | solution.py:81
  10.5 0.9 %collective-permute-start.1 = (bf16[16,512]{1,0:T(8,128)(2,1)S(1)}, bf16[16,512]{1,0:T(8,128)(2,1)S(1)}, u32[]{:S(2)}, u32[]{:S(2)}) collective-permute-start(bf16[16,512]{1,0:T(8,128)(2,1)S(1)} %gather_fusion.1), channel_id=1, source_target_pairs={{0,8},{1,9},{2,10},{3,11},{4,12},{5,13},{6,14},{7,15},{8,0},{9,1},... | collective-permute-start | bytes 49160 | tf_op jit(solution)/shard_map/ppermute | solution.py:65
  11.4 0.6 %gather_fusion = bf16[16,512]{1,0:T(8,128)(2,1)S(1)} fusion(bf16[256,512]{1,0:T(8,128)(2,1)S(1)} %copy-done.1, s32[1024]{0:T(1024)S(1)} %pad_clamp_fusion.2), kind=kCustom, calls=%fused_computation | custom fusion | bytes 32832 | tf_op jit(solution)/shard_map/gather | solution.py:81
  12.0 0.0 copy-start.4
  12.0 2.3 %collective-permute-start = (bf16[16,512]{1,0:T(8,128)(2,1)S(1)}, bf16[16,512]{1,0:T(8,128)(2,1)S(1)}, u32[]{:S(2)}, u32[]{:S(2)}) collective-permute-start(bf16[16,512]{1,0:T(8,128)(2,1)S(1)} %gather_fusion), channel_id=1, source_target_pairs={{0,4},{1,5},{2,6},{3,7},{4,0},{5,1},{6,2},{7,3},{8,12},{9,13},{10,... | collective-permute-start | bytes 49160 | tf_op jit(solution)/shard_map/ppermute | solution.py:65
  14.3 0.0 copy-done.3
  14.3 0.0 copy-done.4
  14.5 0.0 collective-permute-done.2
  14.5 0.8 %collective-permute-done.1 = bf16[16,512]{1,0:T(8,128)(2,1)S(1)} collective-permute-done((bf16[16,512]{1,0:T(8,128)(2,1)S(1)}, bf16[16,512]{1,0:T(8,128)(2,1)S(1)}, u32[]{:S(2)}, u32[]{:S(2)}) %collective-permute-start.1) | collective-permute-done | bytes 16416 | tf_op jit(solution)/shard_map/ppermute | solution.py:65
  15.2 0.8 %collective-permute-done = bf16[16,512]{1,0:T(8,128)(2,1)S(1)} collective-permute-done((bf16[16,512]{1,0:T(8,128)(2,1)S(1)}, bf16[16,512]{1,0:T(8,128)(2,1)S(1)}, u32[]{:S(2)}, u32[]{:S(2)}) %collective-permute-start) | collective-permute-done | bytes 16416 | tf_op jit(solution)/shard_map/ppermute | solution.py:65
  16.0 1.1 %multiply_reduce_fusion.1 = (f32[256]{0:T(256)S(1)}, bf16[256,512]{1,0:T(8,128)(2,1)S(1)}) fusion(f32[256]{0:T(256)S(1)} %broadcast_add_fusion, bf16[16,512]{1,0:T(8,128)(2,1)S(1)} %collective-permute-done.2, bf16[16,512]{1,0:T(8,128)(2,1)S(1)} %collective-permute-done.1, bf16[16,512]{1,0:T(8,128)(2,1)S(1)} %collective-permute-done, ...), kind=kOutput, calls=%fused_computation.8 | convolution fusion | flops 84160256 | bytes 595968 | tf_op jit(solution)/shard_map/dot_general | solution.py:88
  17.1 0.0 copy-start
  17.1 0.1 collective-permute-start.5
  17.2 0.0 collective-permute-done.7
  17.2 1.6 %collective-permute-start.8 = (bf16[128,512]{1,0:T(8,128)(2,1)S(1)}, bf16[128,512]{1,0:T(8,128)(2,1)S(1)}, u32[]{:S(2)}, u32[]{:S(2)}) collective-permute-start(bf16[128,512]{1,0:T(8,128)(2,1)S(1)} %collective-permute-done.7), channel_id=1, source_target_pairs={{0,17},{1,5},{2,19},{3,7},{4,0},{5,20},{6,2},{7,22},{8,25},{9,13},... | collective-permute-start | bytes 393224 | tf_op jit(solution)/shard_map/ppermute | solution.py:65
  18.8 3.5 %collective-permute-start.11 = (bf16[128,512]{1,0:T(8,128)(2,1)S(1)}, bf16[128,512]{1,0:T(8,128)(2,1)S(1)}, u32[]{:S(2)}, u32[]{:S(2)}) collective-permute-start(bf16[128,512]{1,0:T(8,128)(2,1)S(1)} %collective-permute-done.7), channel_id=1, source_target_pairs={{0,21},{2,23},{5,16},{7,18},{8,29},{10,31},{13,24},{15,26},{16,5},... | collective-permute-start | bytes 393224 | tf_op jit(solution)/shard_map/ppermute | solution.py:65
  22.4 0.1 collective-permute-start.9
  22.5 0.0 collective-permute-done.3
  22.5 1.5 %collective-permute-start.4 = (bf16[128,512]{1,0:T(8,128)(2,1)S(1)}, bf16[128,512]{1,0:T(8,128)(2,1)S(1)}, u32[]{:S(2)}, u32[]{:S(2)}) collective-permute-start(bf16[128,512]{1,0:T(8,128)(2,1)S(1)} %collective-permute-done.3), channel_id=1, source_target_pairs={{0,16},{1,17},{2,18},{3,19},{4,20},{5,21},{6,22},{7,23},{8,24},{9,... | collective-permute-start | bytes 393224 | tf_op jit(solution)/shard_map/ppermute | solution.py:65
  24.1 0.1 broadcast_select_fusion.7
  24.1 4.3 %collective-permute-done.4 = bf16[128,512]{1,0:T(8,128)(2,1)S(1)} collective-permute-done((bf16[128,512]{1,0:T(8,128)(2,1)S(1)}, bf16[128,512]{1,0:T(8,128)(2,1)S(1)}, u32[]{:S(2)}, u32[]{:S(2)}) %collective-permute-start.4) | collective-permute-done | bytes 131104 | tf_op jit(solution)/shard_map/ppermute | solution.py:65
  28.4 0.0 collective-permute-start.10
  28.4 0.1 broadcast_select_fusion.6
  28.5 0.0 collective-permute-done.9
  28.5 1.5 %collective-permute-start.6 = (bf16[256,512]{1,0:T(8,128)(2,1)S(1)}, bf16[256,512]{1,0:T(8,128)(2,1)S(1)}, u32[]{:S(2)}, u32[]{:S(2)}) collective-permute-start(bf16[256,512]{1,0:T(8,128)(2,1)S(1)} %pad_maximum_fusion), channel_id=1, source_target_pairs={{0,1},{1,0},{2,3},{3,2},{4,5},{5,4},{6,7},{7,6},{8,9},{9,8},{10,11... | collective-permute-start | bytes 786440 | tf_op jit(solution)/shard_map/ppermute | solution.py:65
  30.0 4.3 %collective-permute-done.10 = bf16[128,512]{1,0:T(8,128)(2,1)S(1)} collective-permute-done((bf16[128,512]{1,0:T(8,128)(2,1)S(1)}, bf16[128,512]{1,0:T(8,128)(2,1)S(1)}, u32[]{:S(2)}, u32[]{:S(2)}) %collective-permute-start.10) | collective-permute-done | bytes 131104 | tf_op jit(solution)/shard_map/ppermute | solution.py:65
  34.3 0.0 collective-permute-done.8
  34.3 0.0 collective-permute-done.11
  34.3 0.0 collective-permute-done.5
  34.4 0.1 multiply_reduce_fusion
  34.5 1.6 %collective-permute-start.13 = (f32[256]{0:T(256)S(1)}, f32[256]{0:T(256)S(1)}, u32[]{:S(2)}, u32[]{:S(2)}) collective-permute-start(f32[256]{0:T(256)S(1)} %add.158), channel_id=1, source_target_pairs={{0,2},{1,3},{2,0},{3,1},{4,6},{5,7},{6,4},{7,5},{8,10},{9,11},{10,... | collective-permute-start | bytes 3080 | tf_op jit(solution)/shard_map/ppermute | solution.py:65
  36.1 0.3 fusion.14
  36.3 0.0 collective-permute-done.6
  36.3 0.3 fusion.65
  36.6 0.3 convolution_add_fusion.1
  36.9 0.3 select_convert_fusion
  37.1 0.6 %collective-permute-start.12 = (bf16[256,256]{0,1:T(8,128)(2,1)S(1)}, bf16[256,256]{0,1:T(8,128)(2,1)S(1)}, u32[]{:S(2)}, u32[]{:S(2)}) collective-permute-start(bf16[256,256]{0,1:T(8,128)(2,1)S(1)} %get-tuple-element.37), channel_id=1, source_target_pairs={{0,2},{1,3},{2,0},{3,1},{4,6},{5,7},{6,4},{7,5},{8,10},{9,11},{10,... | collective-permute-start | bytes 393224 | tf_op jit(solution)/shard_map/ppermute | solution.py:65
  37.7 0.4 collective-permute-done.13
  38.2 4.0 %collective-permute-done.12 = bf16[256,256]{0,1:T(8,128)(2,1)S(1)} collective-permute-done((bf16[256,256]{0,1:T(8,128)(2,1)S(1)}, bf16[256,256]{0,1:T(8,128)(2,1)S(1)}, u32[]{:S(2)}, u32[]{:S(2)}) %collective-permute-start.12) | collective-permute-done | bytes 131104 | tf_op jit(solution)/shard_map/ppermute | solution.py:65
  42.3 0.8 %copy.7 = bf16[256,256]{1,0:T(8,128)(2,1)} copy(bf16[256,256]{0,1:T(8,128)(2,1)S(1)} %maximum_select_fusion) | data formatting | bytes 262144
  (22 shorter events, 0.3 us)
Async XLA Ops:
  0.6 7.3 %copy-start.1 = (bf16[256,512]{1,0:T(8,128)(2,1)S(1)}, bf16[256,512]{1,0:T(8,128)(2,1)}, u32[]{:S(2)}) copy-start(bf16[256,512]{1,0:T(8,128)(2,1)} %param.5) | copy-start | bytes 786436
  1.6 20.9 %collective-permute-start.3 = (bf16[128,512]{1,0:T(8,128)(2,1)S(1)}, bf16[128,512]{1,0:T(8,128)(2,1)S(1)}, u32[]{:S(2)}, u32[]{:S(2)}) collective-permute-start(bf16[128,512]{1,0:T(8,128)(2,1)S(1)} %constant_dynamic-slice_fusion), channel_id=1, source_target_pairs={{0,4},{1,5},{2,6},{3,7},{4,0},{5,1},{6,2},{7,3},{8,12},{9,13},{10,... | collective-permute-start | bytes 393224 | tf_op jit(solution)/shard_map/ppermute | solution.py:65
  4.7 12.5 %collective-permute-start.7 = (bf16[128,512]{1,0:T(8,128)(2,1)S(1)}, bf16[128,512]{1,0:T(8,128)(2,1)S(1)}, u32[]{:S(2)}, u32[]{:S(2)}) collective-permute-start(bf16[128,512]{1,0:T(8,128)(2,1)S(1)} %constant_dynamic-slice_fusion), channel_id=1, source_target_pairs={{0,12},{1,13},{2,14},{3,15},{4,8},{5,9},{6,10},{7,11},{8,4},{9,5},... | collective-permute-start | bytes 393224 | tf_op jit(solution)/shard_map/ppermute | solution.py:65
  7.2 0.7 %copy-start.5 = (s32[1,64]{1,0:T(1,128)S(1)}, s32[1,64]{1,0:T(1,128)}, u32[]{:S(2)}) copy-start(s32[1,64]{1,0:T(1,128)} %param.8) | copy-start | bytes 772
  8.5 5.9 %collective-permute-start.2 = (bf16[16,512]{1,0:T(8,128)(2,1)S(1)}, bf16[16,512]{1,0:T(8,128)(2,1)S(1)}, u32[]{:S(2)}, u32[]{:S(2)}) collective-permute-start(bf16[16,512]{1,0:T(8,128)(2,1)S(1)} %gather_fusion.2), channel_id=1, source_target_pairs={{0,12},{1,13},{2,14},{3,15},{4,8},{5,9},{6,10},{7,11},{8,4},{9,5},... | collective-permute-start | bytes 49160 | tf_op jit(solution)/shard_map/ppermute | solution.py:65
  10.5 4.7 %collective-permute-start.1 = (bf16[16,512]{1,0:T(8,128)(2,1)S(1)}, bf16[16,512]{1,0:T(8,128)(2,1)S(1)}, u32[]{:S(2)}, u32[]{:S(2)}) collective-permute-start(bf16[16,512]{1,0:T(8,128)(2,1)S(1)} %gather_fusion.1), channel_id=1, source_target_pairs={{0,8},{1,9},{2,10},{3,11},{4,12},{5,13},{6,14},{7,15},{8,0},{9,1},... | collective-permute-start | bytes 49160 | tf_op jit(solution)/shard_map/ppermute | solution.py:65
  11.4 2.9 %copy-start.3 = (s32[256,10]{0,1:T(8,128)S(1)}, s32[256,10]{0,1:T(8,128)}, u32[]{:S(2)}) copy-start(s32[256,10]{0,1:T(8,128)} %param.7) | copy-start | bytes 30724
  12.0 2.4 %copy-start.4 = (s32[256,10]{0,1:T(8,128)S(1)}, s32[256,10]{0,1:T(8,128)}, u32[]{:S(2)}) copy-start(s32[256,10]{0,1:T(8,128)} %param.6) | copy-start | bytes 30724
  12.0 4.0 %collective-permute-start = (bf16[16,512]{1,0:T(8,128)(2,1)S(1)}, bf16[16,512]{1,0:T(8,128)(2,1)S(1)}, u32[]{:S(2)}, u32[]{:S(2)}) collective-permute-start(bf16[16,512]{1,0:T(8,128)(2,1)S(1)} %gather_fusion), channel_id=1, source_target_pairs={{0,4},{1,5},{2,6},{3,7},{4,0},{5,1},{6,2},{7,3},{8,12},{9,13},{10,... | collective-permute-start | bytes 49160 | tf_op jit(solution)/shard_map/ppermute | solution.py:65
  16.0 8.0 %copy-start.2 = (bf16[256,512]{1,0:T(8,128)(2,1)S(1)}, bf16[256,512]{1,0:T(8,128)(2,1)}, u32[]{:S(2)}) copy-start(bf16[256,512]{1,0:T(8,128)(2,1)} %param.9) | copy-start | bytes 786436
  17.1 19.7 %copy-start = (bf16[256,512]{1,0:T(8,128)(2,1)}, bf16[256,512]{1,0:T(8,128)(2,1)S(1)}, u32[]{:S(2)}) copy-start(bf16[256,512]{1,0:T(8,128)(2,1)S(1)} %get-tuple-element.40) | copy-start | bytes 786436
  17.1 17.2 %collective-permute-start.5 = (bf16[256,512]{1,0:T(8,128)(2,1)S(1)}, bf16[256,512]{1,0:T(8,128)(2,1)S(1)}, u32[]{:S(2)}, u32[]{:S(2)}) collective-permute-start(bf16[256,512]{1,0:T(8,128)(2,1)S(1)} %get-tuple-element.40), channel_id=1, source_target_pairs={{0,1},{1,0},{2,3},{3,2},{4,5},{5,4},{6,7},{7,6},{8,9},{9,8},{10,11... | collective-permute-start | bytes 786440 | tf_op jit(solution)/shard_map/ppermute | solution.py:65
  17.2 17.1 %collective-permute-start.8 = (bf16[128,512]{1,0:T(8,128)(2,1)S(1)}, bf16[128,512]{1,0:T(8,128)(2,1)S(1)}, u32[]{:S(2)}, u32[]{:S(2)}) collective-permute-start(bf16[128,512]{1,0:T(8,128)(2,1)S(1)} %collective-permute-done.7), channel_id=1, source_target_pairs={{0,17},{1,5},{2,19},{3,7},{4,0},{5,20},{6,2},{7,22},{8,25},{9,13},... | collective-permute-start | bytes 393224 | tf_op jit(solution)/shard_map/ppermute | solution.py:65
  18.8 15.5 %collective-permute-start.11 = (bf16[128,512]{1,0:T(8,128)(2,1)S(1)}, bf16[128,512]{1,0:T(8,128)(2,1)S(1)}, u32[]{:S(2)}, u32[]{:S(2)}) collective-permute-start(bf16[128,512]{1,0:T(8,128)(2,1)S(1)} %collective-permute-done.7), channel_id=1, source_target_pairs={{0,21},{2,23},{5,16},{7,18},{8,29},{10,31},{13,24},{15,26},{16,5},... | collective-permute-start | bytes 393224 | tf_op jit(solution)/shard_map/ppermute | solution.py:65
  22.4 6.1 %collective-permute-start.9 = (bf16[128,512]{1,0:T(8,128)(2,1)S(1)}, bf16[128,512]{1,0:T(8,128)(2,1)S(1)}, u32[]{:S(2)}, u32[]{:S(2)}) collective-permute-start(bf16[128,512]{1,0:T(8,128)(2,1)S(1)} %collective-permute-done.7), channel_id=1, source_target_pairs={{0,5},{1,17},{2,7},{3,19},{4,20},{5,0},{6,22},{7,2},{8,13},{9,25},... | collective-permute-start | bytes 393224 | tf_op jit(solution)/shard_map/ppermute | solution.py:65
  22.5 5.9 %collective-permute-start.4 = (bf16[128,512]{1,0:T(8,128)(2,1)S(1)}, bf16[128,512]{1,0:T(8,128)(2,1)S(1)}, u32[]{:S(2)}, u32[]{:S(2)}) collective-permute-start(bf16[128,512]{1,0:T(8,128)(2,1)S(1)} %collective-permute-done.3), channel_id=1, source_target_pairs={{0,16},{1,17},{2,18},{3,19},{4,20},{5,21},{6,22},{7,23},{8,24},{9,... | collective-permute-start | bytes 393224 | tf_op jit(solution)/shard_map/ppermute | solution.py:65
  28.4 5.9 %collective-permute-start.10 = (bf16[128,512]{1,0:T(8,128)(2,1)S(1)}, bf16[128,512]{1,0:T(8,128)(2,1)S(1)}, u32[]{:S(2)}, u32[]{:S(2)}) collective-permute-start(bf16[128,512]{1,0:T(8,128)(2,1)S(1)} %collective-permute-done.7), channel_id=1, source_target_pairs={{0,1},{1,21},{2,3},{3,23},{4,16},{5,4},{6,18},{7,6},{8,9},{9,29},{... | collective-permute-start | bytes 393224 | tf_op jit(solution)/shard_map/ppermute | solution.py:65
  28.5 7.8 %collective-permute-start.6 = (bf16[256,512]{1,0:T(8,128)(2,1)S(1)}, bf16[256,512]{1,0:T(8,128)(2,1)S(1)}, u32[]{:S(2)}, u32[]{:S(2)}) collective-permute-start(bf16[256,512]{1,0:T(8,128)(2,1)S(1)} %pad_maximum_fusion), channel_id=1, source_target_pairs={{0,1},{1,0},{2,3},{3,2},{4,5},{5,4},{6,7},{7,6},{8,9},{9,8},{10,11... | collective-permute-start | bytes 786440 | tf_op jit(solution)/shard_map/ppermute | solution.py:65
  34.5 3.7 %collective-permute-start.13 = (f32[256]{0:T(256)S(1)}, f32[256]{0:T(256)S(1)}, u32[]{:S(2)}, u32[]{:S(2)}) collective-permute-start(f32[256]{0:T(256)S(1)} %add.158), channel_id=1, source_target_pairs={{0,2},{1,3},{2,0},{3,1},{4,6},{5,7},{6,4},{7,5},{8,10},{9,11},{10,... | collective-permute-start | bytes 3080 | tf_op jit(solution)/shard_map/ppermute | solution.py:65
  37.1 5.0 %collective-permute-start.12 = (bf16[256,256]{0,1:T(8,128)(2,1)S(1)}, bf16[256,256]{0,1:T(8,128)(2,1)S(1)}, u32[]{:S(2)}, u32[]{:S(2)}) collective-permute-start(bf16[256,256]{0,1:T(8,128)(2,1)S(1)} %get-tuple-element.37), channel_id=1, source_target_pairs={{0,2},{1,3},{2,0},{3,1},{4,6},{5,7},{6,4},{7,5},{8,10},{9,11},{10,... | collective-permute-start | bytes 393224 | tf_op jit(solution)/shard_map/ppermute | solution.py:65

commit v2 on v1

v2 whole, which is shorter than its diff:
```python
import functools
import math

import jax
import jax.numpy as jnp
from jax import lax
from jax.experimental import pallas as pl
from jax.experimental.pallas import tpu as pltpu
from jax.sharding import PartitionSpec as P

D = 2048


self_weight = 4.0
epsilon = 1e-06

AXES = ("groups", "gallery", "query")


def weight_matrix(columns, neighbour, weights, width):
    row_count = neighbour.shape[0]
    places = lax.broadcasted_iota(jnp.int32, (row_count, width), 1)
    owners = lax.broadcasted_iota(jnp.int32, (row_count, width), 0)
    matrix = jnp.where(places == owners, jnp.int32(self_weight), 0)
    for which in range(neighbour.shape[1]):
        matrix = matrix + jnp.where(places == columns[:, which][:, None], weights[:, which][:, None], 0)
    return matrix.astype(jnp.bfloat16)


def dot_rows(left, right):
    return lax.dot_general(left, right, (((1,), (1,)), ((), ())), preferred_element_type=jnp.float32)


def generic(gallery, neighbour, weights, send_rows, queries):
    row_count = gallery.shape[0]
    arrived = lax.all_to_all(gallery[send_rows[0]], "gallery", split_axis=0, concat_axis=0, tiled=True)
    table = jnp.concatenate([gallery, arrived], axis=0)
    matrix = weight_matrix(neighbour, neighbour, weights, table.shape[0])
    summed = lax.dot_general(matrix, table, (((1,), (0,)), ((), ())), preferred_element_type=jnp.float32)
    denominator = self_weight + jnp.sum(weights.astype(jnp.float32), axis=1)
    refined = (summed / denominator[:, None]).astype(jnp.bfloat16)
    floats = refined.astype(jnp.float32)
    squares = lax.psum(jnp.sum(floats * floats, axis=1), "query")
    partial_value = dot_rows(refined, lax.all_gather(queries, "gallery", axis=0, tiled=True))
    raw = lax.psum_scatter(partial_value, "query", scatter_dimension=1, tiled=True)
    inverse = lax.rsqrt(squares / D + epsilon) / math.sqrt(D)
    return (refined, (raw * inverse[:, None]).astype(jnp.bfloat16))


VMEM = pl.BlockSpec(memory_space=pltpu.VMEM)
SPARE = 16


def call(kernel, outs, *operands, scratch=(), flops=0, specs=None):
    size = sum(math.prod(item.shape) * item.dtype.itemsize for item in (*outs, *operands))
    return pl.pallas_call(
        kernel,
        out_shape=list(outs),
        in_specs=specs or [VMEM] * len(operands),
        out_specs=[VMEM] * len(outs),
        scratch_shapes=list(scratch),
        compiler_params=pltpu.CompilerParams(vmem_limit_bytes=16 * 1024 * 1024),
        cost_estimate=pl.CostEstimate(flops=flops, bytes_accessed=size, transcendentals=0),
    )(*operands)


def array(shape, kind):
    return pltpu.VMEM(shape, kind)


def dot_columns(left, right):
    return lax.dot_general(left, right, (((0,), (0,)), ((), ())), preferred_element_type=jnp.float32)


def three_parts(row):
    high = row.astype(jnp.bfloat16).astype(jnp.float32)
    middle = (row - high).astype(jnp.bfloat16).astype(jnp.float32)
    low = row - high - middle
    index = lax.broadcasted_iota(jnp.int32, row.shape, 0)
    parts = jnp.where(index == 0, high, jnp.where(index == 1, middle, jnp.where(index == 2, low, 0.0)))
    return parts.astype(jnp.bfloat16)


def pack_kernel(
    cap, queries, gallery, send_rows, to_third, to_first, to_second, rows_in, lists_in, picked, arrived
):
    g, z = lax.axis_index("groups"), lax.axis_index("gallery")
    half = to_third.shape[0] - cap
    mine = queries.at[pl.ds(pl.multiple_of(g * half, half), half), :]
    copies = [
        pltpu.make_async_copy(send_rows, lists_in, arrived.at[0]),
        pltpu.make_async_copy(gallery, rows_in, arrived.at[1]),
        pltpu.make_async_copy(mine, to_third.at[0:half, :], arrived.at[2]),
        pltpu.make_async_copy(mine, to_first.at[0:half, :], arrived.at[3]),
    ]
    for copy in copies:
        copy.start()
    copies[0].wait()
    shape = (rows_in.shape[0], lists_in.shape[1])
    hot = jnp.where(lax.broadcasted_iota(jnp.int32, shape, 0) == lists_in[0:1, :], 1.0, 0.0).astype(jnp.bfloat16)
    copies[1].wait()
    picked[...] = dot_columns(hot, rows_in[...]).astype(jnp.bfloat16)

    def rows(step):
        return picked[pl.ds(pl.multiple_of(jnp.bitwise_xor(z, step) * cap, cap), cap), :]

    to_third[half:, :] = rows(3)
    to_first[half:, :] = rows(1)
    to_second[...] = rows(2)
    copies[2].wait()
    copies[3].wait()


def refine_kernel(cap, gallery, neighbour, weights, first, second, third, refined, squares):
    z = lax.axis_index("gallery")
    row_count, col_count = gallery.shape
    index = neighbour[...]
    weight = weights[...].astype(jnp.float32)
    slot = jnp.maximum(index - row_count, 0)
    far = (jnp.bitwise_xor(lax.div(slot, cap), z) - 1) * cap + lax.rem(slot, cap)
    far = jnp.where(index >= row_count, far, -1)

    def matrix(places, height, base):
        places_of = lax.broadcasted_iota(jnp.int32, (height, row_count), 0)
        total = base(places_of)
        for which in range(index.shape[0]):
            total = total + jnp.where(places_of == places[which : which + 1, :], weight[which : which + 1, :], 0.0)
        return total.astype(jnp.bfloat16)

    def own(places_of):
        return jnp.where(places_of == lax.broadcasted_iota(jnp.int32, places_of.shape, 1), self_weight, 0.0)

    near_matrix = matrix(index, row_count, own)
    far_matrix = matrix(far, 3 * cap, lambda places_of: jnp.zeros(places_of.shape, jnp.float32))
    half = first.shape[0] - cap
    table = jnp.concatenate([first[half:, :], second[...], third[half:, :]], axis=0)
    summed = dot_columns(near_matrix, gallery[...]) + dot_columns(far_matrix, table)
    denominator = dot_columns(near_matrix, jnp.ones((row_count, 128), jnp.bfloat16)) + dot_columns(
        far_matrix, jnp.ones((3 * cap, 128), jnp.bfloat16)
    )
    for start in range(0, col_count, 128):
        refined[:, start : start + 128] = (summed[:, start : start + 128] / denominator).astype(jnp.bfloat16)
    floats = refined[...].astype(jnp.float32)
    floats = floats * floats
    high = floats.astype(jnp.bfloat16)
    low = (floats - high.astype(jnp.float32)).astype(jnp.bfloat16)
    ones = jnp.ones((SPARE, col_count), jnp.bfloat16)
    squares[...] = dot_rows(ones, high) + dot_rows(ones, low)


def early_kernel(refined, squares, queries, first, first_other, keep, give):
    g, z, q = (lax.axis_index(name) for name in AXES)
    half = first_other.shape[0]
    row_count = refined.shape[0]
    odd = lax.rem(q + z, 2) == 1
    rows = refined[...]
    for place, one in ((g, first), (1 - g, first_other)):
        columns = pl.ds(pl.multiple_of(place * half, half), half)
        mine = queries[columns, :]
        came = one[0:half, :]
        keep[:, columns] = dot_rows(rows, jnp.where(odd, came, mine))
        give[0:row_count, columns] = dot_rows(rows, jnp.where(odd, mine, came)).astype(jnp.bfloat16)
    give[row_count:, :] = three_parts(squares[...])


def late_kernel(refined, third, third_other, second, second_other, keep, give):
    g, z, q = (lax.axis_index(name) for name in AXES)
    half = third_other.shape[0]
    odd = lax.rem(q + z, 2) == 1
    rows = refined[...]
    for place, one, two in ((g, third, second), (1 - g, third_other, second_other)):
        columns = pl.ds(pl.multiple_of(place * half, half), half)
        one, two = one[0:half, :], two[0:half, :]
        keep[:, columns] = dot_rows(rows, jnp.where(odd, one, two))
        give[:, columns] = dot_rows(rows, jnp.where(odd, two, one)).astype(jnp.bfloat16)


def whole(parts):
    return jnp.sum(parts.astype(jnp.float32), axis=0, keepdims=True)


def leave_kernel(early, early_came, squares, late, late_came, stay, leave):
    z, q = lax.axis_index("gallery"), lax.axis_index("query")
    row_count = late.shape[0]
    near = lax.div(q, 2) == lax.div(z, 2)
    early_sum = early[...] + early_came[0:row_count, :].astype(jnp.float32)
    late_sum = late[...] + late_came[...].astype(jnp.float32)
    row = squares[...] + whole(early_came[row_count:, :])
    stay[0:row_count, :] = jnp.where(near, early_sum, late_sum)
    stay[row_count:, :] = row
    leave[0:row_count, :] = jnp.where(near, late_sum, early_sum).astype(jnp.bfloat16)
    leave[row_count:, :] = three_parts(row)


def score_kernel(stay, came, scores):
    row_count = scores.shape[0]
    squares = stay[row_count : row_count + 1, :] + whole(came[row_count:, :])
    inverse = lax.rsqrt(squares / D + epsilon) / math.sqrt(D)
    shape = (row_count, row_count)
    same = lax.broadcasted_iota(jnp.int32, shape, 0) == lax.broadcasted_iota(jnp.int32, shape, 1)
    inverse = jnp.sum(jnp.where(same, inverse, 0.0), axis=1, keepdims=True)
    scores[...] = ((stay[0:row_count, :] + came[0:row_count, :].astype(jnp.float32)) * inverse).astype(jnp.bfloat16)


def line_of_four(shape, gallery, neighbour, weights, send_rows, queries):
    groups, shards, blocks = shape
    row_count, col_count = gallery.shape
    query_count = queries.shape[0]
    half = query_count // 2
    cap = send_rows.shape[1] // shards
    low, high = jnp.bfloat16, jnp.float32

    def place(device):
        return (device[0] * shards + device[1]) * blocks + device[2]

    def send(value, to):
        pairs = []
        for g in range(groups):
            for z in range(shards):
                for q in range(blocks):
                    pairs.append((place((g, z, q)), place(to(g, z, q))))
        return lax.ppermute(value, AXES, pairs)

    to_third, to_first, to_second = call(
        functools.partial(pack_kernel, cap),
        [array((half + cap, col_count), low), array((half + cap, col_count), low), array((cap, col_count), low)],
        *(pltpu.with_memory_space_constraint(item, pltpu.HBM) for item in (queries, gallery, send_rows)),
        specs=[pl.BlockSpec(memory_space=pltpu.HBM)] * 3,
        scratch=[
            pltpu.VMEM(gallery.shape, low),
            pltpu.VMEM(send_rows.shape, jnp.int32),
            pltpu.VMEM((shards * cap, col_count), low),
            pltpu.SemaphoreType.DMA((4,)),
        ],
    )
    third = send(to_third, lambda g, z, q: (g, z ^ 3, q))
    first = send(to_first, lambda g, z, q: (g, z ^ 1, q))
    second_rows = send(to_second, lambda g, z, q: (g, z ^ 2, q))

    passed, second_rows = lax.optimization_barrier((third[0:half], second_rows))
    third_other = send(passed, lambda g, z, q: (1 - g, z, q))
    second = send(passed, lambda g, z, q: (g, z ^ 1, q))
    second_other = send(passed, lambda g, z, q: (1 - g, z ^ 1, q))
    first_other = send(first[0:half], lambda g, z, q: (1 - g, z, q))

    refined, squares = call(
        functools.partial(refine_kernel, cap),
        [array((row_count, col_count), low), array((SPARE, row_count), high)],
        gallery,
        neighbour.T,
        weights.T,
        first,
        second_rows,
        third,
    )
    early, early_give = call(
        early_kernel,
        [array((row_count, query_count), high), array((row_count + SPARE, query_count), low)],
        refined,
        squares,
        queries,
        first,
        first_other,
    )
    early_came = send(early_give, lambda g, z, q: (g, z, q ^ 1))
    late, late_give = call(
        late_kernel,
        [array((row_count, query_count), high), array((row_count, query_count), low)],
        refined,
        third,
        third_other,
        second,
        second_other,
    )
    late_came = send(late_give, lambda g, z, q: (g, z, q ^ 1))
    stay, leave = call(
        leave_kernel,
        [array((row_count + SPARE, query_count), high), array((row_count + SPARE, query_count), low)],
        early,
        early_came,
        squares,
        late,
        late_came,
    )
    came = send(leave, lambda g, z, q: (g, z, q ^ 2))
    (scores,) = call(score_kernel, [jax.ShapeDtypeStruct((row_count, query_count), low)], stay, came)
    return (refined, scores)


def solution(mesh):
    shape = tuple(mesh.shape[name] for name in AXES)

    def per_device(*arrays):
        if shape == (2, 4, 4):
            return line_of_four(shape, *arrays)
        return generic(*arrays)

    return jax.shard_map(
        per_device,
        mesh=mesh,
        in_specs=(
            P(("groups", "gallery"), "query"),
            P(("groups", "gallery"), None),
            P(("groups", "gallery"), None),
            P(("groups", "gallery"), None),
            P("gallery", "query"),
        ),
        out_specs=(P(("groups", "gallery"), "query"), P(("groups", "gallery"), "query")),
        check_vma=False,
    )
```

time: 43.3 us -> 31.5 us (0.73)
  starting transfers between devices: 20.7 us -> 12.4 us
  Pallas kernels: 0 us -> 4.04 us
  local copies, waits for them, and re-layouts: 4.19 us -> 0.74 us
  matrix products: 2.14 us -> 0 us
  waiting for transfers between devices: 14.6 us -> 13.4 us
  other arithmetic: 0.55 us -> 0 us
    ppermute x14 -> x10, starting transfers between devices: 20.7 us -> 12.4 us  [send(): return lax.ppermute(value, AXES, pairs)]
    pallas_call x0 -> x6, Pallas kernels: none -> 4.04 us  [call(): pl.pallas_call(kernel, out_shape=list(outs), in_specs=specs or [VMEM] * l...]
    dot_general x5 -> x0, matrix products: 2.14 us -> none  [the longest x1 1.1 us: line_of_four(): lax.dot_general(matrix, table, (((1,), (0,)), ((), ())), preferred_elemen...]
    gather x3 -> x0, local copies, waits for them, and re-layouts: 1.77 us -> none  [line_of_four(): gallery[wanted]]
    ppermute x14 -> x10, waiting for transfers between devices: 14.6 us -> 13.4 us  [send(): return lax.ppermute(value, AXES, pairs)]
    dynamic_slice x1 -> x0, local copies, waits for them, and re-layouts: 0.96 us -> none  [line_of_four(): mine = lax.dynamic_slice_in_dim(queries, g * half_rows, half_rows)]
    unnamed x13 -> x9, local copies, waits for them, and re-layouts: 1.44 us -> 0.72 us
  transfers between devices with their start and end apart: 14 -> 10, of which waited for: 6 -> 8; matrix products, arithmetic and copies ran while one was open for 10% -> 2% of each run, Pallas kernels for 0% -> 6%
where the time goes in v2:
time: 31.5 us; the launch traced here: 31.3 us
  waiting for transfers between devices  13.4 us (43%)
  starting transfers between devices  12.4 us (39%)
  Pallas kernels  4.04 us (13%)
  local copies, waits for them, and re-layouts  0.74 us (2%)
  between operations  0.74 us (2%)
    ppermute x10, waiting for transfers between devices, send(): return lax.ppermute(value, AXES, pairs)  13.4 us
    ppermute x10, starting transfers between devices, send(): return lax.ppermute(value, AXES, pairs)  12.4 us
    pallas_call x6, Pallas kernels, call(): pl.pallas_call(kernel, out_shape=list(outs), in_specs=specs or [VMEM] * l...  4.04 us
    unnamed x9, local copies, waits for them, and re-layouts  0.72 us
  transfers between devices with their start and end apart: 10, of which 8 were waited for; matrix products, arithmetic and copies ran while one was open for 2% of the time, Pallas kernels for 6%

profile of v2, /device:TPU:0, one launch (start us, length us, event | category | flops | bytes accessed | tf_op | source)
XLA Modules:
  0.0 31.3 jit_solution(16582749031467486032)
XLA Ops:
  0.6 1.2 %shard_map.68 = (bf16[144,512]{1,0:T(8,128)(2,1)S(1)}, bf16[144,512]{1,0:T(8,128)(2,1)S(1)}, bf16[16,512]{1,0:T(8,128)(2,1)S(1)}) custom-call(bf16[256,512]{1,0:T(8,128)(2,1)} %queries.3, bf16[256,512]{1,0:T(8,128)(2,1)} %gallery.3, s32[1,64]{1,0:T(1,128)} %send_rows.1), custom_call_target="tpu_custom_call" | custom-call | bytes 835840 | tf_op jit(solution)/shard_map/pallas_call | solution.py:56
  1.8 3.1 %collective-permute-start = (bf16[144,512]{1,0:T(8,128)(2,1)S(1)}, bf16[144,512]{1,0:T(8,128)(2,1)S(1)}, u32[]{:S(2)}, u32[]{:S(2)}) collective-permute-start(bf16[144,512]{1,0:T(8,128)(2,1)S(1)} %get-tuple-element.15), channel_id=1, source_target_pairs={{0,4},{1,5},{2,6},{3,7},{4,0},{5,1},{6,2},{7,3},{8,12},{9,13},{10,... | collective-permute-start | bytes 442376 | tf_op jit(solution)/shard_map/ppermute | solution.py:222
  4.9 2.5 %collective-permute-start.1 = (bf16[144,512]{1,0:T(8,128)(2,1)S(1)}, bf16[144,512]{1,0:T(8,128)(2,1)S(1)}, u32[]{:S(2)}, u32[]{:S(2)}) collective-permute-start(bf16[144,512]{1,0:T(8,128)(2,1)S(1)} %get-tuple-element.16), channel_id=1, source_target_pairs={{0,12},{1,13},{2,14},{3,15},{4,8},{5,9},{6,10},{7,11},{8,4},{9,5},... | collective-permute-start | bytes 442376 | tf_op jit(solution)/shard_map/ppermute | solution.py:222
  7.4 0.0 copy-start.1
  7.4 0.1 collective-permute-start.2
  7.5 1.5 %collective-permute-done.first = bf16[144,512]{1,0:T(8,128)(2,1)S(1)} collective-permute-done((bf16[144,512]{1,0:T(8,128)(2,1)S(1)}, bf16[144,512]{1,0:T(8,128)(2,1)S(1)}, u32[]{:S(2)}, u32[]{:S(2)}) %collective-permute-start) | collective-permute-done | bytes 147488 | tf_op jit(solution)/shard_map/ppermute | solution.py:222
  9.0 0.0 copy-start.2
  9.0 0.0 copy-start.3
  9.0 1.6 %collective-permute-start.3 = (bf16[128,512]{1,0:T(8,128)(2,1)S(1)}, bf16[128,512]{1,0:T(8,128)(2,1)S(1)}, u32[]{:S(2)}, u32[]{:S(2)}) collective-permute-start(bf16[128,512]{1,0:T(8,128)(2,1)S(1)} %slice.9), channel_id=1, source_target_pairs={{0,16},{1,17},{2,18},{3,19},{4,20},{5,21},{6,22},{7,23},{8,24},{9,... | collective-permute-start | bytes 393224 | tf_op jit(solution)/shard_map/ppermute | solution.py:222
  10.6 3.8 %collective-permute-done.1.third = bf16[144,512]{1,0:T(8,128)(2,1)S(1)} collective-permute-done((bf16[144,512]{1,0:T(8,128)(2,1)S(1)}, bf16[144,512]{1,0:T(8,128)(2,1)S(1)}, u32[]{:S(2)}, u32[]{:S(2)}) %collective-permute-start.1) | collective-permute-done | bytes 147488 | tf_op jit(solution)/shard_map/ppermute | solution.py:222
  14.4 0.5 %collective-permute-done.2.second = bf16[16,512]{1,0:T(8,128)(2,1)S(1)} collective-permute-done((bf16[16,512]{1,0:T(8,128)(2,1)S(1)}, bf16[16,512]{1,0:T(8,128)(2,1)S(1)}, u32[]{:S(2)}, u32[]{:S(2)}) %collective-permute-start.2) | collective-permute-done | bytes 16416 | tf_op jit(solution)/shard_map/ppermute | solution.py:222
  14.9 1.5 %collective-permute-start.5 = (bf16[128,512]{1,0:T(8,128)(2,1)S(1)}, bf16[128,512]{1,0:T(8,128)(2,1)S(1)}, u32[]{:S(2)}, u32[]{:S(2)}) collective-permute-start(bf16[128,512]{1,0:T(8,128)(2,1)S(1)} %slice.8), channel_id=1, source_target_pairs={{0,16},{1,17},{2,18},{3,19},{4,20},{5,21},{6,22},{7,23},{8,24},{9,... | collective-permute-start | bytes 393224 | tf_op jit(solution)/shard_map/ppermute | solution.py:222
  16.5 0.5 %collective-permute-start.6 = (bf16[128,512]{1,0:T(8,128)(2,1)S(1)}, bf16[128,512]{1,0:T(8,128)(2,1)S(1)}, u32[]{:S(2)}, u32[]{:S(2)}) collective-permute-start(bf16[128,512]{1,0:T(8,128)(2,1)S(1)} %slice.8), channel_id=1, source_target_pairs={{0,4},{1,5},{2,6},{3,7},{4,0},{5,1},{6,2},{7,3},{8,12},{9,13},{10,... | collective-permute-start | bytes 393224 | tf_op jit(solution)/shard_map/ppermute | solution.py:222
  16.9 1.5 %collective-permute-start.7 = (bf16[128,512]{1,0:T(8,128)(2,1)S(1)}, bf16[128,512]{1,0:T(8,128)(2,1)S(1)}, u32[]{:S(2)}, u32[]{:S(2)}) collective-permute-start(bf16[128,512]{1,0:T(8,128)(2,1)S(1)} %slice.8), channel_id=1, source_target_pairs={{0,20},{1,21},{2,22},{3,23},{4,16},{5,17},{6,18},{7,19},{8,28},{9,... | collective-permute-start | bytes 393224 | tf_op jit(solution)/shard_map/ppermute | solution.py:222
  18.4 0.0 copy-done.1
  18.4 0.0 copy-done.2
  18.4 0.0 copy-done.3
  18.4 0.0 copy-start
  18.4 1.1 %shard_map.69 = (bf16[256,512]{1,0:T(8,128)(2,1)S(1)}, f32[16,256]{1,0:T(8,128)S(1)}) custom-call(bf16[256,512]{1,0:T(8,128)(2,1)S(1)} %copy-done.1, s32[10,256]{1,0:T(8,128)S(1)} %bitcast.2, s32[10,256]{1,0:T(8,128)S(1)} %bitcast.3, bf16[144,512]{1,0:T(8,128)(2,1)S(1)} %collective-permute-done.first, bf16[16,512]{1,0:T(8,128)(2,1)S(1)} %collective-permute-done.2.second, ...), custom_call_target="tpu_custom_call" | custom-call | bytes 872448 | tf_op jit(solution)/shard_map/pallas_call | solution.py:56
  19.5 0.0 collective-permute-done.3.first_other
  19.5 0.0 copy-done
  19.6 0.4 %shard_map.70 = (f32[256,256]{1,0:T(8,128)S(1)}, bf16[272,256]{1,0:T(8,128)(2,1)S(1)}) custom-call(bf16[256,512]{1,0:T(8,128)(2,1)S(1)} %get-tuple-element.28.refined, f32[16,256]{1,0:T(8,128)S(1)} %get-tuple-element.20.squares, bf16[256,512]{1,0:T(8,128)(2,1)S(1)} %copy-done, bf16[144,512]{1,0:T(8,128)(2,1)S(1)} %collective-permute-done.first, ...), custom_call_target="tpu_custom_call" | custom-call | bytes 1220608 | tf_op jit(solution)/shard_map/pallas_call | solution.py:56
  20.0 0.1 collective-permute-start.4
  20.1 1.1 %collective-permute-done.5.third_other = bf16[128,512]{1,0:T(8,128)(2,1)S(1)} collective-permute-done((bf16[128,512]{1,0:T(8,128)(2,1)S(1)}, bf16[128,512]{1,0:T(8,128)(2,1)S(1)}, u32[]{:S(2)}, u32[]{:S(2)}) %collective-permute-start.5) | collective-permute-done | bytes 131104 | tf_op jit(solution)/shard_map/ppermute | solution.py:222
  21.2 0.3 collective-permute-done.6.second
  21.4 1.4 %collective-permute-done.7.second_other = bf16[128,512]{1,0:T(8,128)(2,1)S(1)} collective-permute-done((bf16[128,512]{1,0:T(8,128)(2,1)S(1)}, bf16[128,512]{1,0:T(8,128)(2,1)S(1)}, u32[]{:S(2)}, u32[]{:S(2)}) %collective-permute-start.7) | collective-permute-done | bytes 131104 | tf_op jit(solution)/shard_map/ppermute | solution.py:222
  22.8 0.4 %shard_map.71 = (f32[256,256]{1,0:T(8,128)S(1)}, bf16[256,256]{1,0:T(8,128)(2,1)S(1)}) custom-call(bf16[256,512]{1,0:T(8,128)(2,1)S(1)} %get-tuple-element.28.refined, bf16[144,512]{1,0:T(8,128)(2,1)S(1)} %collective-permute-done.1.third, bf16[128,512]{1,0:T(8,128)(2,1)S(1)} %collective-permute-done.5.third_other, ...), custom_call_target="tpu_custom_call" | custom-call | bytes 1196032 | tf_op jit(solution)/shard_map/pallas_call | solution.py:56
  23.3 0.1 collective-permute-start.8
  23.3 1.3 %collective-permute-done.8.late_came = bf16[256,256]{1,0:T(8,128)(2,1)S(1)} collective-permute-done((bf16[256,256]{1,0:T(8,128)(2,1)S(1)}, bf16[256,256]{1,0:T(8,128)(2,1)S(1)}, u32[]{:S(2)}, u32[]{:S(2)}) %collective-permute-start.8) | collective-permute-done | bytes 131104 | tf_op jit(solution)/shard_map/ppermute | solution.py:222
  24.7 0.0 collective-permute-done.4.early_came
  24.7 0.1 shard_map.72
  24.8 1.6 %collective-permute-start.9 = (bf16[272,256]{1,0:T(8,128)(2,1)S(1)}, bf16[272,256]{1,0:T(8,128)(2,1)S(1)}, u32[]{:S(2)}, u32[]{:S(2)}) collective-permute-start(bf16[272,256]{1,0:T(8,128)(2,1)S(1)} %get-tuple-element.27), channel_id=1, source_target_pairs={{0,2},{1,3},{2,0},{3,1},{4,6},{5,7},{6,4},{7,5},{8,10},{9,11},{10,... | collective-permute-start | bytes 417800 | tf_op jit(solution)/shard_map/ppermute | solution.py:222
  26.3 0.7 %copy.7 = bf16[256,512]{1,0:T(8,128)(2,1)} copy(bf16[256,512]{1,0:T(8,128)(2,1)S(1)} %get-tuple-element.28.refined) | data formatting | bytes 524288
  27.0 3.5 %collective-permute-done.9.came = bf16[272,256]{1,0:T(8,128)(2,1)S(1)} collective-permute-done((bf16[272,256]{1,0:T(8,128)(2,1)S(1)}, bf16[272,256]{1,0:T(8,128)(2,1)S(1)}, u32[]{:S(2)}, u32[]{:S(2)}) %collective-permute-start.9) | collective-permute-done | bytes 139296 | tf_op jit(solution)/shard_map/ppermute | solution.py:222
  30.5 0.8 %shard_map.73 = bf16[256,256]{1,0:T(8,128)(2,1)} custom-call(f32[272,256]{1,0:T(8,128)S(1)} %get-tuple-element.26.stay, bf16[272,256]{1,0:T(8,128)(2,1)S(1)} %collective-permute-done.9.came), custom_call_target="tpu_custom_call" | custom-call | bytes 548864 | tf_op jit(solution)/shard_map/pallas_call | solution.py:56
  (2 shorter events, 0.0 us)
Async XLA Ops:
  1.8 7.1 %collective-permute-start = (bf16[144,512]{1,0:T(8,128)(2,1)S(1)}, bf16[144,512]{1,0:T(8,128)(2,1)S(1)}, u32[]{:S(2)}, u32[]{:S(2)}) collective-permute-start(bf16[144,512]{1,0:T(8,128)(2,1)S(1)} %get-tuple-element.15), channel_id=1, source_target_pairs={{0,4},{1,5},{2,6},{3,7},{4,0},{5,1},{6,2},{7,3},{8,12},{9,13},{10,... | collective-permute-start | bytes 442376 | tf_op jit(solution)/shard_map/ppermute | solution.py:222
  4.9 9.5 %collective-permute-start.1 = (bf16[144,512]{1,0:T(8,128)(2,1)S(1)}, bf16[144,512]{1,0:T(8,128)(2,1)S(1)}, u32[]{:S(2)}, u32[]{:S(2)}) collective-permute-start(bf16[144,512]{1,0:T(8,128)(2,1)S(1)} %get-tuple-element.16), channel_id=1, source_target_pairs={{0,12},{1,13},{2,14},{3,15},{4,8},{5,9},{6,10},{7,11},{8,4},{9,5},... | collective-permute-start | bytes 442376 | tf_op jit(solution)/shard_map/ppermute | solution.py:222
  7.4 11.0 %copy-start.1 = (bf16[256,512]{1,0:T(8,128)(2,1)S(1)}, bf16[256,512]{1,0:T(8,128)(2,1)}, u32[]{:S(2)}) copy-start(bf16[256,512]{1,0:T(8,128)(2,1)} %gallery.3) | copy-start | bytes 786436
  7.4 7.5 %collective-permute-start.2 = (bf16[16,512]{1,0:T(8,128)(2,1)S(1)}, bf16[16,512]{1,0:T(8,128)(2,1)S(1)}, u32[]{:S(2)}, u32[]{:S(2)}) collective-permute-start(bf16[16,512]{1,0:T(8,128)(2,1)S(1)} %get-tuple-element.17), channel_id=1, source_target_pairs={{0,8},{1,9},{2,10},{3,11},{4,12},{5,13},{6,14},{7,15},{8,0},{9,1},... | collective-permute-start | bytes 49160 | tf_op jit(solution)/shard_map/ppermute | solution.py:222
  9.0 9.4 %copy-start.2 = (s32[256,10]{0,1:T(8,128)S(1)}, s32[256,10]{0,1:T(8,128)}, u32[]{:S(2)}) copy-start(s32[256,10]{0,1:T(8,128)} %param.6) | copy-start | bytes 30724
  9.0 9.4 %copy-start.3 = (s32[256,10]{0,1:T(8,128)S(1)}, s32[256,10]{0,1:T(8,128)}, u32[]{:S(2)}) copy-start(s32[256,10]{0,1:T(8,128)} %param.7) | copy-start | bytes 30724
  9.0 10.5 %collective-permute-start.3 = (bf16[128,512]{1,0:T(8,128)(2,1)S(1)}, bf16[128,512]{1,0:T(8,128)(2,1)S(1)}, u32[]{:S(2)}, u32[]{:S(2)}) collective-permute-start(bf16[128,512]{1,0:T(8,128)(2,1)S(1)} %slice.9), channel_id=1, source_target_pairs={{0,16},{1,17},{2,18},{3,19},{4,20},{5,21},{6,22},{7,23},{8,24},{9,... | collective-permute-start | bytes 393224 | tf_op jit(solution)/shard_map/ppermute | solution.py:222
  14.9 6.2 %collective-permute-start.5 = (bf16[128,512]{1,0:T(8,128)(2,1)S(1)}, bf16[128,512]{1,0:T(8,128)(2,1)S(1)}, u32[]{:S(2)}, u32[]{:S(2)}) collective-permute-start(bf16[128,512]{1,0:T(8,128)(2,1)S(1)} %slice.8), channel_id=1, source_target_pairs={{0,16},{1,17},{2,18},{3,19},{4,20},{5,21},{6,22},{7,23},{8,24},{9,... | collective-permute-start | bytes 393224 | tf_op jit(solution)/shard_map/ppermute | solution.py:222
  16.5 5.0 %collective-permute-start.6 = (bf16[128,512]{1,0:T(8,128)(2,1)S(1)}, bf16[128,512]{1,0:T(8,128)(2,1)S(1)}, u32[]{:S(2)}, u32[]{:S(2)}) collective-permute-start(bf16[128,512]{1,0:T(8,128)(2,1)S(1)} %slice.8), channel_id=1, source_target_pairs={{0,4},{1,5},{2,6},{3,7},{4,0},{5,1},{6,2},{7,3},{8,12},{9,13},{10,... | collective-permute-start | bytes 393224 | tf_op jit(solution)/shard_map/ppermute | solution.py:222
  16.9 5.9 %collective-permute-start.7 = (bf16[128,512]{1,0:T(8,128)(2,1)S(1)}, bf16[128,512]{1,0:T(8,128)(2,1)S(1)}, u32[]{:S(2)}, u32[]{:S(2)}) collective-permute-start(bf16[128,512]{1,0:T(8,128)(2,1)S(1)} %slice.8), channel_id=1, source_target_pairs={{0,20},{1,21},{2,22},{3,23},{4,16},{5,17},{6,18},{7,19},{8,28},{9,... | collective-permute-start | bytes 393224 | tf_op jit(solution)/shard_map/ppermute | solution.py:222
  18.4 1.1 %copy-start = (bf16[256,512]{1,0:T(8,128)(2,1)S(1)}, bf16[256,512]{1,0:T(8,128)(2,1)}, u32[]{:S(2)}) copy-start(bf16[256,512]{1,0:T(8,128)(2,1)} %queries.3) | copy-start | bytes 786436
  20.0 4.7 %collective-permute-start.4 = (bf16[272,256]{1,0:T(8,128)(2,1)S(1)}, bf16[272,256]{1,0:T(8,128)(2,1)S(1)}, u32[]{:S(2)}, u32[]{:S(2)}) collective-permute-start(bf16[272,256]{1,0:T(8,128)(2,1)S(1)} %get-tuple-element.22), channel_id=1, source_target_pairs={{0,1},{1,0},{2,3},{3,2},{4,5},{5,4},{6,7},{7,6},{8,9},{9,8},{10,11... | collective-permute-start | bytes 417800 | tf_op jit(solution)/shard_map/ppermute | solution.py:222
  23.3 1.4 %collective-permute-start.8 = (bf16[256,256]{1,0:T(8,128)(2,1)S(1)}, bf16[256,256]{1,0:T(8,128)(2,1)S(1)}, u32[]{:S(2)}, u32[]{:S(2)}) collective-permute-start(bf16[256,256]{1,0:T(8,128)(2,1)S(1)} %get-tuple-element.25), channel_id=1, source_target_pairs={{0,1},{1,0},{2,3},{3,2},{4,5},{5,4},{6,7},{7,6},{8,9},{9,8},{10,11... | collective-permute-start | bytes 393224 | tf_op jit(solution)/shard_map/ppermute | solution.py:222
  24.8 5.8 %collective-permute-start.9 = (bf16[272,256]{1,0:T(8,128)(2,1)S(1)}, bf16[272,256]{1,0:T(8,128)(2,1)S(1)}, u32[]{:S(2)}, u32[]{:S(2)}) collective-permute-start(bf16[272,256]{1,0:T(8,128)(2,1)S(1)} %get-tuple-element.27), channel_id=1, source_target_pairs={{0,2},{1,3},{2,0},{3,1},{4,6},{5,7},{6,4},{7,5},{8,10},{9,11},{10,... | collective-permute-start | bytes 417800 | tf_op jit(solution)/shard_map/ppermute | solution.py:222

commit v3 on v2

--- a/solution.py
+++ b/solution.py
@@ -111,9 +111,9 @@
     copies[3].wait()
 
 
-def refine_kernel(cap, gallery, neighbour, weights, first, second, third, refined, squares):
+def near_kernel(cap, gallery, neighbour, weights, summed, denominator, far_matrix):
     z = lax.axis_index("gallery")
-    row_count, col_count = gallery.shape
+    row_count = gallery.shape[0]
     index = neighbour[...]
     weight = weights[...].astype(jnp.float32)
     slot = jnp.maximum(index - row_count, 0)
@@ -131,15 +131,20 @@
         return jnp.where(places_of == lax.broadcasted_iota(jnp.int32, places_of.shape, 1), self_weight, 0.0)
 
     near_matrix = matrix(index, row_count, own)
-    far_matrix = matrix(far, 3 * cap, lambda places_of: jnp.zeros(places_of.shape, jnp.float32))
+    far_matrix[...] = matrix(far, 3 * cap, lambda places_of: jnp.zeros(places_of.shape, jnp.float32))
+    summed[...] = dot_columns(near_matrix, gallery[...])
+    denominator[...] = dot_columns(near_matrix, jnp.ones((row_count, 128), jnp.bfloat16)) + dot_columns(
+        far_matrix[...], jnp.ones((3 * cap, 128), jnp.bfloat16)
+    )
+
+
+def refine_kernel(cap, summed, denominator, far_matrix, first, second, third, refined, squares):
+    row_count, col_count = summed.shape
     half = first.shape[0] - cap
     table = jnp.concatenate([first[half:, :], second[...], third[half:, :]], axis=0)
-    summed = dot_columns(near_matrix, gallery[...]) + dot_columns(far_matrix, table)
-    denominator = dot_columns(near_matrix, jnp.ones((row_count, 128), jnp.bfloat16)) + dot_columns(
-        far_matrix, jnp.ones((3 * cap, 128), jnp.bfloat16)
-    )
+    total = summed[...] + dot_columns(far_matrix[...], table)
     for start in range(0, col_count, 128):
-        refined[:, start : start + 128] = (summed[:, start : start + 128] / denominator).astype(jnp.bfloat16)
+        refined[:, start : start + 128] = (total[:, start : start + 128] / denominator[...]).astype(jnp.bfloat16)
     floats = refined[...].astype(jnp.float32)
     floats = floats * floats
     high = floats.astype(jnp.bfloat16)
@@ -150,7 +155,7 @@
 
 def early_kernel(refined, squares, queries, first, first_other, keep, give):
     g, z, q = (lax.axis_index(name) for name in AXES)
-    half = first_other.shape[0]
+    half = queries.shape[0] // 2
     row_count = refined.shape[0]
     odd = lax.rem(q + z, 2) == 1
     rows = refined[...]
@@ -163,43 +168,59 @@
     give[row_count:, :] = three_parts(squares[...])
 
 
-def late_kernel(refined, third, third_other, second, second_other, keep, give):
-    g, z, q = (lax.axis_index(name) for name in AXES)
-    half = third_other.shape[0]
+def late_kernel(refined, refined_pair, own_odd, own_even, pair_odd, pair_even, partial):
+    z, q = lax.axis_index("gallery"), lax.axis_index("query")
+    half = partial.shape[1]
     odd = lax.rem(q + z, 2) == 1
-    rows = refined[...]
-    for place, one, two in ((g, third, second), (1 - g, third_other, second_other)):
-        columns = pl.ds(pl.multiple_of(place * half, half), half)
-        one, two = one[0:half, :], two[0:half, :]
-        keep[:, columns] = dot_rows(rows, jnp.where(odd, one, two))
-        give[:, columns] = dot_rows(rows, jnp.where(odd, two, one)).astype(jnp.bfloat16)
+    own = jnp.where(odd, own_odd[0:half, :], own_even[0:half, :])
+    pair = jnp.where(odd, pair_odd[0:half, :], pair_even[0:half, :])
+    partial[...] = dot_rows(refined[...], own) + dot_rows(refined_pair[...], pair)
 
 
 def whole(parts):
     return jnp.sum(parts.astype(jnp.float32), axis=0, keepdims=True)
 
 
-def leave_kernel(early, early_came, squares, late, late_came, stay, leave):
-    z, q = lax.axis_index("gallery"), lax.axis_index("query")
-    row_count = late.shape[0]
-    near = lax.div(q, 2) == lax.div(z, 2)
-    early_sum = early[...] + early_came[0:row_count, :].astype(jnp.float32)
-    late_sum = late[...] + late_came[...].astype(jnp.float32)
+def first_half():
+    g, z, q = (lax.axis_index(name) for name in AXES)
+    odd = lax.rem(q + z, 2) == 1
+    return jnp.where(odd, 1 - g, g), lax.div(q, 2) == lax.div(z, 2)
+
+
+def leave_most_kernel(early, early_came, squares, late, early_sum, stay, chip_squares, leave):
+    row_count, half = late.shape
+    place, near = first_half()
+    early_sum[...] = early[...] + early_came[0:row_count, :].astype(jnp.float32)
+    near_part = early_sum[:, pl.ds(pl.multiple_of(place * half, half), half)]
     row = squares[...] + whole(early_came[row_count:, :])
-    stay[0:row_count, :] = jnp.where(near, early_sum, late_sum)
-    stay[row_count:, :] = row
-    leave[0:row_count, :] = jnp.where(near, late_sum, early_sum).astype(jnp.bfloat16)
-    leave[row_count:, :] = three_parts(row)
-
-
-def score_kernel(stay, came, scores):
-    row_count = scores.shape[0]
-    squares = stay[row_count : row_count + 1, :] + whole(came[row_count:, :])
+    parts = three_parts(row)
+    chip_squares[...] = row
+    stay[...] = jnp.where(near, near_part, late[...])
+    leave[0:row_count, :] = jnp.where(near, late[...], near_part).astype(jnp.bfloat16)
+    leave[row_count : row_count + SPARE, :] = parts[:, 0:half]
+    leave[row_count + SPARE :, :] = parts[:, half:]
+
+
+def leave_last_kernel(early_sum, late, stay, leave):
+    half = late.shape[1]
+    place, near = first_half()
+    near_part = early_sum[:, pl.ds(pl.multiple_of((1 - place) * half, half), half)]
+    stay[...] = jnp.where(near, near_part, late[...])
+    leave[...] = jnp.where(near, late[...], near_part).astype(jnp.bfloat16)
+
+
+def score_kernel(stay_most, chip_squares, came_most, stay_last, came_last, scores):
+    row_count, half = stay_most.shape
+    place, _ = first_half()
+    there = (whole(came_most[row_count : row_count + SPARE, :]), whole(came_most[row_count + SPARE :, :]))
+    squares = chip_squares[0:1, :] + jnp.concatenate(there, axis=1)
     inverse = lax.rsqrt(squares / D + epsilon) / math.sqrt(D)
     shape = (row_count, row_count)
     same = lax.broadcasted_iota(jnp.int32, shape, 0) == lax.broadcasted_iota(jnp.int32, shape, 1)
     inverse = jnp.sum(jnp.where(same, inverse, 0.0), axis=1, keepdims=True)
-    scores[...] = ((stay[0:row_count, :] + came[0:row_count, :].astype(jnp.float32)) * inverse).astype(jnp.bfloat16)
+    for where, stay, came in ((place, stay_most, came_most), (1 - place, stay_last, came_last)):
+        raw = stay[...] + came[0:row_count, :].astype(jnp.float32)
+        scores[:, pl.ds(pl.multiple_of(where * half, half), half)] = (raw * inverse).astype(jnp.bfloat16)
 
 
 def line_of_four(shape, gallery, neighbour, weights, send_rows, queries):
@@ -213,13 +234,17 @@
     def place(device):
         return (device[0] * shards + device[1]) * blocks + device[2]
 
-    def send(value, to):
+    def send(value, to, only=lambda g, z, q: True):
         pairs = []
         for g in range(groups):
             for z in range(shards):
                 for q in range(blocks):
-                    pairs.append((place((g, z, q)), place(to(g, z, q))))
+                    if only(g, z, q):
+                        pairs.append((place((g, z, q)), place(to(g, z, q))))
         return lax.ppermute(value, AXES, pairs)
+
+    def is_odd(z, q):
+        return (q + z) % 2 == 1
 
     to_third, to_first, to_second = call(
         functools.partial(pack_kernel, cap),
@@ -237,22 +262,35 @@
     first = send(to_first, lambda g, z, q: (g, z ^ 1, q))
     second_rows = send(to_second, lambda g, z, q: (g, z ^ 2, q))
 
-    passed, second_rows = lax.optimization_barrier((third[0:half], second_rows))
-    third_other = send(passed, lambda g, z, q: (1 - g, z, q))
-    second = send(passed, lambda g, z, q: (g, z ^ 1, q))
-    second_other = send(passed, lambda g, z, q: (1 - g, z ^ 1, q))
-    first_other = send(first[0:half], lambda g, z, q: (1 - g, z, q))
+    first_other = send(first, lambda g, z, q: (1 - g, z, q))
+    summed, denominator, far_matrix = call(
+        functools.partial(near_kernel, cap),
+        [
+            array((row_count, col_count), high),
+            array((row_count, 128), high),
+            array(((shards - 1) * cap, row_count), low),
+        ],
+        gallery,
+        neighbour.T,
+        weights.T,
+    )
+    passed, second_rows, summed = lax.optimization_barrier((third, second_rows, summed))
+    a = send(passed, lambda g, z, q: (1 - g, z, q) if is_odd(z, q) else (g, z ^ 1, q ^ 1))
+    b = send(passed, lambda g, z, q: (g, z ^ 1, q) if is_odd(z, q) else (1 - g, z, q ^ 1))
+    c = send(passed, lambda g, z, q: (1 - g, z ^ 1, q) if is_odd(z, q) else (g, z, q ^ 1))
+    d = send(passed, lambda g, z, q: (1 - g, z, q) if is_odd(z, q) else (1 - g, z ^ 1, q ^ 1))
 
     refined, squares = call(
         functools.partial(refine_kernel, cap),
         [array((row_count, col_count), low), array((SPARE, row_count), high)],
-        gallery,
-        neighbour.T,
-        weights.T,
+        summed,
+        denominator,
+        far_matrix,
         first,
         second_rows,
         third,
     )
+    refined_pair = send(refined, lambda g, z, q: (g, z, q ^ 1))
     early, early_give = call(
         early_kernel,
         [array((row_count, query_count), high), array((row_count + SPARE, query_count), low)],
@@ -263,27 +301,38 @@
         first_other,
     )
     early_came = send(early_give, lambda g, z, q: (g, z, q ^ 1))
-    late, late_give = call(
-        late_kernel,
-        [array((row_count, query_count), high), array((row_count, query_count), low)],
-        refined,
-        third,
-        third_other,
-        second,
-        second_other,
-    )
-    late_came = send(late_give, lambda g, z, q: (g, z, q ^ 1))
-    stay, leave = call(
-        leave_kernel,
-        [array((row_count + SPARE, query_count), high), array((row_count + SPARE, query_count), low)],
+
+    (late_most,) = call(late_kernel, [array((row_count, half), high)], refined, refined_pair, a, b, b, a)
+    early_sum, stay_most, chip_squares, leave = call(
+        leave_most_kernel,
+        [
+            array((row_count, query_count), high),
+            array((row_count, half), high),
+            array((SPARE, row_count), high),
+            array((row_count + 2 * SPARE, half), low),
+        ],
         early,
         early_came,
         squares,
-        late,
-        late_came,
-    )
-    came = send(leave, lambda g, z, q: (g, z, q ^ 2))
-    (scores,) = call(score_kernel, [jax.ShapeDtypeStruct((row_count, query_count), low)], stay, came)
+        late_most,
+    )
+    came_most = send(leave, lambda g, z, q: (g, z, q ^ 2))
+
+    c, d, _ = lax.optimization_barrier((c, d, leave))
+    (late_last,) = call(late_kernel, [array((row_count, half), high)], refined, refined_pair, third, c, c, d)
+    stay_last, leave = call(
+        leave_last_kernel, [array((row_count, half), high), array((row_count, half), low)], early_sum, late_last
+    )
+    came_last = send(leave, lambda g, z, q: (g, z, q ^ 2))
+    (scores,) = call(
+        score_kernel,
+        [jax.ShapeDtypeStruct((row_count, query_count), low)],
+        stay_most,
+        chip_squares,
+        came_most,
+        stay_last,
+        came_last,
+    )
     return (refined, scores)
 
 

time: 31.5 us -> 31.1 us (0.987)
  waiting for transfers between devices: 13.4 us -> 11 us
  starting transfers between devices: 12.4 us -> 14.1 us
    ppermute x10 -> x12, waiting for transfers between devices: 13.4 us -> 11 us  [send(): return lax.ppermute(value, AXES, pairs)]
    ppermute x10 -> x12, starting transfers between devices: 12.4 us -> 14.1 us  [send(): return lax.ppermute(value, AXES, pairs)]
    pallas_call x6 -> x9, Pallas kernels: 4.04 us -> 4.24 us  [call(): pl.pallas_call(kernel, out_shape=list(outs), in_specs=specs or [VMEM] * l...]
  transfers between devices with their start and end apart: 10 -> 12, of which waited for: 8 -> 6; matrix products, arithmetic and copies ran while one was open for 2% -> 2% of each run, Pallas kernels for 6% -> 7%
where the time goes in v3:
time: 31.1 us; the launch traced here: 30.8 us
  starting transfers between devices  14.1 us (45%)
  waiting for transfers between devices  11 us (35%)
  Pallas kernels  4.24 us (14%)
  between operations  0.73 us (2%)
  local copies, waits for them, and re-layouts  0.72 us (2%)
    ppermute x12, starting transfers between devices, send(): return lax.ppermute(value, AXES, pairs)  14.1 us
    ppermute x12, waiting for transfers between devices, send(): return lax.ppermute(value, AXES, pairs)  11 us
    pallas_call x9, Pallas kernels, call(): pl.pallas_call(kernel, out_shape=list(outs), in_specs=specs or [VMEM] * l...  4.24 us
    unnamed x9, local copies, waits for them, and re-layouts  0.72 us
  transfers between devices with their start and end apart: 12, of which 6 were waited for; matrix products, arithmetic and copies ran while one was open for 2% of the time, Pallas kernels for 7%

profile of v3, /device:TPU:0, one launch (start us, length us, event | category | flops | bytes accessed | tf_op | source)
XLA Modules:
  0.0 30.8 jit_solution(17107878870038343042)
XLA Ops:
  0.6 0.0 copy-start.1
  0.6 0.0 copy-start.2
  0.7 0.0 copy-start.3
  0.7 1.2 %shard_map.68 = (bf16[144,512]{1,0:T(8,128)(2,1)S(1)}, bf16[144,512]{1,0:T(8,128)(2,1)S(1)}, bf16[16,512]{1,0:T(8,128)(2,1)S(1)}) custom-call(bf16[256,512]{1,0:T(8,128)(2,1)} %queries.3, bf16[256,512]{1,0:T(8,128)(2,1)} %gallery.3, s32[1,64]{1,0:T(1,128)} %send_rows.1), custom_call_target="tpu_custom_call" | custom-call | bytes 835840 | tf_op jit(solution)/shard_map/pallas_call | solution.py:56
  1.9 3.1 %collective-permute-start.2 = (bf16[144,512]{1,0:T(8,128)(2,1)S(1)}, bf16[144,512]{1,0:T(8,128)(2,1)S(1)}, u32[]{:S(2)}, u32[]{:S(2)}) collective-permute-start(bf16[144,512]{1,0:T(8,128)(2,1)S(1)} %get-tuple-element.29), channel_id=1, source_target_pairs={{0,4},{1,5},{2,6},{3,7},{4,0},{5,1},{6,2},{7,3},{8,12},{9,13},{10,... | collective-permute-start | bytes 442376 | tf_op jit(solution)/shard_map/ppermute | solution.py:244
  5.0 2.5 %collective-permute-start = (bf16[144,512]{1,0:T(8,128)(2,1)S(1)}, bf16[144,512]{1,0:T(8,128)(2,1)S(1)}, u32[]{:S(2)}, u32[]{:S(2)}) collective-permute-start(bf16[144,512]{1,0:T(8,128)(2,1)S(1)} %get-tuple-element.23), channel_id=1, source_target_pairs={{0,12},{1,13},{2,14},{3,15},{4,8},{5,9},{6,10},{7,11},{8,4},{9,5},... | collective-permute-start | bytes 442376 | tf_op jit(solution)/shard_map/ppermute | solution.py:244
  7.5 0.1 collective-permute-start.1
  7.6 0.0 copy-done.1
  7.6 0.0 copy-done.2
  7.6 0.0 copy-done.3
  7.6 0.6 %shard_map.69 = (f32[256,512]{1,0:T(8,128)S(1)}, f32[256,128]{1,0:T(8,128)S(1)}, bf16[48,256]{1,0:T(8,128)(2,1)S(1)}) custom-call(bf16[256,512]{1,0:T(8,128)(2,1)S(1)} %copy-done.1, s32[10,256]{1,0:T(8,128)S(1)} %bitcast.2, s32[10,256]{1,0:T(8,128)S(1)} %bitcast.3), custom_call_target="tpu_custom_call" | custom-call | bytes 962560 | tf_op jit(solution)/shard_map/pallas_call | solution.py:56
  8.2 0.9 %collective-permute-done.2.first = bf16[144,512]{1,0:T(8,128)(2,1)S(1)} collective-permute-done((bf16[144,512]{1,0:T(8,128)(2,1)S(1)}, bf16[144,512]{1,0:T(8,128)(2,1)S(1)}, u32[]{:S(2)}, u32[]{:S(2)}) %collective-permute-start.2) | collective-permute-done | bytes 147488 | tf_op jit(solution)/shard_map/ppermute | solution.py:244
  9.1 1.5 %collective-permute-start.3 = (bf16[144,512]{1,0:T(8,128)(2,1)S(1)}, bf16[144,512]{1,0:T(8,128)(2,1)S(1)}, u32[]{:S(2)}, u32[]{:S(2)}) collective-permute-start(bf16[144,512]{1,0:T(8,128)(2,1)S(1)} %collective-permute-done.2.first), channel_id=1, source_target_pairs={{0,16},{1,17},{2,18},{3,19},{4,20},{5,21},{6,22},{7,23},{8,24},{9,... | collective-permute-start | bytes 442376 | tf_op jit(solution)/shard_map/ppermute | solution.py:244
  10.6 4.4 %collective-permute-done.1.second = bf16[16,512]{1,0:T(8,128)(2,1)S(1)} collective-permute-done((bf16[16,512]{1,0:T(8,128)(2,1)S(1)}, bf16[16,512]{1,0:T(8,128)(2,1)S(1)}, u32[]{:S(2)}, u32[]{:S(2)}) %collective-permute-start.1) | collective-permute-done | bytes 16416 | tf_op jit(solution)/shard_map/ppermute | solution.py:244
  15.0 0.0 collective-permute-done.third.own_odd
  15.0 0.0 collective-permute-start.6
  15.0 0.0 copy-start
  15.0 0.5 %shard_map.70 = (bf16[256,512]{1,0:T(8,128)(2,1)S(1)}, f32[16,256]{1,0:T(8,128)S(1)}) custom-call(f32[256,512]{1,0:T(8,128)S(1)} %get-tuple-element.26.summed, f32[256,128]{1,0:T(8,128)S(1)} %get-tuple-element.27.denominator, bf16[48,256]{1,0:T(8,128)(2,1)S(1)} %get-tuple-element.28.far_matrix, bf16[144,512]{1,0:T(8,128)(2,1)S(1)} %collective-permute-done.2.first, ...), custom_call_target="tpu_custom_call" | custom-call | bytes 1269760 | tf_op jit(solution)/shard_map/pallas_call | solution.py:56
  15.5 0.0 collective-permute-start.5
  15.5 1.6 %collective-permute-start.7 = (bf16[144,512]{1,0:T(8,128)(2,1)S(1)}, bf16[144,512]{1,0:T(8,128)(2,1)S(1)}, u32[]{:S(2)}, u32[]{:S(2)}) collective-permute-start(bf16[144,512]{1,0:T(8,128)(2,1)S(1)} %collective-permute-done.third.own_odd), channel_id=1, source_target_pairs={{0,17},{1,5},{2,19},{3,7},{4,0},{5,20},{6,2},{7,22},{8,25},{9,13},... | collective-permute-start | bytes 442376 | tf_op jit(solution)/shard_map/ppermute | solution.py:244
  17.1 1.7 %collective-permute-start.10 = (bf16[144,512]{1,0:T(8,128)(2,1)S(1)}, bf16[144,512]{1,0:T(8,128)(2,1)S(1)}, u32[]{:S(2)}, u32[]{:S(2)}) collective-permute-start(bf16[144,512]{1,0:T(8,128)(2,1)S(1)} %collective-permute-done.third.own_odd), channel_id=1, source_target_pairs={{0,21},{1,17},{2,23},{3,19},{4,20},{5,16},{6,22},{7,18},{8,29},{9,... | collective-permute-start | bytes 442376 | tf_op jit(solution)/shard_map/ppermute | solution.py:244
  18.8 0.0 collective-permute-done.3.first_other
  18.8 0.0 collective-permute-start.9
  18.8 0.0 copy-done
  18.8 0.4 %shard_map.71 = (f32[256,256]{1,0:T(8,128)S(1)}, bf16[272,256]{1,0:T(8,128)(2,1)S(1)}) custom-call(bf16[256,512]{1,0:T(8,128)(2,1)S(1)} %get-tuple-element.44.refined, f32[16,256]{1,0:T(8,128)S(1)} %get-tuple-element.32.squares, bf16[256,512]{1,0:T(8,128)(2,1)S(1)} %copy-done, bf16[144,512]{1,0:T(8,128)(2,1)S(1)} %collective-permute-done.2.first, ...), custom_call_target="tpu_custom_call" | custom-call | bytes 1236992 | tf_op jit(solution)/shard_map/pallas_call | solution.py:56
  19.3 0.7 %collective-permute-done.6.own_odd.pair_even = bf16[144,512]{1,0:T(8,128)(2,1)S(1)} collective-permute-done((bf16[144,512]{1,0:T(8,128)(2,1)S(1)}, bf16[144,512]{1,0:T(8,128)(2,1)S(1)}, u32[]{:S(2)}, u32[]{:S(2)}) %collective-permute-start.6) | collective-permute-done | bytes 147488 | tf_op jit(solution)/shard_map/ppermute | solution.py:244
  20.0 0.5 %collective-permute-start.4 = (bf16[272,256]{1,0:T(8,128)(2,1)S(1)}, bf16[272,256]{1,0:T(8,128)(2,1)S(1)}, u32[]{:S(2)}, u32[]{:S(2)}) collective-permute-start(bf16[272,256]{1,0:T(8,128)(2,1)S(1)} %get-tuple-element.34), channel_id=1, source_target_pairs={{0,1},{1,0},{2,3},{3,2},{4,5},{5,4},{6,7},{7,6},{8,9},{9,8},{10,11... | collective-permute-start | bytes 417800 | tf_op jit(solution)/shard_map/ppermute | solution.py:244
  20.4 1.8 %collective-permute-done.7.own_even.pair_odd = bf16[144,512]{1,0:T(8,128)(2,1)S(1)} collective-permute-done((bf16[144,512]{1,0:T(8,128)(2,1)S(1)}, bf16[144,512]{1,0:T(8,128)(2,1)S(1)}, u32[]{:S(2)}, u32[]{:S(2)}) %collective-permute-start.7) | collective-permute-done | bytes 147488 | tf_op jit(solution)/shard_map/ppermute | solution.py:244
  22.2 0.0 collective-permute-done.5.refined_pair
  22.2 0.3 shard_map.72.late
  22.5 0.0 collective-permute-done.4.early_came
  22.5 0.1 shard_map.73
  22.6 1.6 %collective-permute-start.8 = (bf16[288,128]{1,0:T(8,128)(2,1)S(1)}, bf16[288,128]{1,0:T(8,128)(2,1)S(1)}, u32[]{:S(2)}, u32[]{:S(2)}) collective-permute-start(bf16[288,128]{1,0:T(8,128)(2,1)S(1)} %get-tuple-element.38), channel_id=1, source_target_pairs={{0,2},{1,3},{2,0},{3,1},{4,6},{5,7},{6,4},{7,5},{8,10},{9,11},{10,... | collective-permute-start | bytes 221192 | tf_op jit(solution)/shard_map/ppermute | solution.py:244
  24.2 0.0 collective-permute-done.10.pair_even
  24.2 1.2 %collective-permute-done.9.own_even.pair_odd = bf16[144,512]{1,0:T(8,128)(2,1)S(1)} collective-permute-done((bf16[144,512]{1,0:T(8,128)(2,1)S(1)}, bf16[144,512]{1,0:T(8,128)(2,1)S(1)}, u32[]{:S(2)}, u32[]{:S(2)}) %collective-permute-start.9) | collective-permute-done | bytes 147488 | tf_op jit(solution)/shard_map/ppermute | solution.py:244
  25.3 0.3 shard_map.74.late
  25.7 1.6 %collective-permute-start.11 = (bf16[256,128]{1,0:T(8,128)(2,1)S(1)}, bf16[256,128]{1,0:T(8,128)(2,1)S(1)}, u32[]{:S(2)}, u32[]{:S(2)}) collective-permute-start(bf16[256,128]{1,0:T(8,128)(2,1)S(1)} %get-tuple-element.43), channel_id=1, source_target_pairs={{0,2},{1,3},{2,0},{3,1},{4,6},{5,7},{6,4},{7,5},{8,10},{9,11},{10,... | collective-permute-start | bytes 196616 | tf_op jit(solution)/shard_map/ppermute | solution.py:244
  27.2 0.7 %copy.7 = bf16[256,512]{1,0:T(8,128)(2,1)} copy(bf16[256,512]{1,0:T(8,128)(2,1)S(1)} %get-tuple-element.44.refined) | data formatting | bytes 524288
  27.9 2.1 %collective-permute-done.11.came_last = bf16[256,128]{1,0:T(8,128)(2,1)S(1)} collective-permute-done((bf16[256,128]{1,0:T(8,128)(2,1)S(1)}, bf16[256,128]{1,0:T(8,128)(2,1)S(1)}, u32[]{:S(2)}, u32[]{:S(2)}) %collective-permute-start.11) | collective-permute-done | bytes 65568 | tf_op jit(solution)/shard_map/ppermute | solution.py:244
  30.0 0.0 collective-permute-done.8.came_most
  30.0 0.8 %shard_map.76 = bf16[256,256]{1,0:T(8,128)(2,1)} custom-call(f32[256,128]{1,0:T(8,128)S(1)} %get-tuple-element.36.stay_most, f32[16,256]{1,0:T(8,128)S(1)} %get-tuple-element.37.chip_squares, bf16[288,128]{1,0:T(8,128)(2,1)S(1)} %collective-permute-done.8.came_most, f32[256,128]{1,0:T(8,128)S(1)} %get-tuple-element.42.stay_last, ...), custom_call_target="tpu_custom_call" | custom-call | bytes 548864 | tf_op jit(solution)/shard_map/pallas_call | solution.py:56
  (1 shorter events, 0.0 us)
Async XLA Ops:
  0.6 7.0 %copy-start.1 = (bf16[256,512]{1,0:T(8,128)(2,1)S(1)}, bf16[256,512]{1,0:T(8,128)(2,1)}, u32[]{:S(2)}) copy-start(bf16[256,512]{1,0:T(8,128)(2,1)} %gallery.3) | copy-start | bytes 786436
  0.6 6.9 %copy-start.2 = (s32[256,10]{0,1:T(8,128)S(1)}, s32[256,10]{0,1:T(8,128)}, u32[]{:S(2)}) copy-start(s32[256,10]{0,1:T(8,128)} %param.6) | copy-start | bytes 30724
  0.7 6.9 %copy-start.3 = (s32[256,10]{0,1:T(8,128)S(1)}, s32[256,10]{0,1:T(8,128)}, u32[]{:S(2)}) copy-start(s32[256,10]{0,1:T(8,128)} %param.7) | copy-start | bytes 30724
  1.9 7.1 %collective-permute-start.2 = (bf16[144,512]{1,0:T(8,128)(2,1)S(1)}, bf16[144,512]{1,0:T(8,128)(2,1)S(1)}, u32[]{:S(2)}, u32[]{:S(2)}) collective-permute-start(bf16[144,512]{1,0:T(8,128)(2,1)S(1)} %get-tuple-element.29), channel_id=1, source_target_pairs={{0,4},{1,5},{2,6},{3,7},{4,0},{5,1},{6,2},{7,3},{8,12},{9,13},{10,... | collective-permute-start | bytes 442376 | tf_op jit(solution)/shard_map/ppermute | solution.py:244
  5.0 10.0 %collective-permute-start = (bf16[144,512]{1,0:T(8,128)(2,1)S(1)}, bf16[144,512]{1,0:T(8,128)(2,1)S(1)}, u32[]{:S(2)}, u32[]{:S(2)}) collective-permute-start(bf16[144,512]{1,0:T(8,128)(2,1)S(1)} %get-tuple-element.23), channel_id=1, source_target_pairs={{0,12},{1,13},{2,14},{3,15},{4,8},{5,9},{6,10},{7,11},{8,4},{9,5},... | collective-permute-start | bytes 442376 | tf_op jit(solution)/shard_map/ppermute | solution.py:244
  7.5 7.5 %collective-permute-start.1 = (bf16[16,512]{1,0:T(8,128)(2,1)S(1)}, bf16[16,512]{1,0:T(8,128)(2,1)S(1)}, u32[]{:S(2)}, u32[]{:S(2)}) collective-permute-start(bf16[16,512]{1,0:T(8,128)(2,1)S(1)} %get-tuple-element.24), channel_id=1, source_target_pairs={{0,8},{1,9},{2,10},{3,11},{4,12},{5,13},{6,14},{7,15},{8,0},{9,1},... | collective-permute-start | bytes 49160 | tf_op jit(solution)/shard_map/ppermute | solution.py:244
  9.1 9.8 %collective-permute-start.3 = (bf16[144,512]{1,0:T(8,128)(2,1)S(1)}, bf16[144,512]{1,0:T(8,128)(2,1)S(1)}, u32[]{:S(2)}, u32[]{:S(2)}) collective-permute-start(bf16[144,512]{1,0:T(8,128)(2,1)S(1)} %collective-permute-done.2.first), channel_id=1, source_target_pairs={{0,16},{1,17},{2,18},{3,19},{4,20},{5,21},{6,22},{7,23},{8,24},{9,... | collective-permute-start | bytes 442376 | tf_op jit(solution)/shard_map/ppermute | solution.py:244
  15.0 5.0 %collective-permute-start.6 = (bf16[144,512]{1,0:T(8,128)(2,1)S(1)}, bf16[144,512]{1,0:T(8,128)(2,1)S(1)}, u32[]{:S(2)}, u32[]{:S(2)}) collective-permute-start(bf16[144,512]{1,0:T(8,128)(2,1)S(1)} %collective-permute-done.third.own_odd), channel_id=1, source_target_pairs={{0,5},{1,17},{2,7},{3,19},{4,20},{5,0},{6,22},{7,2},{8,13},{9,25},... | collective-permute-start | bytes 442376 | tf_op jit(solution)/shard_map/ppermute | solution.py:244
  15.0 3.8 %copy-start = (bf16[256,512]{1,0:T(8,128)(2,1)S(1)}, bf16[256,512]{1,0:T(8,128)(2,1)}, u32[]{:S(2)}) copy-start(bf16[256,512]{1,0:T(8,128)(2,1)} %queries.3) | copy-start | bytes 786436
  15.5 6.7 %collective-permute-start.5 = (bf16[256,512]{1,0:T(8,128)(2,1)S(1)}, bf16[256,512]{1,0:T(8,128)(2,1)S(1)}, u32[]{:S(2)}, u32[]{:S(2)}) collective-permute-start(bf16[256,512]{1,0:T(8,128)(2,1)S(1)} %get-tuple-element.44.refined), channel_id=1, source_target_pairs={{0,1},{1,0},{2,3},{3,2},{4,5},{5,4},{6,7},{7,6},{8,9},{9,8},{10,11... | collective-permute-start | bytes 786440 | tf_op jit(solution)/shard_map/ppermute | solution.py:244
  15.5 6.7 %collective-permute-start.7 = (bf16[144,512]{1,0:T(8,128)(2,1)S(1)}, bf16[144,512]{1,0:T(8,128)(2,1)S(1)}, u32[]{:S(2)}, u32[]{:S(2)}) collective-permute-start(bf16[144,512]{1,0:T(8,128)(2,1)S(1)} %collective-permute-done.third.own_odd), channel_id=1, source_target_pairs={{0,17},{1,5},{2,19},{3,7},{4,0},{5,20},{6,2},{7,22},{8,25},{9,13},... | collective-permute-start | bytes 442376 | tf_op jit(solution)/shard_map/ppermute | solution.py:244
  17.1 7.0 %collective-permute-start.10 = (bf16[144,512]{1,0:T(8,128)(2,1)S(1)}, bf16[144,512]{1,0:T(8,128)(2,1)S(1)}, u32[]{:S(2)}, u32[]{:S(2)}) collective-permute-start(bf16[144,512]{1,0:T(8,128)(2,1)S(1)} %collective-permute-done.third.own_odd), channel_id=1, source_target_pairs={{0,21},{1,17},{2,23},{3,19},{4,20},{5,16},{6,22},{7,18},{8,29},{9,... | collective-permute-start | bytes 442376 | tf_op jit(solution)/shard_map/ppermute | solution.py:244
  18.8 6.5 %collective-permute-start.9 = (bf16[144,512]{1,0:T(8,128)(2,1)S(1)}, bf16[144,512]{1,0:T(8,128)(2,1)S(1)}, u32[]{:S(2)}, u32[]{:S(2)}) collective-permute-start(bf16[144,512]{1,0:T(8,128)(2,1)S(1)} %collective-permute-done.third.own_odd), channel_id=1, source_target_pairs={{0,1},{1,21},{2,3},{3,23},{4,16},{5,4},{6,18},{7,6},{8,9},{9,29},{... | collective-permute-start | bytes 442376 | tf_op jit(solution)/shard_map/ppermute | solution.py:244
  20.0 2.6 %collective-permute-start.4 = (bf16[272,256]{1,0:T(8,128)(2,1)S(1)}, bf16[272,256]{1,0:T(8,128)(2,1)S(1)}, u32[]{:S(2)}, u32[]{:S(2)}) collective-permute-start(bf16[272,256]{1,0:T(8,128)(2,1)S(1)} %get-tuple-element.34), channel_id=1, source_target_pairs={{0,1},{1,0},{2,3},{3,2},{4,5},{5,4},{6,7},{7,6},{8,9},{9,8},{10,11... | collective-permute-start | bytes 417800 | tf_op jit(solution)/shard_map/ppermute | solution.py:244
  22.6 7.4 %collective-permute-start.8 = (bf16[288,128]{1,0:T(8,128)(2,1)S(1)}, bf16[288,128]{1,0:T(8,128)(2,1)S(1)}, u32[]{:S(2)}, u32[]{:S(2)}) collective-permute-start(bf16[288,128]{1,0:T(8,128)(2,1)S(1)} %get-tuple-element.38), channel_id=1, source_target_pairs={{0,2},{1,3},{2,0},{3,1},{4,6},{5,7},{6,4},{7,5},{8,10},{9,11},{10,... | collective-permute-start | bytes 221192 | tf_op jit(solution)/shard_map/ppermute | solution.py:244
  25.7 4.3 %collective-permute-start.11 = (bf16[256,128]{1,0:T(8,128)(2,1)S(1)}, bf16[256,128]{1,0:T(8,128)(2,1)S(1)}, u32[]{:S(2)}, u32[]{:S(2)}) collective-permute-start(bf16[256,128]{1,0:T(8,128)(2,1)S(1)} %get-tuple-element.43), channel_id=1, source_target_pairs={{0,2},{1,3},{2,0},{3,1},{4,6},{5,7},{6,4},{7,5},{8,10},{9,11},{10,... | collective-permute-start | bytes 196616 | tf_op jit(solution)/shard_map/ppermute | solution.py:244

commit v4 on v2

--- a/solution.py
+++ b/solution.py
@@ -163,7 +163,7 @@
     give[row_count:, :] = three_parts(squares[...])
 
 
-def late_kernel(refined, third, third_other, second, second_other, keep, give):
+def late_kernel(refined, third, second_other, third_other, second, keep, give):
     g, z, q = (lax.axis_index(name) for name in AXES)
     half = third_other.shape[0]
     odd = lax.rem(q + z, 2) == 1
@@ -268,9 +268,9 @@
         [array((row_count, query_count), high), array((row_count, query_count), low)],
         refined,
         third,
+        second_other,
         third_other,
         second,
-        second_other,
     )
     late_came = send(late_give, lambda g, z, q: (g, z, q ^ 1))
     stay, leave = call(

time: 31.5 us -> 31.2 us (level)
    ppermute x10, waiting for transfers between devices: 13.4 us -> 13.1 us  [send(): return lax.ppermute(value, AXES, pairs)]
  transfers between devices with their start and end apart: 10 -> 10, of which waited for: 8 -> 7; matrix products, arithmetic and copies ran while one was open for 2% -> 2% of each run, Pallas kernels for 6% -> 6%
where the time goes in v4:
time: 31.2 us; the launch traced here: 31 us
  waiting for transfers between devices  13.1 us (42%)
  starting transfers between devices  12.4 us (40%)
  Pallas kernels  4.03 us (13%)
  local copies, waits for them, and re-layouts  0.74 us (2%)
  between operations  0.74 us (2%)
    ppermute x10, waiting for transfers between devices, send(): return lax.ppermute(value, AXES, pairs)  13.1 us
    ppermute x10, starting transfers between devices, send(): return lax.ppermute(value, AXES, pairs)  12.4 us
    pallas_call x6, Pallas kernels, call(): pl.pallas_call(kernel, out_shape=list(outs), in_specs=specs or [VMEM] * l...  4.03 us
    unnamed x9, local copies, waits for them, and re-layouts  0.72 us
  transfers between devices with their start and end apart: 10, of which 7 were waited for; matrix products, arithmetic and copies ran while one was open for 2% of the time, Pallas kernels for 6%

profile of v4, /device:TPU:0, one launch (start us, length us, event | category | flops | bytes accessed | tf_op | source)
XLA Modules:
  0.0 31.0 jit_solution(5846357393417786497)
XLA Ops:
  0.6 1.2 %shard_map.68 = (bf16[144,512]{1,0:T(8,128)(2,1)S(1)}, bf16[144,512]{1,0:T(8,128)(2,1)S(1)}, bf16[16,512]{1,0:T(8,128)(2,1)S(1)}) custom-call(bf16[256,512]{1,0:T(8,128)(2,1)} %queries.3, bf16[256,512]{1,0:T(8,128)(2,1)} %gallery.3, s32[1,64]{1,0:T(1,128)} %send_rows.1), custom_call_target="tpu_custom_call" | custom-call | bytes 835840 | tf_op jit(solution)/shard_map/pallas_call | solution.py:56
  1.8 3.1 %collective-permute-start = (bf16[144,512]{1,0:T(8,128)(2,1)S(1)}, bf16[144,512]{1,0:T(8,128)(2,1)S(1)}, u32[]{:S(2)}, u32[]{:S(2)}) collective-permute-start(bf16[144,512]{1,0:T(8,128)(2,1)S(1)} %get-tuple-element.15), channel_id=1, source_target_pairs={{0,4},{1,5},{2,6},{3,7},{4,0},{5,1},{6,2},{7,3},{8,12},{9,13},{10,... | collective-permute-start | bytes 442376 | tf_op jit(solution)/shard_map/ppermute | solution.py:222
  4.9 2.5 %collective-permute-start.1 = (bf16[144,512]{1,0:T(8,128)(2,1)S(1)}, bf16[144,512]{1,0:T(8,128)(2,1)S(1)}, u32[]{:S(2)}, u32[]{:S(2)}) collective-permute-start(bf16[144,512]{1,0:T(8,128)(2,1)S(1)} %get-tuple-element.16), channel_id=1, source_target_pairs={{0,12},{1,13},{2,14},{3,15},{4,8},{5,9},{6,10},{7,11},{8,4},{9,5},... | collective-permute-start | bytes 442376 | tf_op jit(solution)/shard_map/ppermute | solution.py:222
  7.4 0.0 copy-start.1
  7.4 0.1 collective-permute-start.2
  7.5 1.5 %collective-permute-done.first = bf16[144,512]{1,0:T(8,128)(2,1)S(1)} collective-permute-done((bf16[144,512]{1,0:T(8,128)(2,1)S(1)}, bf16[144,512]{1,0:T(8,128)(2,1)S(1)}, u32[]{:S(2)}, u32[]{:S(2)}) %collective-permute-start) | collective-permute-done | bytes 147488 | tf_op jit(solution)/shard_map/ppermute | solution.py:222
  9.0 0.0 copy-start.2
  9.0 0.0 copy-start.3
  9.0 1.6 %collective-permute-start.3 = (bf16[128,512]{1,0:T(8,128)(2,1)S(1)}, bf16[128,512]{1,0:T(8,128)(2,1)S(1)}, u32[]{:S(2)}, u32[]{:S(2)}) collective-permute-start(bf16[128,512]{1,0:T(8,128)(2,1)S(1)} %slice.9), channel_id=1, source_target_pairs={{0,16},{1,17},{2,18},{3,19},{4,20},{5,21},{6,22},{7,23},{8,24},{9,... | collective-permute-start | bytes 393224 | tf_op jit(solution)/shard_map/ppermute | solution.py:222
  10.6 3.8 %collective-permute-done.1.third = bf16[144,512]{1,0:T(8,128)(2,1)S(1)} collective-permute-done((bf16[144,512]{1,0:T(8,128)(2,1)S(1)}, bf16[144,512]{1,0:T(8,128)(2,1)S(1)}, u32[]{:S(2)}, u32[]{:S(2)}) %collective-permute-start.1) | collective-permute-done | bytes 147488 | tf_op jit(solution)/shard_map/ppermute | solution.py:222
  14.4 0.5 %collective-permute-done.2.second = bf16[16,512]{1,0:T(8,128)(2,1)S(1)} collective-permute-done((bf16[16,512]{1,0:T(8,128)(2,1)S(1)}, bf16[16,512]{1,0:T(8,128)(2,1)S(1)}, u32[]{:S(2)}, u32[]{:S(2)}) %collective-permute-start.2) | collective-permute-done | bytes 16416 | tf_op jit(solution)/shard_map/ppermute | solution.py:222
  14.9 1.4 %collective-permute-start.5 = (bf16[128,512]{1,0:T(8,128)(2,1)S(1)}, bf16[128,512]{1,0:T(8,128)(2,1)S(1)}, u32[]{:S(2)}, u32[]{:S(2)}) collective-permute-start(bf16[128,512]{1,0:T(8,128)(2,1)S(1)} %slice.8), channel_id=1, source_target_pairs={{0,20},{1,21},{2,22},{3,23},{4,16},{5,17},{6,18},{7,19},{8,28},{9,... | collective-permute-start | bytes 393224 | tf_op jit(solution)/shard_map/ppermute | solution.py:222
  16.4 0.5 %collective-permute-start.6 = (bf16[128,512]{1,0:T(8,128)(2,1)S(1)}, bf16[128,512]{1,0:T(8,128)(2,1)S(1)}, u32[]{:S(2)}, u32[]{:S(2)}) collective-permute-start(bf16[128,512]{1,0:T(8,128)(2,1)S(1)} %slice.8), channel_id=1, source_target_pairs={{0,16},{1,17},{2,18},{3,19},{4,20},{5,21},{6,22},{7,23},{8,24},{9,... | collective-permute-start | bytes 393224 | tf_op jit(solution)/shard_map/ppermute | solution.py:222
  16.9 1.5 %collective-permute-start.7 = (bf16[128,512]{1,0:T(8,128)(2,1)S(1)}, bf16[128,512]{1,0:T(8,128)(2,1)S(1)}, u32[]{:S(2)}, u32[]{:S(2)}) collective-permute-start(bf16[128,512]{1,0:T(8,128)(2,1)S(1)} %slice.8), channel_id=1, source_target_pairs={{0,4},{1,5},{2,6},{3,7},{4,0},{5,1},{6,2},{7,3},{8,12},{9,13},{10,... | collective-permute-start | bytes 393224 | tf_op jit(solution)/shard_map/ppermute | solution.py:222
  18.4 0.0 copy-done.1
  18.4 0.0 copy-done.2
  18.4 0.0 copy-done.3
  18.4 0.0 copy-start
  18.4 1.1 %shard_map.69 = (bf16[256,512]{1,0:T(8,128)(2,1)S(1)}, f32[16,256]{1,0:T(8,128)S(1)}) custom-call(bf16[256,512]{1,0:T(8,128)(2,1)S(1)} %copy-done.1, s32[10,256]{1,0:T(8,128)S(1)} %bitcast.2, s32[10,256]{1,0:T(8,128)S(1)} %bitcast.3, bf16[144,512]{1,0:T(8,128)(2,1)S(1)} %collective-permute-done.first, bf16[16,512]{1,0:T(8,128)(2,1)S(1)} %collective-permute-done.2.second, ...), custom_call_target="tpu_custom_call" | custom-call | bytes 872448 | tf_op jit(solution)/shard_map/pallas_call | solution.py:56
  19.5 0.0 collective-permute-done.3.first_other
  19.5 0.0 copy-done
  19.6 0.4 %shard_map.70 = (f32[256,256]{1,0:T(8,128)S(1)}, bf16[272,256]{1,0:T(8,128)(2,1)S(1)}) custom-call(bf16[256,512]{1,0:T(8,128)(2,1)S(1)} %get-tuple-element.28.refined, f32[16,256]{1,0:T(8,128)S(1)} %get-tuple-element.20.squares, bf16[256,512]{1,0:T(8,128)(2,1)S(1)} %copy-done, bf16[144,512]{1,0:T(8,128)(2,1)S(1)} %collective-permute-done.first, ...), custom_call_target="tpu_custom_call" | custom-call | bytes 1220608 | tf_op jit(solution)/shard_map/pallas_call | solution.py:56
  20.0 0.1 collective-permute-start.4
  20.1 1.1 %collective-permute-done.5.second_other = bf16[128,512]{1,0:T(8,128)(2,1)S(1)} collective-permute-done((bf16[128,512]{1,0:T(8,128)(2,1)S(1)}, bf16[128,512]{1,0:T(8,128)(2,1)S(1)}, u32[]{:S(2)}, u32[]{:S(2)}) %collective-permute-start.5) | collective-permute-done | bytes 131104 | tf_op jit(solution)/shard_map/ppermute | solution.py:222
  21.2 1.3 %collective-permute-done.6.third_other = bf16[128,512]{1,0:T(8,128)(2,1)S(1)} collective-permute-done((bf16[128,512]{1,0:T(8,128)(2,1)S(1)}, bf16[128,512]{1,0:T(8,128)(2,1)S(1)}, u32[]{:S(2)}, u32[]{:S(2)}) %collective-permute-start.6) | collective-permute-done | bytes 131104 | tf_op jit(solution)/shard_map/ppermute | solution.py:222
  22.5 0.0 collective-permute-done.7.second
  22.5 0.4 %shard_map.71 = (f32[256,256]{1,0:T(8,128)S(1)}, bf16[256,256]{1,0:T(8,128)(2,1)S(1)}) custom-call(bf16[256,512]{1,0:T(8,128)(2,1)S(1)} %get-tuple-element.28.refined, bf16[144,512]{1,0:T(8,128)(2,1)S(1)} %collective-permute-done.1.third, bf16[128,512]{1,0:T(8,128)(2,1)S(1)} %collective-permute-done.5.second_other, ...), custom_call_target="tpu_custom_call" | custom-call | bytes 1196032 | tf_op jit(solution)/shard_map/pallas_call | solution.py:56
  22.9 0.1 collective-permute-start.8
  23.0 1.3 %collective-permute-done.8.late_came = bf16[256,256]{1,0:T(8,128)(2,1)S(1)} collective-permute-done((bf16[256,256]{1,0:T(8,128)(2,1)S(1)}, bf16[256,256]{1,0:T(8,128)(2,1)S(1)}, u32[]{:S(2)}, u32[]{:S(2)}) %collective-permute-start.8) | collective-permute-done | bytes 131104 | tf_op jit(solution)/shard_map/ppermute | solution.py:222
  24.3 0.0 collective-permute-done.4.early_came
  24.3 0.1 shard_map.72
  24.4 1.5 %collective-permute-start.9 = (bf16[272,256]{1,0:T(8,128)(2,1)S(1)}, bf16[272,256]{1,0:T(8,128)(2,1)S(1)}, u32[]{:S(2)}, u32[]{:S(2)}) collective-permute-start(bf16[272,256]{1,0:T(8,128)(2,1)S(1)} %get-tuple-element.27), channel_id=1, source_target_pairs={{0,2},{1,3},{2,0},{3,1},{4,6},{5,7},{6,4},{7,5},{8,10},{9,11},{10,... | collective-permute-start | bytes 417800 | tf_op jit(solution)/shard_map/ppermute | solution.py:222
  26.0 0.7 %copy.7 = bf16[256,512]{1,0:T(8,128)(2,1)} copy(bf16[256,512]{1,0:T(8,128)(2,1)S(1)} %get-tuple-element.28.refined) | data formatting | bytes 524288
  26.7 3.5 %collective-permute-done.9.came = bf16[272,256]{1,0:T(8,128)(2,1)S(1)} collective-permute-done((bf16[272,256]{1,0:T(8,128)(2,1)S(1)}, bf16[272,256]{1,0:T(8,128)(2,1)S(1)}, u32[]{:S(2)}, u32[]{:S(2)}) %collective-permute-start.9) | collective-permute-done | bytes 139296 | tf_op jit(solution)/shard_map/ppermute | solution.py:222
  30.2 0.8 %shard_map.73 = bf16[256,256]{1,0:T(8,128)(2,1)} custom-call(f32[272,256]{1,0:T(8,128)S(1)} %get-tuple-element.26.stay, bf16[272,256]{1,0:T(8,128)(2,1)S(1)} %collective-permute-done.9.came), custom_call_target="tpu_custom_call" | custom-call | bytes 548864 | tf_op jit(solution)/shard_map/pallas_call | solution.py:56
  (2 shorter events, 0.0 us)
Async XLA Ops:
  1.8 7.1 %collective-permute-start = (bf16[144,512]{1,0:T(8,128)(2,1)S(1)}, bf16[144,512]{1,0:T(8,128)(2,1)S(1)}, u32[]{:S(2)}, u32[]{:S(2)}) collective-permute-start(bf16[144,512]{1,0:T(8,128)(2,1)S(1)} %get-tuple-element.15), channel_id=1, source_target_pairs={{0,4},{1,5},{2,6},{3,7},{4,0},{5,1},{6,2},{7,3},{8,12},{9,13},{10,... | collective-permute-start | bytes 442376 | tf_op jit(solution)/shard_map/ppermute | solution.py:222
  4.9 9.5 %collective-permute-start.1 = (bf16[144,512]{1,0:T(8,128)(2,1)S(1)}, bf16[144,512]{1,0:T(8,128)(2,1)S(1)}, u32[]{:S(2)}, u32[]{:S(2)}) collective-permute-start(bf16[144,512]{1,0:T(8,128)(2,1)S(1)} %get-tuple-element.16), channel_id=1, source_target_pairs={{0,12},{1,13},{2,14},{3,15},{4,8},{5,9},{6,10},{7,11},{8,4},{9,5},... | collective-permute-start | bytes 442376 | tf_op jit(solution)/shard_map/ppermute | solution.py:222
  7.4 11.0 %copy-start.1 = (bf16[256,512]{1,0:T(8,128)(2,1)S(1)}, bf16[256,512]{1,0:T(8,128)(2,1)}, u32[]{:S(2)}) copy-start(bf16[256,512]{1,0:T(8,128)(2,1)} %gallery.3) | copy-start | bytes 786436
  7.4 7.5 %collective-permute-start.2 = (bf16[16,512]{1,0:T(8,128)(2,1)S(1)}, bf16[16,512]{1,0:T(8,128)(2,1)S(1)}, u32[]{:S(2)}, u32[]{:S(2)}) collective-permute-start(bf16[16,512]{1,0:T(8,128)(2,1)S(1)} %get-tuple-element.17), channel_id=1, source_target_pairs={{0,8},{1,9},{2,10},{3,11},{4,12},{5,13},{6,14},{7,15},{8,0},{9,1},... | collective-permute-start | bytes 49160 | tf_op jit(solution)/shard_map/ppermute | solution.py:222
  9.0 9.4 %copy-start.2 = (s32[256,10]{0,1:T(8,128)S(1)}, s32[256,10]{0,1:T(8,128)}, u32[]{:S(2)}) copy-start(s32[256,10]{0,1:T(8,128)} %param.6) | copy-start | bytes 30724
  9.0 9.4 %copy-start.3 = (s32[256,10]{0,1:T(8,128)S(1)}, s32[256,10]{0,1:T(8,128)}, u32[]{:S(2)}) copy-start(s32[256,10]{0,1:T(8,128)} %param.7) | copy-start | bytes 30724
  9.0 10.5 %collective-permute-start.3 = (bf16[128,512]{1,0:T(8,128)(2,1)S(1)}, bf16[128,512]{1,0:T(8,128)(2,1)S(1)}, u32[]{:S(2)}, u32[]{:S(2)}) collective-permute-start(bf16[128,512]{1,0:T(8,128)(2,1)S(1)} %slice.9), channel_id=1, source_target_pairs={{0,16},{1,17},{2,18},{3,19},{4,20},{5,21},{6,22},{7,23},{8,24},{9,... | collective-permute-start | bytes 393224 | tf_op jit(solution)/shard_map/ppermute | solution.py:222
  14.9 6.2 %collective-permute-start.5 = (bf16[128,512]{1,0:T(8,128)(2,1)S(1)}, bf16[128,512]{1,0:T(8,128)(2,1)S(1)}, u32[]{:S(2)}, u32[]{:S(2)}) collective-permute-start(bf16[128,512]{1,0:T(8,128)(2,1)S(1)} %slice.8), channel_id=1, source_target_pairs={{0,20},{1,21},{2,22},{3,23},{4,16},{5,17},{6,18},{7,19},{8,28},{9,... | collective-permute-start | bytes 393224 | tf_op jit(solution)/shard_map/ppermute | solution.py:222
  16.4 6.1 %collective-permute-start.6 = (bf16[128,512]{1,0:T(8,128)(2,1)S(1)}, bf16[128,512]{1,0:T(8,128)(2,1)S(1)}, u32[]{:S(2)}, u32[]{:S(2)}) collective-permute-start(bf16[128,512]{1,0:T(8,128)(2,1)S(1)} %slice.8), channel_id=1, source_target_pairs={{0,16},{1,17},{2,18},{3,19},{4,20},{5,21},{6,22},{7,23},{8,24},{9,... | collective-permute-start | bytes 393224 | tf_op jit(solution)/shard_map/ppermute | solution.py:222
  16.9 5.6 %collective-permute-start.7 = (bf16[128,512]{1,0:T(8,128)(2,1)S(1)}, bf16[128,512]{1,0:T(8,128)(2,1)S(1)}, u32[]{:S(2)}, u32[]{:S(2)}) collective-permute-start(bf16[128,512]{1,0:T(8,128)(2,1)S(1)} %slice.8), channel_id=1, source_target_pairs={{0,4},{1,5},{2,6},{3,7},{4,0},{5,1},{6,2},{7,3},{8,12},{9,13},{10,... | collective-permute-start | bytes 393224 | tf_op jit(solution)/shard_map/ppermute | solution.py:222
  18.4 1.1 %copy-start = (bf16[256,512]{1,0:T(8,128)(2,1)S(1)}, bf16[256,512]{1,0:T(8,128)(2,1)}, u32[]{:S(2)}) copy-start(bf16[256,512]{1,0:T(8,128)(2,1)} %queries.3) | copy-start | bytes 786436
  20.0 4.3 %collective-permute-start.4 = (bf16[272,256]{1,0:T(8,128)(2,1)S(1)}, bf16[272,256]{1,0:T(8,128)(2,1)S(1)}, u32[]{:S(2)}, u32[]{:S(2)}) collective-permute-start(bf16[272,256]{1,0:T(8,128)(2,1)S(1)} %get-tuple-element.22), channel_id=1, source_target_pairs={{0,1},{1,0},{2,3},{3,2},{4,5},{5,4},{6,7},{7,6},{8,9},{9,8},{10,11... | collective-permute-start | bytes 417800 | tf_op jit(solution)/shard_map/ppermute | solution.py:222
  22.9 1.4 %collective-permute-start.8 = (bf16[256,256]{1,0:T(8,128)(2,1)S(1)}, bf16[256,256]{1,0:T(8,128)(2,1)S(1)}, u32[]{:S(2)}, u32[]{:S(2)}) collective-permute-start(bf16[256,256]{1,0:T(8,128)(2,1)S(1)} %get-tuple-element.25), channel_id=1, source_target_pairs={{0,1},{1,0},{2,3},{3,2},{4,5},{5,4},{6,7},{7,6},{8,9},{9,8},{10,11... | collective-permute-start | bytes 393224 | tf_op jit(solution)/shard_map/ppermute | solution.py:222
  24.4 5.8 %collective-permute-start.9 = (bf16[272,256]{1,0:T(8,128)(2,1)S(1)}, bf16[272,256]{1,0:T(8,128)(2,1)S(1)}, u32[]{:S(2)}, u32[]{:S(2)}) collective-permute-start(bf16[272,256]{1,0:T(8,128)(2,1)S(1)} %get-tuple-element.27), channel_id=1, source_target_pairs={{0,2},{1,3},{2,0},{3,1},{4,6},{5,7},{6,4},{7,5},{8,10},{9,11},{10,... | collective-permute-start | bytes 417800 | tf_op jit(solution)/shard_map/ppermute | solution.py:222

commit v5 on v4

--- a/solution.py
+++ b/solution.py
@@ -167,12 +167,14 @@
     g, z, q = (lax.axis_index(name) for name in AXES)
     half = third_other.shape[0]
     odd = lax.rem(q + z, 2) == 1
-    rows = refined[...]
-    for place, one, two in ((g, third, second), (1 - g, third_other, second_other)):
+    one = jnp.concatenate([third[0:half, :], third_other[...]], axis=0)
+    two = jnp.concatenate([second[...], second_other[...]], axis=0)
+    kept = dot_rows(refined[...], jnp.where(odd, one, two))
+    given = dot_rows(refined[...], jnp.where(odd, two, one)).astype(jnp.bfloat16)
+    for place, part in ((g, slice(0, half)), (1 - g, slice(half, 2 * half))):
         columns = pl.ds(pl.multiple_of(place * half, half), half)
-        one, two = one[0:half, :], two[0:half, :]
-        keep[:, columns] = dot_rows(rows, jnp.where(odd, one, two))
-        give[:, columns] = dot_rows(rows, jnp.where(odd, two, one)).astype(jnp.bfloat16)
+        keep[:, columns] = kept[:, part]
+        give[:, columns] = given[:, part]
 
 
 def whole(parts):

time: 31.2 us -> 31.1 us (level)
  no operation moved by 1% of the time
where the time goes in v5:
time: 31.1 us; the launch traced here: 30.9 us
  waiting for transfers between devices  13.1 us (42%)
  starting transfers between devices  12.4 us (40%)
  Pallas kernels  3.93 us (13%)
  local copies, waits for them, and re-layouts  0.74 us (2%)
  between operations  0.74 us (2%)
    ppermute x10, waiting for transfers between devices, send(): return lax.ppermute(value, AXES, pairs)  13.1 us
    ppermute x10, starting transfers between devices, send(): return lax.ppermute(value, AXES, pairs)  12.4 us
    pallas_call x6, Pallas kernels, call(): pl.pallas_call(kernel, out_shape=list(outs), in_specs=specs or [VMEM] * l...  3.93 us
    unnamed x9, local copies, waits for them, and re-layouts  0.72 us
  transfers between devices with their start and end apart: 10, of which 7 were waited for; matrix products, arithmetic and copies ran while one was open for 2% of the time, Pallas kernels for 6%

profile of v5, /device:TPU:0, one launch (start us, length us, event | category | flops | bytes accessed | tf_op | source)
XLA Modules:
  0.0 30.9 jit_solution(5496588757035994708)
XLA Ops:
  0.6 1.2 %shard_map.68 = (bf16[144,512]{1,0:T(8,128)(2,1)S(1)}, bf16[144,512]{1,0:T(8,128)(2,1)S(1)}, bf16[16,512]{1,0:T(8,128)(2,1)S(1)}) custom-call(bf16[256,512]{1,0:T(8,128)(2,1)} %queries.3, bf16[256,512]{1,0:T(8,128)(2,1)} %gallery.3, s32[1,64]{1,0:T(1,128)} %send_rows.1), custom_call_target="tpu_custom_call" | custom-call | bytes 835840 | tf_op jit(solution)/shard_map/pallas_call | solution.py:56
  1.8 3.1 %collective-permute-start = (bf16[144,512]{1,0:T(8,128)(2,1)S(1)}, bf16[144,512]{1,0:T(8,128)(2,1)S(1)}, u32[]{:S(2)}, u32[]{:S(2)}) collective-permute-start(bf16[144,512]{1,0:T(8,128)(2,1)S(1)} %get-tuple-element.15), channel_id=1, source_target_pairs={{0,4},{1,5},{2,6},{3,7},{4,0},{5,1},{6,2},{7,3},{8,12},{9,13},{10,... | collective-permute-start | bytes 442376 | tf_op jit(solution)/shard_map/ppermute | solution.py:224
  4.9 2.5 %collective-permute-start.1 = (bf16[144,512]{1,0:T(8,128)(2,1)S(1)}, bf16[144,512]{1,0:T(8,128)(2,1)S(1)}, u32[]{:S(2)}, u32[]{:S(2)}) collective-permute-start(bf16[144,512]{1,0:T(8,128)(2,1)S(1)} %get-tuple-element.16), channel_id=1, source_target_pairs={{0,12},{1,13},{2,14},{3,15},{4,8},{5,9},{6,10},{7,11},{8,4},{9,5},... | collective-permute-start | bytes 442376 | tf_op jit(solution)/shard_map/ppermute | solution.py:224
  7.4 0.0 copy-start.1
  7.4 0.1 collective-permute-start.2
  7.5 1.5 %collective-permute-done.first = bf16[144,512]{1,0:T(8,128)(2,1)S(1)} collective-permute-done((bf16[144,512]{1,0:T(8,128)(2,1)S(1)}, bf16[144,512]{1,0:T(8,128)(2,1)S(1)}, u32[]{:S(2)}, u32[]{:S(2)}) %collective-permute-start) | collective-permute-done | bytes 147488 | tf_op jit(solution)/shard_map/ppermute | solution.py:224
  9.0 0.0 copy-start.2
  9.0 0.0 copy-start.3
  9.0 1.6 %collective-permute-start.3 = (bf16[128,512]{1,0:T(8,128)(2,1)S(1)}, bf16[128,512]{1,0:T(8,128)(2,1)S(1)}, u32[]{:S(2)}, u32[]{:S(2)}) collective-permute-start(bf16[128,512]{1,0:T(8,128)(2,1)S(1)} %slice.9), channel_id=1, source_target_pairs={{0,16},{1,17},{2,18},{3,19},{4,20},{5,21},{6,22},{7,23},{8,24},{9,... | collective-permute-start | bytes 393224 | tf_op jit(solution)/shard_map/ppermute | solution.py:224
  10.6 3.8 %collective-permute-done.1.third = bf16[144,512]{1,0:T(8,128)(2,1)S(1)} collective-permute-done((bf16[144,512]{1,0:T(8,128)(2,1)S(1)}, bf16[144,512]{1,0:T(8,128)(2,1)S(1)}, u32[]{:S(2)}, u32[]{:S(2)}) %collective-permute-start.1) | collective-permute-done | bytes 147488 | tf_op jit(solution)/shard_map/ppermute | solution.py:224
  14.4 0.5 %collective-permute-done.2.second = bf16[16,512]{1,0:T(8,128)(2,1)S(1)} collective-permute-done((bf16[16,512]{1,0:T(8,128)(2,1)S(1)}, bf16[16,512]{1,0:T(8,128)(2,1)S(1)}, u32[]{:S(2)}, u32[]{:S(2)}) %collective-permute-start.2) | collective-permute-done | bytes 16416 | tf_op jit(solution)/shard_map/ppermute | solution.py:224
  14.9 1.4 %collective-permute-start.5 = (bf16[128,512]{1,0:T(8,128)(2,1)S(1)}, bf16[128,512]{1,0:T(8,128)(2,1)S(1)}, u32[]{:S(2)}, u32[]{:S(2)}) collective-permute-start(bf16[128,512]{1,0:T(8,128)(2,1)S(1)} %slice.8), channel_id=1, source_target_pairs={{0,20},{1,21},{2,22},{3,23},{4,16},{5,17},{6,18},{7,19},{8,28},{9,... | collective-permute-start | bytes 393224 | tf_op jit(solution)/shard_map/ppermute | solution.py:224
  16.4 0.5 %collective-permute-start.6 = (bf16[128,512]{1,0:T(8,128)(2,1)S(1)}, bf16[128,512]{1,0:T(8,128)(2,1)S(1)}, u32[]{:S(2)}, u32[]{:S(2)}) collective-permute-start(bf16[128,512]{1,0:T(8,128)(2,1)S(1)} %slice.8), channel_id=1, source_target_pairs={{0,16},{1,17},{2,18},{3,19},{4,20},{5,21},{6,22},{7,23},{8,24},{9,... | collective-permute-start | bytes 393224 | tf_op jit(solution)/shard_map/ppermute | solution.py:224
  16.9 1.5 %collective-permute-start.7 = (bf16[128,512]{1,0:T(8,128)(2,1)S(1)}, bf16[128,512]{1,0:T(8,128)(2,1)S(1)}, u32[]{:S(2)}, u32[]{:S(2)}) collective-permute-start(bf16[128,512]{1,0:T(8,128)(2,1)S(1)} %slice.8), channel_id=1, source_target_pairs={{0,4},{1,5},{2,6},{3,7},{4,0},{5,1},{6,2},{7,3},{8,12},{9,13},{10,... | collective-permute-start | bytes 393224 | tf_op jit(solution)/shard_map/ppermute | solution.py:224
  18.4 0.0 copy-done.1
  18.4 0.0 copy-done.2
  18.4 0.0 copy-done.3
  18.4 0.0 copy-start
  18.4 1.1 %shard_map.69 = (bf16[256,512]{1,0:T(8,128)(2,1)S(1)}, f32[16,256]{1,0:T(8,128)S(1)}) custom-call(bf16[256,512]{1,0:T(8,128)(2,1)S(1)} %copy-done.1, s32[10,256]{1,0:T(8,128)S(1)} %bitcast.2, s32[10,256]{1,0:T(8,128)S(1)} %bitcast.3, bf16[144,512]{1,0:T(8,128)(2,1)S(1)} %collective-permute-done.first, bf16[16,512]{1,0:T(8,128)(2,1)S(1)} %collective-permute-done.2.second, ...), custom_call_target="tpu_custom_call" | custom-call | bytes 872448 | tf_op jit(solution)/shard_map/pallas_call | solution.py:56
  19.5 0.0 collective-permute-done.3.first_other
  19.5 0.0 copy-done
  19.6 0.4 %shard_map.70 = (f32[256,256]{1,0:T(8,128)S(1)}, bf16[272,256]{1,0:T(8,128)(2,1)S(1)}) custom-call(bf16[256,512]{1,0:T(8,128)(2,1)S(1)} %get-tuple-element.28.refined, f32[16,256]{1,0:T(8,128)S(1)} %get-tuple-element.20.squares, bf16[256,512]{1,0:T(8,128)(2,1)S(1)} %copy-done, bf16[144,512]{1,0:T(8,128)(2,1)S(1)} %collective-permute-done.first, ...), custom_call_target="tpu_custom_call" | custom-call | bytes 1220608 | tf_op jit(solution)/shard_map/pallas_call | solution.py:56
  20.0 0.1 collective-permute-start.4
  20.1 1.1 %collective-permute-done.5.second_other = bf16[128,512]{1,0:T(8,128)(2,1)S(1)} collective-permute-done((bf16[128,512]{1,0:T(8,128)(2,1)S(1)}, bf16[128,512]{1,0:T(8,128)(2,1)S(1)}, u32[]{:S(2)}, u32[]{:S(2)}) %collective-permute-start.5) | collective-permute-done | bytes 131104 | tf_op jit(solution)/shard_map/ppermute | solution.py:224
  21.2 1.3 %collective-permute-done.6.third_other = bf16[128,512]{1,0:T(8,128)(2,1)S(1)} collective-permute-done((bf16[128,512]{1,0:T(8,128)(2,1)S(1)}, bf16[128,512]{1,0:T(8,128)(2,1)S(1)}, u32[]{:S(2)}, u32[]{:S(2)}) %collective-permute-start.6) | collective-permute-done | bytes 131104 | tf_op jit(solution)/shard_map/ppermute | solution.py:224
  22.5 0.0 collective-permute-done.7.second
  22.5 0.3 %shard_map.71 = (f32[256,256]{1,0:T(8,128)S(1)}, bf16[256,256]{1,0:T(8,128)(2,1)S(1)}) custom-call(bf16[256,512]{1,0:T(8,128)(2,1)S(1)} %get-tuple-element.28.refined, bf16[144,512]{1,0:T(8,128)(2,1)S(1)} %collective-permute-done.1.third, bf16[128,512]{1,0:T(8,128)(2,1)S(1)} %collective-permute-done.5.second_other, ...), custom_call_target="tpu_custom_call" | custom-call | bytes 1196032 | tf_op jit(solution)/shard_map/pallas_call | solution.py:56
  22.8 0.1 collective-permute-start.8
  22.9 1.3 %collective-permute-done.8.late_came = bf16[256,256]{1,0:T(8,128)(2,1)S(1)} collective-permute-done((bf16[256,256]{1,0:T(8,128)(2,1)S(1)}, bf16[256,256]{1,0:T(8,128)(2,1)S(1)}, u32[]{:S(2)}, u32[]{:S(2)}) %collective-permute-start.8) | collective-permute-done | bytes 131104 | tf_op jit(solution)/shard_map/ppermute | solution.py:224
  24.2 0.0 collective-permute-done.4.early_came
  24.2 0.1 shard_map.72
  24.3 1.5 %collective-permute-start.9 = (bf16[272,256]{1,0:T(8,128)(2,1)S(1)}, bf16[272,256]{1,0:T(8,128)(2,1)S(1)}, u32[]{:S(2)}, u32[]{:S(2)}) collective-permute-start(bf16[272,256]{1,0:T(8,128)(2,1)S(1)} %get-tuple-element.27), channel_id=1, source_target_pairs={{0,2},{1,3},{2,0},{3,1},{4,6},{5,7},{6,4},{7,5},{8,10},{9,11},{10,... | collective-permute-start | bytes 417800 | tf_op jit(solution)/shard_map/ppermute | solution.py:224
  25.9 0.7 %copy.7 = bf16[256,512]{1,0:T(8,128)(2,1)} copy(bf16[256,512]{1,0:T(8,128)(2,1)S(1)} %get-tuple-element.28.refined) | data formatting | bytes 524288
  26.6 3.5 %collective-permute-done.9.came = bf16[272,256]{1,0:T(8,128)(2,1)S(1)} collective-permute-done((bf16[272,256]{1,0:T(8,128)(2,1)S(1)}, bf16[272,256]{1,0:T(8,128)(2,1)S(1)}, u32[]{:S(2)}, u32[]{:S(2)}) %collective-permute-start.9) | collective-permute-done | bytes 139296 | tf_op jit(solution)/shard_map/ppermute | solution.py:224
  30.1 0.8 %shard_map.73 = bf16[256,256]{1,0:T(8,128)(2,1)} custom-call(f32[272,256]{1,0:T(8,128)S(1)} %get-tuple-element.26.stay, bf16[272,256]{1,0:T(8,128)(2,1)S(1)} %collective-permute-done.9.came), custom_call_target="tpu_custom_call" | custom-call | bytes 548864 | tf_op jit(solution)/shard_map/pallas_call | solution.py:56
  (2 shorter events, 0.0 us)
Async XLA Ops:
  1.8 7.1 %collective-permute-start = (bf16[144,512]{1,0:T(8,128)(2,1)S(1)}, bf16[144,512]{1,0:T(8,128)(2,1)S(1)}, u32[]{:S(2)}, u32[]{:S(2)}) collective-permute-start(bf16[144,512]{1,0:T(8,128)(2,1)S(1)} %get-tuple-element.15), channel_id=1, source_target_pairs={{0,4},{1,5},{2,6},{3,7},{4,0},{5,1},{6,2},{7,3},{8,12},{9,13},{10,... | collective-permute-start | bytes 442376 | tf_op jit(solution)/shard_map/ppermute | solution.py:224
  4.9 9.5 %collective-permute-start.1 = (bf16[144,512]{1,0:T(8,128)(2,1)S(1)}, bf16[144,512]{1,0:T(8,128)(2,1)S(1)}, u32[]{:S(2)}, u32[]{:S(2)}) collective-permute-start(bf16[144,512]{1,0:T(8,128)(2,1)S(1)} %get-tuple-element.16), channel_id=1, source_target_pairs={{0,12},{1,13},{2,14},{3,15},{4,8},{5,9},{6,10},{7,11},{8,4},{9,5},... | collective-permute-start | bytes 442376 | tf_op jit(solution)/shard_map/ppermute | solution.py:224
  7.4 11.0 %copy-start.1 = (bf16[256,512]{1,0:T(8,128)(2,1)S(1)}, bf16[256,512]{1,0:T(8,128)(2,1)}, u32[]{:S(2)}) copy-start(bf16[256,512]{1,0:T(8,128)(2,1)} %gallery.3) | copy-start | bytes 786436
  7.4 7.5 %collective-permute-start.2 = (bf16[16,512]{1,0:T(8,128)(2,1)S(1)}, bf16[16,512]{1,0:T(8,128)(2,1)S(1)}, u32[]{:S(2)}, u32[]{:S(2)}) collective-permute-start(bf16[16,512]{1,0:T(8,128)(2,1)S(1)} %get-tuple-element.17), channel_id=1, source_target_pairs={{0,8},{1,9},{2,10},{3,11},{4,12},{5,13},{6,14},{7,15},{8,0},{9,1},... | collective-permute-start | bytes 49160 | tf_op jit(solution)/shard_map/ppermute | solution.py:224
  9.0 9.4 %copy-start.2 = (s32[256,10]{0,1:T(8,128)S(1)}, s32[256,10]{0,1:T(8,128)}, u32[]{:S(2)}) copy-start(s32[256,10]{0,1:T(8,128)} %param.6) | copy-start | bytes 30724
  9.0 9.4 %copy-start.3 = (s32[256,10]{0,1:T(8,128)S(1)}, s32[256,10]{0,1:T(8,128)}, u32[]{:S(2)}) copy-start(s32[256,10]{0,1:T(8,128)} %param.7) | copy-start | bytes 30724
  9.0 10.5 %collective-permute-start.3 = (bf16[128,512]{1,0:T(8,128)(2,1)S(1)}, bf16[128,512]{1,0:T(8,128)(2,1)S(1)}, u32[]{:S(2)}, u32[]{:S(2)}) collective-permute-start(bf16[128,512]{1,0:T(8,128)(2,1)S(1)} %slice.9), channel_id=1, source_target_pairs={{0,16},{1,17},{2,18},{3,19},{4,20},{5,21},{6,22},{7,23},{8,24},{9,... | collective-permute-start | bytes 393224 | tf_op jit(solution)/shard_map/ppermute | solution.py:224
  14.9 6.2 %collective-permute-start.5 = (bf16[128,512]{1,0:T(8,128)(2,1)S(1)}, bf16[128,512]{1,0:T(8,128)(2,1)S(1)}, u32[]{:S(2)}, u32[]{:S(2)}) collective-permute-start(bf16[128,512]{1,0:T(8,128)(2,1)S(1)} %slice.8), channel_id=1, source_target_pairs={{0,20},{1,21},{2,22},{3,23},{4,16},{5,17},{6,18},{7,19},{8,28},{9,... | collective-permute-start | bytes 393224 | tf_op jit(solution)/shard_map/ppermute | solution.py:224
  16.4 6.1 %collective-permute-start.6 = (bf16[128,512]{1,0:T(8,128)(2,1)S(1)}, bf16[128,512]{1,0:T(8,128)(2,1)S(1)}, u32[]{:S(2)}, u32[]{:S(2)}) collective-permute-start(bf16[128,512]{1,0:T(8,128)(2,1)S(1)} %slice.8), channel_id=1, source_target_pairs={{0,16},{1,17},{2,18},{3,19},{4,20},{5,21},{6,22},{7,23},{8,24},{9,... | collective-permute-start | bytes 393224 | tf_op jit(solution)/shard_map/ppermute | solution.py:224
  16.9 5.6 %collective-permute-start.7 = (bf16[128,512]{1,0:T(8,128)(2,1)S(1)}, bf16[128,512]{1,0:T(8,128)(2,1)S(1)}, u32[]{:S(2)}, u32[]{:S(2)}) collective-permute-start(bf16[128,512]{1,0:T(8,128)(2,1)S(1)} %slice.8), channel_id=1, source_target_pairs={{0,4},{1,5},{2,6},{3,7},{4,0},{5,1},{6,2},{7,3},{8,12},{9,13},{10,... | collective-permute-start | bytes 393224 | tf_op jit(solution)/shard_map/ppermute | solution.py:224
  18.4 1.1 %copy-start = (bf16[256,512]{1,0:T(8,128)(2,1)S(1)}, bf16[256,512]{1,0:T(8,128)(2,1)}, u32[]{:S(2)}) copy-start(bf16[256,512]{1,0:T(8,128)(2,1)} %queries.3) | copy-start | bytes 786436
  20.0 4.2 %collective-permute-start.4 = (bf16[272,256]{1,0:T(8,128)(2,1)S(1)}, bf16[272,256]{1,0:T(8,128)(2,1)S(1)}, u32[]{:S(2)}, u32[]{:S(2)}) collective-permute-start(bf16[272,256]{1,0:T(8,128)(2,1)S(1)} %get-tuple-element.22), channel_id=1, source_target_pairs={{0,1},{1,0},{2,3},{3,2},{4,5},{5,4},{6,7},{7,6},{8,9},{9,8},{10,11... | collective-permute-start | bytes 417800 | tf_op jit(solution)/shard_map/ppermute | solution.py:224
  22.8 1.4 %collective-permute-start.8 = (bf16[256,256]{1,0:T(8,128)(2,1)S(1)}, bf16[256,256]{1,0:T(8,128)(2,1)S(1)}, u32[]{:S(2)}, u32[]{:S(2)}) collective-permute-start(bf16[256,256]{1,0:T(8,128)(2,1)S(1)} %get-tuple-element.25), channel_id=1, source_target_pairs={{0,1},{1,0},{2,3},{3,2},{4,5},{5,4},{6,7},{7,6},{8,9},{9,8},{10,11... | collective-permute-start | bytes 393224 | tf_op jit(solution)/shard_map/ppermute | solution.py:224
  24.3 5.8 %collective-permute-start.9 = (bf16[272,256]{1,0:T(8,128)(2,1)S(1)}, bf16[272,256]{1,0:T(8,128)(2,1)S(1)}, u32[]{:S(2)}, u32[]{:S(2)}) collective-permute-start(bf16[272,256]{1,0:T(8,128)(2,1)S(1)} %get-tuple-element.27), channel_id=1, source_target_pairs={{0,2},{1,3},{2,0},{3,1},{4,6},{5,7},{6,4},{7,5},{8,10},{9,11},{10,... | collective-permute-start | bytes 417800 | tf_op jit(solution)/shard_map/ppermute | solution.py:224

commit v6 on v5

--- a/solution.py
+++ b/solution.py
@@ -51,13 +51,13 @@
 SPARE = 16
 
 
-def call(kernel, outs, *operands, scratch=(), flops=0, specs=None):
+def call(kernel, outs, *operands, scratch=(), flops=0, specs=None, out_specs=None):
     size = sum(math.prod(item.shape) * item.dtype.itemsize for item in (*outs, *operands))
     return pl.pallas_call(
         kernel,
         out_shape=list(outs),
         in_specs=specs or [VMEM] * len(operands),
-        out_specs=[VMEM] * len(outs),
+        out_specs=out_specs or [VMEM] * len(outs),
         scratch_shapes=list(scratch),
         compiler_params=pltpu.CompilerParams(vmem_limit_bytes=16 * 1024 * 1024),
         cost_estimate=pl.CostEstimate(flops=flops, bytes_accessed=size, transcendentals=0),
@@ -93,8 +93,8 @@
         pltpu.make_async_copy(mine, to_third.at[0:half, :], arrived.at[2]),
         pltpu.make_async_copy(mine, to_first.at[0:half, :], arrived.at[3]),
     ]
-    for copy in copies:
-        copy.start()
+    for index in (1, 0, 2, 3):
+        copies[index].start()
     copies[0].wait()
     shape = (rows_in.shape[0], lists_in.shape[1])
     hot = jnp.where(lax.broadcasted_iota(jnp.int32, shape, 0) == lists_in[0:1, :], 1.0, 0.0).astype(jnp.bfloat16)
@@ -153,13 +153,11 @@
     half = first_other.shape[0]
     row_count = refined.shape[0]
     odd = lax.rem(q + z, 2) == 1
-    rows = refined[...]
-    for place, one in ((g, first), (1 - g, first_other)):
-        columns = pl.ds(pl.multiple_of(place * half, half), half)
-        mine = queries[columns, :]
-        came = one[0:half, :]
-        keep[:, columns] = dot_rows(rows, jnp.where(odd, came, mine))
-        give[0:row_count, columns] = dot_rows(rows, jnp.where(odd, mine, came)).astype(jnp.bfloat16)
+    low = g == 0
+    mine, other = first[0:half, :], first_other[...]
+    came = jnp.concatenate([jnp.where(low, mine, other), jnp.where(low, other, mine)], axis=0)
+    keep[...] = dot_rows(refined[...], jnp.where(odd, came, queries[...]))
+    give[0:row_count, :] = dot_rows(refined[...], jnp.where(odd, queries[...], came)).astype(jnp.bfloat16)
     give[row_count:, :] = three_parts(squares[...])
 
 
@@ -194,14 +192,23 @@
     leave[row_count:, :] = three_parts(row)
 
 
-def score_kernel(stay, came, scores):
-    row_count = scores.shape[0]
+def score_kernel(stay, came, scores, held, sent):
+    row_count = held.shape[0]
+    part = row_count // 2
     squares = stay[row_count : row_count + 1, :] + whole(came[row_count:, :])
     inverse = lax.rsqrt(squares / D + epsilon) / math.sqrt(D)
-    shape = (row_count, row_count)
-    same = lax.broadcasted_iota(jnp.int32, shape, 0) == lax.broadcasted_iota(jnp.int32, shape, 1)
-    inverse = jnp.sum(jnp.where(same, inverse, 0.0), axis=1, keepdims=True)
-    scores[...] = ((stay[0:row_count, :] + came[0:row_count, :].astype(jnp.float32)) * inverse).astype(jnp.bfloat16)
+    copies = []
+    for index in range(2):
+        rows = slice(index * part, (index + 1) * part)
+        shape = (part, row_count)
+        places = lax.broadcasted_iota(jnp.int32, shape, 0) + index * part
+        same = places == lax.broadcasted_iota(jnp.int32, shape, 1)
+        scale = jnp.sum(jnp.where(same, inverse, 0.0), axis=1, keepdims=True)
+        held[rows, :] = ((stay[rows, :] + came[rows, :].astype(jnp.float32)) * scale).astype(jnp.bfloat16)
+        copies.append(pltpu.make_async_copy(held.at[rows, :], scores.at[rows, :], sent.at[index]))
+        copies[index].start()
+    for copy in copies:
+        copy.wait()
 
 
 def line_of_four(shape, gallery, neighbour, weights, send_rows, queries):
@@ -285,7 +292,14 @@
         late_came,
     )
     came = send(leave, lambda g, z, q: (g, z, q ^ 2))
-    (scores,) = call(score_kernel, [jax.ShapeDtypeStruct((row_count, query_count), low)], stay, came)
+    (scores,) = call(
+        score_kernel,
+        [jax.ShapeDtypeStruct((row_count, query_count), low)],
+        stay,
+        came,
+        out_specs=[pl.BlockSpec(memory_space=pltpu.HBM)],
+        scratch=[pltpu.VMEM((row_count, query_count), low), pltpu.SemaphoreType.DMA((2,))],
+    )
     return (refined, scores)
 
 

time: 31.1 us -> 31 us (level)
  no operation moved by 1% of the time
where the time goes in v6:
time: 31 us; the launch traced here: 30.9 us
  waiting for transfers between devices  13.1 us (42%)
  starting transfers between devices  12.5 us (40%)
  Pallas kernels  3.83 us (12%)
  local copies, waits for them, and re-layouts  0.74 us (2%)
  between operations  0.74 us (2%)
    ppermute x10, waiting for transfers between devices, send(): return lax.ppermute(value, AXES, pairs)  13.1 us
    ppermute x10, starting transfers between devices, send(): return lax.ppermute(value, AXES, pairs)  12.5 us
    pallas_call x6, Pallas kernels, call(): pl.pallas_call(kernel, out_shape=list(outs), in_specs=specs or [VMEM] * l...  3.83 us
    unnamed x9, local copies, waits for them, and re-layouts  0.72 us
  transfers between devices with their start and end apart: 10, of which 7 were waited for; matrix products, arithmetic and copies ran while one was open for 2% of the time, Pallas kernels for 6%

profile of v6, /device:TPU:0, one launch (start us, length us, event | category | flops | bytes accessed | tf_op | source)
XLA Modules:
  0.0 30.9 jit_solution(17044727389335707077)
XLA Ops:
  0.6 1.2 %shard_map.68 = (bf16[144,512]{1,0:T(8,128)(2,1)S(1)}, bf16[144,512]{1,0:T(8,128)(2,1)S(1)}, bf16[16,512]{1,0:T(8,128)(2,1)S(1)}) custom-call(bf16[256,512]{1,0:T(8,128)(2,1)} %queries.3, bf16[256,512]{1,0:T(8,128)(2,1)} %gallery.3, s32[1,64]{1,0:T(1,128)} %send_rows.1), custom_call_target="tpu_custom_call" | custom-call | bytes 835840 | tf_op jit(solution)/shard_map/pallas_call | solution.py:56
  1.8 3.1 %collective-permute-start = (bf16[144,512]{1,0:T(8,128)(2,1)S(1)}, bf16[144,512]{1,0:T(8,128)(2,1)S(1)}, u32[]{:S(2)}, u32[]{:S(2)}) collective-permute-start(bf16[144,512]{1,0:T(8,128)(2,1)S(1)} %get-tuple-element.15), channel_id=1, source_target_pairs={{0,4},{1,5},{2,6},{3,7},{4,0},{5,1},{6,2},{7,3},{8,12},{9,13},{10,... | collective-permute-start | bytes 442376 | tf_op jit(solution)/shard_map/ppermute | solution.py:231
  4.9 2.5 %collective-permute-start.1 = (bf16[144,512]{1,0:T(8,128)(2,1)S(1)}, bf16[144,512]{1,0:T(8,128)(2,1)S(1)}, u32[]{:S(2)}, u32[]{:S(2)}) collective-permute-start(bf16[144,512]{1,0:T(8,128)(2,1)S(1)} %get-tuple-element.16), channel_id=1, source_target_pairs={{0,12},{1,13},{2,14},{3,15},{4,8},{5,9},{6,10},{7,11},{8,4},{9,5},... | collective-permute-start | bytes 442376 | tf_op jit(solution)/shard_map/ppermute | solution.py:231
  7.4 0.0 copy-start.1
  7.4 0.1 collective-permute-start.2
  7.5 1.5 %collective-permute-done.first = bf16[144,512]{1,0:T(8,128)(2,1)S(1)} collective-permute-done((bf16[144,512]{1,0:T(8,128)(2,1)S(1)}, bf16[144,512]{1,0:T(8,128)(2,1)S(1)}, u32[]{:S(2)}, u32[]{:S(2)}) %collective-permute-start) | collective-permute-done | bytes 147488 | tf_op jit(solution)/shard_map/ppermute | solution.py:231
  9.0 0.0 copy-start.2
  9.0 0.0 copy-start.3
  9.0 1.6 %collective-permute-start.3 = (bf16[128,512]{1,0:T(8,128)(2,1)S(1)}, bf16[128,512]{1,0:T(8,128)(2,1)S(1)}, u32[]{:S(2)}, u32[]{:S(2)}) collective-permute-start(bf16[128,512]{1,0:T(8,128)(2,1)S(1)} %slice.9), channel_id=1, source_target_pairs={{0,16},{1,17},{2,18},{3,19},{4,20},{5,21},{6,22},{7,23},{8,24},{9,... | collective-permute-start | bytes 393224 | tf_op jit(solution)/shard_map/ppermute | solution.py:231
  10.6 3.8 %collective-permute-done.1.third = bf16[144,512]{1,0:T(8,128)(2,1)S(1)} collective-permute-done((bf16[144,512]{1,0:T(8,128)(2,1)S(1)}, bf16[144,512]{1,0:T(8,128)(2,1)S(1)}, u32[]{:S(2)}, u32[]{:S(2)}) %collective-permute-start.1) | collective-permute-done | bytes 147488 | tf_op jit(solution)/shard_map/ppermute | solution.py:231
  14.4 0.5 %collective-permute-done.2.second = bf16[16,512]{1,0:T(8,128)(2,1)S(1)} collective-permute-done((bf16[16,512]{1,0:T(8,128)(2,1)S(1)}, bf16[16,512]{1,0:T(8,128)(2,1)S(1)}, u32[]{:S(2)}, u32[]{:S(2)}) %collective-permute-start.2) | collective-permute-done | bytes 16416 | tf_op jit(solution)/shard_map/ppermute | solution.py:231
  14.9 1.4 %collective-permute-start.5 = (bf16[128,512]{1,0:T(8,128)(2,1)S(1)}, bf16[128,512]{1,0:T(8,128)(2,1)S(1)}, u32[]{:S(2)}, u32[]{:S(2)}) collective-permute-start(bf16[128,512]{1,0:T(8,128)(2,1)S(1)} %slice.8), channel_id=1, source_target_pairs={{0,20},{1,21},{2,22},{3,23},{4,16},{5,17},{6,18},{7,19},{8,28},{9,... | collective-permute-start | bytes 393224 | tf_op jit(solution)/shard_map/ppermute | solution.py:231
  16.4 0.5 %collective-permute-start.6 = (bf16[128,512]{1,0:T(8,128)(2,1)S(1)}, bf16[128,512]{1,0:T(8,128)(2,1)S(1)}, u32[]{:S(2)}, u32[]{:S(2)}) collective-permute-start(bf16[128,512]{1,0:T(8,128)(2,1)S(1)} %slice.8), channel_id=1, source_target_pairs={{0,16},{1,17},{2,18},{3,19},{4,20},{5,21},{6,22},{7,23},{8,24},{9,... | collective-permute-start | bytes 393224 | tf_op jit(solution)/shard_map/ppermute | solution.py:231
  16.9 1.5 %collective-permute-start.7 = (bf16[128,512]{1,0:T(8,128)(2,1)S(1)}, bf16[128,512]{1,0:T(8,128)(2,1)S(1)}, u32[]{:S(2)}, u32[]{:S(2)}) collective-permute-start(bf16[128,512]{1,0:T(8,128)(2,1)S(1)} %slice.8), channel_id=1, source_target_pairs={{0,4},{1,5},{2,6},{3,7},{4,0},{5,1},{6,2},{7,3},{8,12},{9,13},{10,... | collective-permute-start | bytes 393224 | tf_op jit(solution)/shard_map/ppermute | solution.py:231
  18.4 0.0 copy-done.1
  18.4 0.0 copy-done.2
  18.4 0.0 copy-done.3
  18.4 0.0 copy-start
  18.4 1.1 %shard_map.69 = (bf16[256,512]{1,0:T(8,128)(2,1)S(1)}, f32[16,256]{1,0:T(8,128)S(1)}) custom-call(bf16[256,512]{1,0:T(8,128)(2,1)S(1)} %copy-done.1, s32[10,256]{1,0:T(8,128)S(1)} %bitcast.2, s32[10,256]{1,0:T(8,128)S(1)} %bitcast.3, bf16[144,512]{1,0:T(8,128)(2,1)S(1)} %collective-permute-done.first, bf16[16,512]{1,0:T(8,128)(2,1)S(1)} %collective-permute-done.2.second, ...), custom_call_target="tpu_custom_call" | custom-call | bytes 872448 | tf_op jit(solution)/shard_map/pallas_call | solution.py:56
  19.5 0.0 collective-permute-done.3.first_other
  19.5 0.0 copy-done
  19.5 0.4 %shard_map.70 = (f32[256,256]{1,0:T(8,128)S(1)}, bf16[272,256]{1,0:T(8,128)(2,1)S(1)}) custom-call(bf16[256,512]{1,0:T(8,128)(2,1)S(1)} %get-tuple-element.28.refined, f32[16,256]{1,0:T(8,128)S(1)} %get-tuple-element.20.squares, bf16[256,512]{1,0:T(8,128)(2,1)S(1)} %copy-done, bf16[144,512]{1,0:T(8,128)(2,1)S(1)} %collective-permute-done.first, ...), custom_call_target="tpu_custom_call" | custom-call | bytes 1220608 | tf_op jit(solution)/shard_map/pallas_call | solution.py:56
  19.9 0.1 collective-permute-start.4
  20.0 1.2 %collective-permute-done.5.second_other = bf16[128,512]{1,0:T(8,128)(2,1)S(1)} collective-permute-done((bf16[128,512]{1,0:T(8,128)(2,1)S(1)}, bf16[128,512]{1,0:T(8,128)(2,1)S(1)}, u32[]{:S(2)}, u32[]{:S(2)}) %collective-permute-start.5) | collective-permute-done | bytes 131104 | tf_op jit(solution)/shard_map/ppermute | solution.py:231
  21.1 1.3 %collective-permute-done.6.third_other = bf16[128,512]{1,0:T(8,128)(2,1)S(1)} collective-permute-done((bf16[128,512]{1,0:T(8,128)(2,1)S(1)}, bf16[128,512]{1,0:T(8,128)(2,1)S(1)}, u32[]{:S(2)}, u32[]{:S(2)}) %collective-permute-start.6) | collective-permute-done | bytes 131104 | tf_op jit(solution)/shard_map/ppermute | solution.py:231
  22.4 0.0 collective-permute-done.7.second
  22.5 0.3 %shard_map.71 = (f32[256,256]{1,0:T(8,128)S(1)}, bf16[256,256]{1,0:T(8,128)(2,1)S(1)}) custom-call(bf16[256,512]{1,0:T(8,128)(2,1)S(1)} %get-tuple-element.28.refined, bf16[144,512]{1,0:T(8,128)(2,1)S(1)} %collective-permute-done.1.third, bf16[128,512]{1,0:T(8,128)(2,1)S(1)} %collective-permute-done.5.second_other, ...), custom_call_target="tpu_custom_call" | custom-call | bytes 1196032 | tf_op jit(solution)/shard_map/pallas_call | solution.py:56
  22.8 0.1 collective-permute-start.8
  22.9 1.3 %collective-permute-done.8.late_came = bf16[256,256]{1,0:T(8,128)(2,1)S(1)} collective-permute-done((bf16[256,256]{1,0:T(8,128)(2,1)S(1)}, bf16[256,256]{1,0:T(8,128)(2,1)S(1)}, u32[]{:S(2)}, u32[]{:S(2)}) %collective-permute-start.8) | collective-permute-done | bytes 131104 | tf_op jit(solution)/shard_map/ppermute | solution.py:231
  24.2 0.0 collective-permute-done.4.early_came
  24.2 0.1 shard_map.72
  24.3 1.6 %collective-permute-start.9 = (bf16[272,256]{1,0:T(8,128)(2,1)S(1)}, bf16[272,256]{1,0:T(8,128)(2,1)S(1)}, u32[]{:S(2)}, u32[]{:S(2)}) collective-permute-start(bf16[272,256]{1,0:T(8,128)(2,1)S(1)} %get-tuple-element.27), channel_id=1, source_target_pairs={{0,2},{1,3},{2,0},{3,1},{4,6},{5,7},{6,4},{7,5},{8,10},{9,11},{10,... | collective-permute-start | bytes 417800 | tf_op jit(solution)/shard_map/ppermute | solution.py:231
  25.9 0.7 %copy.7 = bf16[256,512]{1,0:T(8,128)(2,1)} copy(bf16[256,512]{1,0:T(8,128)(2,1)S(1)} %get-tuple-element.28.refined) | data formatting | bytes 524288
  26.6 3.5 %collective-permute-done.9.came = bf16[272,256]{1,0:T(8,128)(2,1)S(1)} collective-permute-done((bf16[272,256]{1,0:T(8,128)(2,1)S(1)}, bf16[272,256]{1,0:T(8,128)(2,1)S(1)}, u32[]{:S(2)}, u32[]{:S(2)}) %collective-permute-start.9) | collective-permute-done | bytes 139296 | tf_op jit(solution)/shard_map/ppermute | solution.py:231
  30.1 0.8 %shard_map.73 = bf16[256,256]{1,0:T(8,128)(2,1)} custom-call(f32[272,256]{1,0:T(8,128)S(1)} %get-tuple-element.26.stay, bf16[272,256]{1,0:T(8,128)(2,1)S(1)} %collective-permute-done.9.came), custom_call_target="tpu_custom_call" | custom-call | bytes 548864 | tf_op jit(solution)/shard_map/pallas_call | solution.py:56
  (2 shorter events, 0.0 us)
Async XLA Ops:
  1.8 7.1 %collective-permute-start = (bf16[144,512]{1,0:T(8,128)(2,1)S(1)}, bf16[144,512]{1,0:T(8,128)(2,1)S(1)}, u32[]{:S(2)}, u32[]{:S(2)}) collective-permute-start(bf16[144,512]{1,0:T(8,128)(2,1)S(1)} %get-tuple-element.15), channel_id=1, source_target_pairs={{0,4},{1,5},{2,6},{3,7},{4,0},{5,1},{6,2},{7,3},{8,12},{9,13},{10,... | collective-permute-start | bytes 442376 | tf_op jit(solution)/shard_map/ppermute | solution.py:231
  4.9 9.5 %collective-permute-start.1 = (bf16[144,512]{1,0:T(8,128)(2,1)S(1)}, bf16[144,512]{1,0:T(8,128)(2,1)S(1)}, u32[]{:S(2)}, u32[]{:S(2)}) collective-permute-start(bf16[144,512]{1,0:T(8,128)(2,1)S(1)} %get-tuple-element.16), channel_id=1, source_target_pairs={{0,12},{1,13},{2,14},{3,15},{4,8},{5,9},{6,10},{7,11},{8,4},{9,5},... | collective-permute-start | bytes 442376 | tf_op jit(solution)/shard_map/ppermute | solution.py:231
  7.4 11.0 %copy-start.1 = (bf16[256,512]{1,0:T(8,128)(2,1)S(1)}, bf16[256,512]{1,0:T(8,128)(2,1)}, u32[]{:S(2)}) copy-start(bf16[256,512]{1,0:T(8,128)(2,1)} %gallery.3) | copy-start | bytes 786436
  7.4 7.5 %collective-permute-start.2 = (bf16[16,512]{1,0:T(8,128)(2,1)S(1)}, bf16[16,512]{1,0:T(8,128)(2,1)S(1)}, u32[]{:S(2)}, u32[]{:S(2)}) collective-permute-start(bf16[16,512]{1,0:T(8,128)(2,1)S(1)} %get-tuple-element.17), channel_id=1, source_target_pairs={{0,8},{1,9},{2,10},{3,11},{4,12},{5,13},{6,14},{7,15},{8,0},{9,1},... | collective-permute-start | bytes 49160 | tf_op jit(solution)/shard_map/ppermute | solution.py:231
  9.0 9.4 %copy-start.2 = (s32[256,10]{0,1:T(8,128)S(1)}, s32[256,10]{0,1:T(8,128)}, u32[]{:S(2)}) copy-start(s32[256,10]{0,1:T(8,128)} %param.6) | copy-start | bytes 30724
  9.0 9.4 %copy-start.3 = (s32[256,10]{0,1:T(8,128)S(1)}, s32[256,10]{0,1:T(8,128)}, u32[]{:S(2)}) copy-start(s32[256,10]{0,1:T(8,128)} %param.7) | copy-start | bytes 30724
  9.0 10.5 %collective-permute-start.3 = (bf16[128,512]{1,0:T(8,128)(2,1)S(1)}, bf16[128,512]{1,0:T(8,128)(2,1)S(1)}, u32[]{:S(2)}, u32[]{:S(2)}) collective-permute-start(bf16[128,512]{1,0:T(8,128)(2,1)S(1)} %slice.9), channel_id=1, source_target_pairs={{0,16},{1,17},{2,18},{3,19},{4,20},{5,21},{6,22},{7,23},{8,24},{9,... | collective-permute-start | bytes 393224 | tf_op jit(solution)/shard_map/ppermute | solution.py:231
  14.9 6.2 %collective-permute-start.5 = (bf16[128,512]{1,0:T(8,128)(2,1)S(1)}, bf16[128,512]{1,0:T(8,128)(2,1)S(1)}, u32[]{:S(2)}, u32[]{:S(2)}) collective-permute-start(bf16[128,512]{1,0:T(8,128)(2,1)S(1)} %slice.8), channel_id=1, source_target_pairs={{0,20},{1,21},{2,22},{3,23},{4,16},{5,17},{6,18},{7,19},{8,28},{9,... | collective-permute-start | bytes 393224 | tf_op jit(solution)/shard_map/ppermute | solution.py:231
  16.4 6.1 %collective-permute-start.6 = (bf16[128,512]{1,0:T(8,128)(2,1)S(1)}, bf16[128,512]{1,0:T(8,128)(2,1)S(1)}, u32[]{:S(2)}, u32[]{:S(2)}) collective-permute-start(bf16[128,512]{1,0:T(8,128)(2,1)S(1)} %slice.8), channel_id=1, source_target_pairs={{0,16},{1,17},{2,18},{3,19},{4,20},{5,21},{6,22},{7,23},{8,24},{9,... | collective-permute-start | bytes 393224 | tf_op jit(solution)/shard_map/ppermute | solution.py:231
  16.9 5.6 %collective-permute-start.7 = (bf16[128,512]{1,0:T(8,128)(2,1)S(1)}, bf16[128,512]{1,0:T(8,128)(2,1)S(1)}, u32[]{:S(2)}, u32[]{:S(2)}) collective-permute-start(bf16[128,512]{1,0:T(8,128)(2,1)S(1)} %slice.8), channel_id=1, source_target_pairs={{0,4},{1,5},{2,6},{3,7},{4,0},{5,1},{6,2},{7,3},{8,12},{9,13},{10,... | collective-permute-start | bytes 393224 | tf_op jit(solution)/shard_map/ppermute | solution.py:231
  18.4 1.1 %copy-start = (bf16[256,512]{1,0:T(8,128)(2,1)S(1)}, bf16[256,512]{1,0:T(8,128)(2,1)}, u32[]{:S(2)}) copy-start(bf16[256,512]{1,0:T(8,128)(2,1)} %queries.3) | copy-start | bytes 786436
  19.9 4.3 %collective-permute-start.4 = (bf16[272,256]{1,0:T(8,128)(2,1)S(1)}, bf16[272,256]{1,0:T(8,128)(2,1)S(1)}, u32[]{:S(2)}, u32[]{:S(2)}) collective-permute-start(bf16[272,256]{1,0:T(8,128)(2,1)S(1)} %get-tuple-element.22), channel_id=1, source_target_pairs={{0,1},{1,0},{2,3},{3,2},{4,5},{5,4},{6,7},{7,6},{8,9},{9,8},{10,11... | collective-permute-start | bytes 417800 | tf_op jit(solution)/shard_map/ppermute | solution.py:231
  22.8 1.4 %collective-permute-start.8 = (bf16[256,256]{1,0:T(8,128)(2,1)S(1)}, bf16[256,256]{1,0:T(8,128)(2,1)S(1)}, u32[]{:S(2)}, u32[]{:S(2)}) collective-permute-start(bf16[256,256]{1,0:T(8,128)(2,1)S(1)} %get-tuple-element.25), channel_id=1, source_target_pairs={{0,1},{1,0},{2,3},{3,2},{4,5},{5,4},{6,7},{7,6},{8,9},{9,8},{10,11... | collective-permute-start | bytes 393224 | tf_op jit(solution)/shard_map/ppermute | solution.py:231
  24.3 5.8 %collective-permute-start.9 = (bf16[272,256]{1,0:T(8,128)(2,1)S(1)}, bf16[272,256]{1,0:T(8,128)(2,1)S(1)}, u32[]{:S(2)}, u32[]{:S(2)}) collective-permute-start(bf16[272,256]{1,0:T(8,128)(2,1)S(1)} %get-tuple-element.27), channel_id=1, source_target_pairs={{0,2},{1,3},{2,0},{3,1},{4,6},{5,7},{6,4},{7,5},{8,10},{9,11},{10,... | collective-permute-start | bytes 417800 | tf_op jit(solution)/shard_map/ppermute | solution.py:231

commit v7 on v5

--- a/solution.py
+++ b/solution.py
@@ -153,13 +153,11 @@
     half = first_other.shape[0]
     row_count = refined.shape[0]
     odd = lax.rem(q + z, 2) == 1
-    rows = refined[...]
-    for place, one in ((g, first), (1 - g, first_other)):
-        columns = pl.ds(pl.multiple_of(place * half, half), half)
-        mine = queries[columns, :]
-        came = one[0:half, :]
-        keep[:, columns] = dot_rows(rows, jnp.where(odd, came, mine))
-        give[0:row_count, columns] = dot_rows(rows, jnp.where(odd, mine, came)).astype(jnp.bfloat16)
+    low = g == 0
+    mine, other = first[0:half, :], first_other[...]
+    came = jnp.concatenate([jnp.where(low, mine, other), jnp.where(low, other, mine)], axis=0)
+    keep[...] = dot_rows(refined[...], jnp.where(odd, came, queries[...]))
+    give[0:row_count, :] = dot_rows(refined[...], jnp.where(odd, queries[...], came)).astype(jnp.bfloat16)
     give[row_count:, :] = three_parts(squares[...])
 
 
@@ -181,7 +179,7 @@
     return jnp.sum(parts.astype(jnp.float32), axis=0, keepdims=True)
 
 
-def leave_kernel(early, early_came, squares, late, late_came, stay, leave):
+def leave_kernel(late, late_came, early, early_came, squares, stay, leave):
     z, q = lax.axis_index("gallery"), lax.axis_index("query")
     row_count = late.shape[0]
     near = lax.div(q, 2) == lax.div(z, 2)
@@ -278,11 +276,11 @@
     stay, leave = call(
         leave_kernel,
         [array((row_count + SPARE, query_count), high), array((row_count + SPARE, query_count), low)],
+        late,
+        late_came,
         early,
         early_came,
         squares,
-        late,
-        late_came,
     )
     came = send(leave, lambda g, z, q: (g, z, q ^ 2))
     (scores,) = call(score_kernel, [jax.ShapeDtypeStruct((row_count, query_count), low)], stay, came)

time: 31.1 us -> 31.1 us (level)
  no operation moved by 1% of the time
where the time goes in v7:
time: 31.1 us; the launch traced here: 30.9 us
  waiting for transfers between devices  13.1 us (42%)
  starting transfers between devices  12.4 us (40%)
  Pallas kernels  3.84 us (12%)
  local copies, waits for them, and re-layouts  0.74 us (2%)
  between operations  0.74 us (2%)
    ppermute x10, waiting for transfers between devices, send(): return lax.ppermute(value, AXES, pairs)  13.1 us
    ppermute x10, starting transfers between devices, send(): return lax.ppermute(value, AXES, pairs)  12.4 us
    pallas_call x6, Pallas kernels, call(): pl.pallas_call(kernel, out_shape=list(outs), in_specs=specs or [VMEM] * l...  3.84 us
    unnamed x9, local copies, waits for them, and re-layouts  0.72 us
  transfers between devices with their start and end apart: 10, of which 7 were waited for; matrix products, arithmetic and copies ran while one was open for 2% of the time, Pallas kernels for 6%

profile of v7, /device:TPU:0, one launch (start us, length us, event | category | flops | bytes accessed | tf_op | source)
XLA Modules:
  0.0 30.9 jit_solution(5441653152083398282)
XLA Ops:
  0.6 1.2 %shard_map.68 = (bf16[144,512]{1,0:T(8,128)(2,1)S(1)}, bf16[144,512]{1,0:T(8,128)(2,1)S(1)}, bf16[16,512]{1,0:T(8,128)(2,1)S(1)}) custom-call(bf16[256,512]{1,0:T(8,128)(2,1)} %queries.3, bf16[256,512]{1,0:T(8,128)(2,1)} %gallery.3, s32[1,64]{1,0:T(1,128)} %send_rows.1), custom_call_target="tpu_custom_call" | custom-call | bytes 835840 | tf_op jit(solution)/shard_map/pallas_call | solution.py:56
  1.8 3.1 %collective-permute-start = (bf16[144,512]{1,0:T(8,128)(2,1)S(1)}, bf16[144,512]{1,0:T(8,128)(2,1)S(1)}, u32[]{:S(2)}, u32[]{:S(2)}) collective-permute-start(bf16[144,512]{1,0:T(8,128)(2,1)S(1)} %get-tuple-element.15), channel_id=1, source_target_pairs={{0,4},{1,5},{2,6},{3,7},{4,0},{5,1},{6,2},{7,3},{8,12},{9,13},{10,... | collective-permute-start | bytes 442376 | tf_op jit(solution)/shard_map/ppermute | solution.py:222
  4.9 2.5 %collective-permute-start.1 = (bf16[144,512]{1,0:T(8,128)(2,1)S(1)}, bf16[144,512]{1,0:T(8,128)(2,1)S(1)}, u32[]{:S(2)}, u32[]{:S(2)}) collective-permute-start(bf16[144,512]{1,0:T(8,128)(2,1)S(1)} %get-tuple-element.16), channel_id=1, source_target_pairs={{0,12},{1,13},{2,14},{3,15},{4,8},{5,9},{6,10},{7,11},{8,4},{9,5},... | collective-permute-start | bytes 442376 | tf_op jit(solution)/shard_map/ppermute | solution.py:222
  7.4 0.0 copy-start.1
  7.4 0.1 collective-permute-start.2
  7.5 1.5 %collective-permute-done.first = bf16[144,512]{1,0:T(8,128)(2,1)S(1)} collective-permute-done((bf16[144,512]{1,0:T(8,128)(2,1)S(1)}, bf16[144,512]{1,0:T(8,128)(2,1)S(1)}, u32[]{:S(2)}, u32[]{:S(2)}) %collective-permute-start) | collective-permute-done | bytes 147488 | tf_op jit(solution)/shard_map/ppermute | solution.py:222
  9.0 0.0 copy-start.2
  9.0 0.0 copy-start.3
  9.0 1.6 %collective-permute-start.7 = (bf16[128,512]{1,0:T(8,128)(2,1)S(1)}, bf16[128,512]{1,0:T(8,128)(2,1)S(1)}, u32[]{:S(2)}, u32[]{:S(2)}) collective-permute-start(bf16[128,512]{1,0:T(8,128)(2,1)S(1)} %slice.9), channel_id=1, source_target_pairs={{0,16},{1,17},{2,18},{3,19},{4,20},{5,21},{6,22},{7,23},{8,24},{9,... | collective-permute-start | bytes 393224 | tf_op jit(solution)/shard_map/ppermute | solution.py:222
  10.6 3.8 %collective-permute-done.1.third = bf16[144,512]{1,0:T(8,128)(2,1)S(1)} collective-permute-done((bf16[144,512]{1,0:T(8,128)(2,1)S(1)}, bf16[144,512]{1,0:T(8,128)(2,1)S(1)}, u32[]{:S(2)}, u32[]{:S(2)}) %collective-permute-start.1) | collective-permute-done | bytes 147488 | tf_op jit(solution)/shard_map/ppermute | solution.py:222
  14.4 0.5 %collective-permute-done.2.second = bf16[16,512]{1,0:T(8,128)(2,1)S(1)} collective-permute-done((bf16[16,512]{1,0:T(8,128)(2,1)S(1)}, bf16[16,512]{1,0:T(8,128)(2,1)S(1)}, u32[]{:S(2)}, u32[]{:S(2)}) %collective-permute-start.2) | collective-permute-done | bytes 16416 | tf_op jit(solution)/shard_map/ppermute | solution.py:222
  14.9 1.4 %collective-permute-start.3 = (bf16[128,512]{1,0:T(8,128)(2,1)S(1)}, bf16[128,512]{1,0:T(8,128)(2,1)S(1)}, u32[]{:S(2)}, u32[]{:S(2)}) collective-permute-start(bf16[128,512]{1,0:T(8,128)(2,1)S(1)} %slice.8), channel_id=1, source_target_pairs={{0,20},{1,21},{2,22},{3,23},{4,16},{5,17},{6,18},{7,19},{8,28},{9,... | collective-permute-start | bytes 393224 | tf_op jit(solution)/shard_map/ppermute | solution.py:222
  16.4 0.5 %collective-permute-start.4 = (bf16[128,512]{1,0:T(8,128)(2,1)S(1)}, bf16[128,512]{1,0:T(8,128)(2,1)S(1)}, u32[]{:S(2)}, u32[]{:S(2)}) collective-permute-start(bf16[128,512]{1,0:T(8,128)(2,1)S(1)} %slice.8), channel_id=1, source_target_pairs={{0,16},{1,17},{2,18},{3,19},{4,20},{5,21},{6,22},{7,23},{8,24},{9,... | collective-permute-start | bytes 393224 | tf_op jit(solution)/shard_map/ppermute | solution.py:222
  16.9 1.5 %collective-permute-start.5 = (bf16[128,512]{1,0:T(8,128)(2,1)S(1)}, bf16[128,512]{1,0:T(8,128)(2,1)S(1)}, u32[]{:S(2)}, u32[]{:S(2)}) collective-permute-start(bf16[128,512]{1,0:T(8,128)(2,1)S(1)} %slice.8), channel_id=1, source_target_pairs={{0,4},{1,5},{2,6},{3,7},{4,0},{5,1},{6,2},{7,3},{8,12},{9,13},{10,... | collective-permute-start | bytes 393224 | tf_op jit(solution)/shard_map/ppermute | solution.py:222
  18.4 0.0 copy-done.1
  18.4 0.0 copy-done.2
  18.4 0.0 copy-done.3
  18.4 0.0 copy-start
  18.4 1.1 %shard_map.69 = (bf16[256,512]{1,0:T(8,128)(2,1)S(1)}, f32[16,256]{1,0:T(8,128)S(1)}) custom-call(bf16[256,512]{1,0:T(8,128)(2,1)S(1)} %copy-done.1, s32[10,256]{1,0:T(8,128)S(1)} %bitcast.2, s32[10,256]{1,0:T(8,128)S(1)} %bitcast.3, bf16[144,512]{1,0:T(8,128)(2,1)S(1)} %collective-permute-done.first, bf16[16,512]{1,0:T(8,128)(2,1)S(1)} %collective-permute-done.2.second, ...), custom_call_target="tpu_custom_call" | custom-call | bytes 872448 | tf_op jit(solution)/shard_map/pallas_call | solution.py:56
  19.5 0.0 collective-permute-done.7.first_other
  19.5 0.0 copy-done
  19.6 0.4 %shard_map.71 = (f32[256,256]{1,0:T(8,128)S(1)}, bf16[272,256]{1,0:T(8,128)(2,1)S(1)}) custom-call(bf16[256,512]{1,0:T(8,128)(2,1)S(1)} %get-tuple-element.28.refined, f32[16,256]{1,0:T(8,128)S(1)} %get-tuple-element.23.squares, bf16[256,512]{1,0:T(8,128)(2,1)S(1)} %copy-done, bf16[144,512]{1,0:T(8,128)(2,1)S(1)} %collective-permute-done.first, ...), custom_call_target="tpu_custom_call" | custom-call | bytes 1220608 | tf_op jit(solution)/shard_map/pallas_call | solution.py:56
  19.9 0.1 collective-permute-start.8
  20.0 1.2 %collective-permute-done.3.second_other = bf16[128,512]{1,0:T(8,128)(2,1)S(1)} collective-permute-done((bf16[128,512]{1,0:T(8,128)(2,1)S(1)}, bf16[128,512]{1,0:T(8,128)(2,1)S(1)}, u32[]{:S(2)}, u32[]{:S(2)}) %collective-permute-start.3) | collective-permute-done | bytes 131104 | tf_op jit(solution)/shard_map/ppermute | solution.py:222
  21.2 1.3 %collective-permute-done.4.third_other = bf16[128,512]{1,0:T(8,128)(2,1)S(1)} collective-permute-done((bf16[128,512]{1,0:T(8,128)(2,1)S(1)}, bf16[128,512]{1,0:T(8,128)(2,1)S(1)}, u32[]{:S(2)}, u32[]{:S(2)}) %collective-permute-start.4) | collective-permute-done | bytes 131104 | tf_op jit(solution)/shard_map/ppermute | solution.py:222
  22.5 0.0 collective-permute-done.5.second
  22.5 0.3 %shard_map.70 = (f32[256,256]{1,0:T(8,128)S(1)}, bf16[256,256]{1,0:T(8,128)(2,1)S(1)}) custom-call(bf16[256,512]{1,0:T(8,128)(2,1)S(1)} %get-tuple-element.28.refined, bf16[144,512]{1,0:T(8,128)(2,1)S(1)} %collective-permute-done.1.third, bf16[128,512]{1,0:T(8,128)(2,1)S(1)} %collective-permute-done.3.second_other, ...), custom_call_target="tpu_custom_call" | custom-call | bytes 1196032 | tf_op jit(solution)/shard_map/pallas_call | solution.py:56
  22.8 0.1 collective-permute-start.6
  22.9 1.3 %collective-permute-done.6.late_came = bf16[256,256]{1,0:T(8,128)(2,1)S(1)} collective-permute-done((bf16[256,256]{1,0:T(8,128)(2,1)S(1)}, bf16[256,256]{1,0:T(8,128)(2,1)S(1)}, u32[]{:S(2)}, u32[]{:S(2)}) %collective-permute-start.6) | collective-permute-done | bytes 131104 | tf_op jit(solution)/shard_map/ppermute | solution.py:222
  24.2 0.0 collective-permute-done.8.early_came
  24.2 0.1 shard_map.72
  24.3 1.5 %collective-permute-start.9 = (bf16[272,256]{1,0:T(8,128)(2,1)S(1)}, bf16[272,256]{1,0:T(8,128)(2,1)S(1)}, u32[]{:S(2)}, u32[]{:S(2)}) collective-permute-start(bf16[272,256]{1,0:T(8,128)(2,1)S(1)} %get-tuple-element.27), channel_id=1, source_target_pairs={{0,2},{1,3},{2,0},{3,1},{4,6},{5,7},{6,4},{7,5},{8,10},{9,11},{10,... | collective-permute-start | bytes 417800 | tf_op jit(solution)/shard_map/ppermute | solution.py:222
  25.9 0.7 %copy.7 = bf16[256,512]{1,0:T(8,128)(2,1)} copy(bf16[256,512]{1,0:T(8,128)(2,1)S(1)} %get-tuple-element.28.refined) | data formatting | bytes 524288
  26.6 3.5 %collective-permute-done.9.came = bf16[272,256]{1,0:T(8,128)(2,1)S(1)} collective-permute-done((bf16[272,256]{1,0:T(8,128)(2,1)S(1)}, bf16[272,256]{1,0:T(8,128)(2,1)S(1)}, u32[]{:S(2)}, u32[]{:S(2)}) %collective-permute-start.9) | collective-permute-done | bytes 139296 | tf_op jit(solution)/shard_map/ppermute | solution.py:222
  30.1 0.8 %shard_map.73 = bf16[256,256]{1,0:T(8,128)(2,1)} custom-call(f32[272,256]{1,0:T(8,128)S(1)} %get-tuple-element.26.stay, bf16[272,256]{1,0:T(8,128)(2,1)S(1)} %collective-permute-done.9.came), custom_call_target="tpu_custom_call" | custom-call | bytes 548864 | tf_op jit(solution)/shard_map/pallas_call | solution.py:56
  (2 shorter events, 0.0 us)
Async XLA Ops:
  1.8 7.1 %collective-permute-start = (bf16[144,512]{1,0:T(8,128)(2,1)S(1)}, bf16[144,512]{1,0:T(8,128)(2,1)S(1)}, u32[]{:S(2)}, u32[]{:S(2)}) collective-permute-start(bf16[144,512]{1,0:T(8,128)(2,1)S(1)} %get-tuple-element.15), channel_id=1, source_target_pairs={{0,4},{1,5},{2,6},{3,7},{4,0},{5,1},{6,2},{7,3},{8,12},{9,13},{10,... | collective-permute-start | bytes 442376 | tf_op jit(solution)/shard_map/ppermute | solution.py:222
  4.9 9.5 %collective-permute-start.1 = (bf16[144,512]{1,0:T(8,128)(2,1)S(1)}, bf16[144,512]{1,0:T(8,128)(2,1)S(1)}, u32[]{:S(2)}, u32[]{:S(2)}) collective-permute-start(bf16[144,512]{1,0:T(8,128)(2,1)S(1)} %get-tuple-element.16), channel_id=1, source_target_pairs={{0,12},{1,13},{2,14},{3,15},{4,8},{5,9},{6,10},{7,11},{8,4},{9,5},... | collective-permute-start | bytes 442376 | tf_op jit(solution)/shard_map/ppermute | solution.py:222
  7.4 11.0 %copy-start.1 = (bf16[256,512]{1,0:T(8,128)(2,1)S(1)}, bf16[256,512]{1,0:T(8,128)(2,1)}, u32[]{:S(2)}) copy-start(bf16[256,512]{1,0:T(8,128)(2,1)} %gallery.3) | copy-start | bytes 786436
  7.4 7.5 %collective-permute-start.2 = (bf16[16,512]{1,0:T(8,128)(2,1)S(1)}, bf16[16,512]{1,0:T(8,128)(2,1)S(1)}, u32[]{:S(2)}, u32[]{:S(2)}) collective-permute-start(bf16[16,512]{1,0:T(8,128)(2,1)S(1)} %get-tuple-element.17), channel_id=1, source_target_pairs={{0,8},{1,9},{2,10},{3,11},{4,12},{5,13},{6,14},{7,15},{8,0},{9,1},... | collective-permute-start | bytes 49160 | tf_op jit(solution)/shard_map/ppermute | solution.py:222
  9.0 9.4 %copy-start.2 = (s32[256,10]{0,1:T(8,128)S(1)}, s32[256,10]{0,1:T(8,128)}, u32[]{:S(2)}) copy-start(s32[256,10]{0,1:T(8,128)} %param.6) | copy-start | bytes 30724
  9.0 9.4 %copy-start.3 = (s32[256,10]{0,1:T(8,128)S(1)}, s32[256,10]{0,1:T(8,128)}, u32[]{:S(2)}) copy-start(s32[256,10]{0,1:T(8,128)} %param.7) | copy-start | bytes 30724
  9.0 10.5 %collective-permute-start.7 = (bf16[128,512]{1,0:T(8,128)(2,1)S(1)}, bf16[128,512]{1,0:T(8,128)(2,1)S(1)}, u32[]{:S(2)}, u32[]{:S(2)}) collective-permute-start(bf16[128,512]{1,0:T(8,128)(2,1)S(1)} %slice.9), channel_id=1, source_target_pairs={{0,16},{1,17},{2,18},{3,19},{4,20},{5,21},{6,22},{7,23},{8,24},{9,... | collective-permute-start | bytes 393224 | tf_op jit(solution)/shard_map/ppermute | solution.py:222
  14.9 6.2 %collective-permute-start.3 = (bf16[128,512]{1,0:T(8,128)(2,1)S(1)}, bf16[128,512]{1,0:T(8,128)(2,1)S(1)}, u32[]{:S(2)}, u32[]{:S(2)}) collective-permute-start(bf16[128,512]{1,0:T(8,128)(2,1)S(1)} %slice.8), channel_id=1, source_target_pairs={{0,20},{1,21},{2,22},{3,23},{4,16},{5,17},{6,18},{7,19},{8,28},{9,... | collective-permute-start | bytes 393224 | tf_op jit(solution)/shard_map/ppermute | solution.py:222
  16.4 6.1 %collective-permute-start.4 = (bf16[128,512]{1,0:T(8,128)(2,1)S(1)}, bf16[128,512]{1,0:T(8,128)(2,1)S(1)}, u32[]{:S(2)}, u32[]{:S(2)}) collective-permute-start(bf16[128,512]{1,0:T(8,128)(2,1)S(1)} %slice.8), channel_id=1, source_target_pairs={{0,16},{1,17},{2,18},{3,19},{4,20},{5,21},{6,22},{7,23},{8,24},{9,... | collective-permute-start | bytes 393224 | tf_op jit(solution)/shard_map/ppermute | solution.py:222
  16.9 5.6 %collective-permute-start.5 = (bf16[128,512]{1,0:T(8,128)(2,1)S(1)}, bf16[128,512]{1,0:T(8,128)(2,1)S(1)}, u32[]{:S(2)}, u32[]{:S(2)}) collective-permute-start(bf16[128,512]{1,0:T(8,128)(2,1)S(1)} %slice.8), channel_id=1, source_target_pairs={{0,4},{1,5},{2,6},{3,7},{4,0},{5,1},{6,2},{7,3},{8,12},{9,13},{10,... | collective-permute-start | bytes 393224 | tf_op jit(solution)/shard_map/ppermute | solution.py:222
  18.4 1.1 %copy-start = (bf16[256,512]{1,0:T(8,128)(2,1)S(1)}, bf16[256,512]{1,0:T(8,128)(2,1)}, u32[]{:S(2)}) copy-start(bf16[256,512]{1,0:T(8,128)(2,1)} %queries.3) | copy-start | bytes 786436
  19.9 4.3 %collective-permute-start.8 = (bf16[272,256]{1,0:T(8,128)(2,1)S(1)}, bf16[272,256]{1,0:T(8,128)(2,1)S(1)}, u32[]{:S(2)}, u32[]{:S(2)}) collective-permute-start(bf16[272,256]{1,0:T(8,128)(2,1)S(1)} %get-tuple-element.25), channel_id=1, source_target_pairs={{0,1},{1,0},{2,3},{3,2},{4,5},{5,4},{6,7},{7,6},{8,9},{9,8},{10,11... | collective-permute-start | bytes 417800 | tf_op jit(solution)/shard_map/ppermute | solution.py:222
  22.8 1.4 %collective-permute-start.6 = (bf16[256,256]{1,0:T(8,128)(2,1)S(1)}, bf16[256,256]{1,0:T(8,128)(2,1)S(1)}, u32[]{:S(2)}, u32[]{:S(2)}) collective-permute-start(bf16[256,256]{1,0:T(8,128)(2,1)S(1)} %get-tuple-element.22), channel_id=1, source_target_pairs={{0,1},{1,0},{2,3},{3,2},{4,5},{5,4},{6,7},{7,6},{8,9},{9,8},{10,11... | collective-permute-start | bytes 393224 | tf_op jit(solution)/shard_map/ppermute | solution.py:222
  24.3 5.8 %collective-permute-start.9 = (bf16[272,256]{1,0:T(8,128)(2,1)S(1)}, bf16[272,256]{1,0:T(8,128)(2,1)S(1)}, u32[]{:S(2)}, u32[]{:S(2)}) collective-permute-start(bf16[272,256]{1,0:T(8,128)(2,1)S(1)} %get-tuple-element.27), channel_id=1, source_target_pairs={{0,2},{1,3},{2,0},{3,1},{4,6},{5,7},{6,4},{7,5},{8,10},{9,11},{10,... | collective-permute-start | bytes 417800 | tf_op jit(solution)/shard_map/ppermute | solution.py:222
